TPU v7x, 128 devices: a whole 4x4x4 slice. The times are simulated.
128 devices in a mesh: dp: 16 (over y_lo, z, core), seq: 8 (over x, y_hi).
Axes of the slice: x: 4, y: 4 (y_hi: 2, y_lo: 2; y = y_hi * 2 + y_lo), z: 4, core: 2. Of those that a mesh axis runs over, the one named last changes fastest.
Arguments:
- tokens: int32 [16, 131072], P('dp', 'seq'), may hold values from 0 to 4
- stem_weight: bfloat16 [60, 768], replicated, may hold values from -1.5 to 1.5
- stem_bias: float32 [768], replicated, may hold values from -3 to 3
- conv_gain: float32 [768], replicated, may hold values from 0.1 to 1.9
- conv_weight: bfloat16 [5, 768, 1536], P(None, 'dp'), may hold values from -0.09375 to 0.09375
- conv_bias: float32 [1536], replicated, may hold values from -3 to 3
- attn_gain: float32 [1536], replicated, may hold values from 0.1 to 1.9
- w_query: bfloat16 [1536, 1024], P('dp'), may hold values from -7 to 7
- w_key: bfloat16 [1536, 128], P('dp'), may hold values from -0.15625 to 0.15625
- w_value: bfloat16 [1536, 192], P('dp'), may hold values from -0.15625 to 0.15625
- w_out: bfloat16 [1536, 1536], P('dp'), may hold values from -0.4375 to 0.4375
Outputs:
- features: bfloat16 [16, 1024, 1536], P('dp', 'seq')
Inputs may be any that keep to these rules, and one draw needn't show every extreme that they name: `tokens`: 0 is an unknown base; 1 to 4 are A, C, G, T.
All inputs are finite; a program needn't handle non-finite values.
Results may differ from a plain program's by a relative error of at most 0.009.
The roundings to bfloat16 on the way count: a program that leaves them out, or rounds other values in their place, can miss the bound.
Values may be sent and summed in bfloat16 or wider, within the bound.
No kernel may reach another device: no remote copies, remote signals or barrier semaphores. Data moves between devices by JAX's collectives and lax.ppermute only.
A program may use at most 192 MiB of HBM per device.

v0:
```python
import jax
import jax.numpy as jnp
from jax import lax
from jax.sharding import PartitionSpec as P

HEADS = 8
HEAD_K = 128
HEAD_V = 192
KW_STEM = 15
KW = 5
POOL_A = 8
POOL_B = 16


epsilon = 1e-06


def with_halo(block, sides, width):
    for axis, dim in sides:
        count = lax.axis_size(axis)
        forward = [(i, i + 1) for i in range(count - 1)]
        backward = [(target, source) for source, target in forward]
        low = lax.ppermute(
            lax.slice_in_dim(block, block.shape[dim] - width, None, axis=dim), axis, forward
        )
        high = lax.ppermute(lax.slice_in_dim(block, 0, width, axis=dim), axis, backward)
        block = jnp.concatenate([low, block, high], axis=dim)
    return block


def stem_pool(padded_tokens, count, stem_weight, stem_bias):
    columns = jnp.stack(
        [padded_tokens[offset : offset + count] for offset in range(KW_STEM)], axis=1
    )
    codes = jnp.arange(1, 5, dtype=jnp.int32)
    onehot = (columns[:, :, None] == codes).astype(jnp.bfloat16).reshape(count, KW_STEM * 4)
    block_len = min(count, 1024)
    onehot = onehot.reshape(count // block_len, block_len, KW_STEM * 4)

    def one_block(inputs):
        stem_rows = jnp.dot(inputs, stem_weight, preferred_element_type=jnp.float32) + stem_bias
        return jax.nn.gelu(jnp.max(stem_rows.reshape(block_len // POOL_A, POOL_A, -1), axis=1))

    return lax.map(one_block, onehot).reshape(count // POOL_A, -1).astype(jnp.bfloat16)


def rms_scale(values, gain):
    return values * lax.rsqrt(jnp.mean(values * values, axis=-1, keepdims=True) + epsilon) * gain


def rotate(values, angles):
    half_dim = values.shape[-1] // 2
    first = values[..., :half_dim]
    second = values[..., half_dim:]
    cosine = jnp.cos(angles)
    sine = jnp.sin(angles)
    return jnp.concatenate(
        [first * cosine - second * sine, second * cosine + first * sine], axis=-1
    )


def body(
    tokens,
    stem_weight,
    stem_bias,
    conv_gain,
    conv_weight,
    conv_bias,
    attn_gain,
    w_query,
    w_key,
    w_value,
    w_out,
):
    seq_local = tokens.shape[1]
    rows_enc = seq_local // POOL_A
    rows_att = rows_enc // POOL_B
    reach = KW_STEM // 2
    edge_rows = KW // 2
    padded_tokens = with_halo(tokens, (("seq", 1),), reach)[0]
    pooled = stem_pool(padded_tokens, seq_local, stem_weight, stem_bias)
    normed = rms_scale(pooled.astype(jnp.float32), conv_gain).astype(jnp.bfloat16)
    padded_rows = with_halo(normed, (("seq", 0),), edge_rows)
    out_channels = conv_weight.shape[2]
    full_weight = lax.all_gather(conv_weight, "dp", axis=1, tiled=True)
    conv_sum = jnp.dot(padded_rows[0:rows_enc], full_weight[0], preferred_element_type=jnp.float32)
    for tap_index in range(1, KW):
        conv_sum = conv_sum + jnp.dot(
            padded_rows[tap_index : tap_index + rows_enc],
            full_weight[tap_index],
            preferred_element_type=jnp.float32,
        )
    conv_sum = conv_sum + conv_bias
    coarse = jnp.max(jax.nn.gelu(conv_sum).reshape(rows_att, POOL_B, out_channels), axis=1).astype(
        jnp.bfloat16
    )
    residual = coarse.astype(jnp.float32)
    hidden = rms_scale(residual, attn_gain).astype(jnp.bfloat16)
    weight_rows = (
        lax.all_gather(w_query, "dp", axis=0, tiled=True),
        lax.all_gather(w_key, "dp", axis=0, tiled=True),
        lax.all_gather(w_value, "dp", axis=0, tiled=True),
    )
    inputs = hidden
    query, keys, values = tuple(
        (
            jnp.dot(inputs, rows_piece, preferred_element_type=jnp.float32)
            for rows_piece in weight_rows
        )
    )
    half_dim = HEAD_K // 2
    freqs = 10000.0 ** (-jnp.arange(half_dim, dtype=jnp.float32) / half_dim)
    positions = lax.axis_index("seq") * rows_att + jnp.arange(rows_att, dtype=jnp.int32)
    angles = positions.astype(jnp.float32)[:, None] * freqs[None, :]
    query = rotate(query.reshape(rows_att, HEADS, HEAD_K), angles[:, None, :]).astype(jnp.bfloat16)
    keys = rotate(keys, angles).astype(jnp.bfloat16)
    values = values.astype(jnp.bfloat16)
    keys_all, values_all = (
        lax.all_gather(keys, "seq", axis=0, tiled=True),
        lax.all_gather(values, "seq", axis=0, tiled=True),
    )
    scores = jnp.einsum(
        "rhd,kd->hrk", query, keys_all, preferred_element_type=jnp.float32
    ) * HEAD_K ** (-0.5)
    weights = jax.nn.softmax(scores, axis=-1).astype(jnp.bfloat16)
    mixed = jnp.einsum(
        "hrk,kd->rhd", weights, values_all, preferred_element_type=jnp.float32
    ).astype(jnp.bfloat16)
    mixed = mixed.reshape(rows_att, HEADS * HEAD_V)
    inputs = mixed
    projected = jnp.dot(
        inputs, lax.all_gather(w_out, "dp", axis=0, tiled=True), preferred_element_type=jnp.float32
    )
    return (residual + projected).astype(jnp.bfloat16)[None]


def solution(mesh):
    in_specs = (
        P("dp", "seq"),
        P(),
        P(),
        P(),
        P(None, "dp", None),
        P(),
        P(),
        P("dp", None),
        P("dp", None),
        P("dp", None),
        P("dp", None),
    )
    out_specs = P("dp", "seq", None)
    return jax.shard_map(body, mesh=mesh, in_specs=in_specs, out_specs=out_specs, check_vma=False)
```

profile of v0, /device:TPU:0, one launch (start us, length us, event | category | flops | bytes accessed | tf_op | source)
XLA Modules:
  0.0 315.3 jit_solution(13570759723456411119)
XLA Ops:
  8.8 5.2 %collective-permute-start = (s32[1,7]{1,0:T(1,128)S(1)}, s32[1,7]{1,0:T(1,128)S(1)}, u32[]{:S(2)}, u32[]{:S(2)}) collective-permute-start(s32[1,7]{1,0:T(1,128)S(1)} %get-tuple-element.70), channel_id=1, source_target_pairs={{0,1},{1,2},{2,3},{3,4},{4,5},{5,6},{6,7},{8,9},{9,10},{10,11},{11... | collective-permute-start | bytes 92 | tf_op jit(solution)/shard_map/ppermute | solution.py:23
  15.4 27.9 %all_gather.22 = bf16[1536,192]{1,0:T(8,128)(2,1)} all-gather(bf16[96,192]{1,0:T(8,128)(2,1)} %param.22), channel_id=1, replica_groups=mesh['dp'=16,'seq'=8] {'dp'}, dimensions={0}, use_global_device_ids=true | all-gather | bytes 626688 | tf_op jit(solution)/shard_map/all_gather | solution.py:102
  43.3 21.0 %all_gather.24 = bf16[1536,128]{1,0:T(8,128)(2,1)} all-gather(bf16[96,128]{1,0:T(8,128)(2,1)} %param.21), channel_id=1, replica_groups=mesh['dp'=16,'seq'=8] {'dp'}, dimensions={0}, use_global_device_ids=true | all-gather | bytes 417792 | tf_op jit(solution)/shard_map/all_gather | solution.py:101
  64.3 2.8 fusion.59
  70.4 4.4 %stack.63 = s32[16384,15]{0,1:T(8,128)} concatenate(s32[16384,1]{0,1:T(1,128)} %get-tuple-element.64, s32[16384,1]{0,1:T(1,128)} %get-tuple-element.65, s32[16384,1]{0,1:T(1,128)} %get-tuple-element.66, s32[16384,1]{0,1:T(1,128)} %get-tuple-element.67, s32[16384,1]{0,1:T(1,128)} %get-tuple-element.68, s32[16384,1]{0,1:T(1,128)} %fusion.65, s32[16384,1]{0,1:T(1,128)} %get-tuple-element.63, ...), dimensions={1} | concatenate | bytes 1966080 | tf_op jit(solution)/shard_map/stack | solution.py:32
  74.8 4.1 %eq.20 = s32[16384,15,4]{0,2,1:T(4,128)} broadcast(s32[16384,15]{0,1:T(8,128)} %stack.63), dimensions={0,1} | broadcast | bytes 4915200 | tf_op jit(solution)/shard_map/eq | solution.py:36
  78.9 5.8 %eq.21 = s32[16,1024,60]{1,0,2:T(8,128)} reshape(s32[16384,15,4]{0,2,1:T(4,128)} %eq.20) | data formatting | bytes 7864320 | tf_op jit(solution)/shard_map/eq | solution.py:36
  84.7 3.8 %compare_convert_fusion = bf16[16,1024,60]{1,0,2:T(8,128)(2,1)} fusion(s32[16,1024,60]{1,0,2:T(8,128)} %eq.21, s32[60]{0:T(128)S(1)} %eq.23), kind=kLoop, calls=%fused_computation.32 | loop fusion | flops 1966080 | bytes 5898480 | tf_op jit(solution)/shard_map/convert_element_type | solution.py:36
  88.5 72.0 %while.10 = (s32[]{:T(128)}, bf16[16,128,768]{2,1,0:T(8,128)(2,1)S(1)}, bf16[16,1024,60]{1,0,2:T(8,128)(2,1)}, bf16[60,768]{1,0:T(8,128)(2,1)S(1)}, f32[768]{0:T(1024)S(1)}, /*index=5*/s32[]{:T(128)}) while((s32[]{:T(128)}, bf16[16,128,768]{2,1,0:T(8,128)(2,1)S(1)}, bf16[16,1024,60]{1,0,2:T(8,128)(2,1)}, bf16[60,768]{1,0:T(8,128)(2,1)S(1)}, ...), condition=%wide.region_2.3_spmd, body=%wide.region_0.2_spmd.sunk | while | flops 96632832 | bytes 1889357 | solution.py:44
  90.9 1.9 bitcast_reduce_fusion.4
  95.4 1.9 bitcast_reduce_fusion.4
  99.9 1.9 bitcast_reduce_fusion.4
  104.4 2.0 bitcast_reduce_fusion.4
  113.4 1.9 bitcast_reduce_fusion.4
  117.9 2.0 bitcast_reduce_fusion.4
  122.4 2.0 bitcast_reduce_fusion.4
  131.3 1.9 bitcast_reduce_fusion.4
  135.9 2.0 bitcast_reduce_fusion.4
  154.0 2.0 bitcast_reduce_fusion.4
  162.1 7.6 %collective-permute-start.2 = (bf16[2,768]{1,0:T(2,128)(2,1)S(1)}, bf16[2,768]{1,0:T(2,128)(2,1)}, u32[]{:S(2)}, u32[]{:S(2)}) collective-permute-start(bf16[2,768]{1,0:T(2,128)(2,1)S(1)} %get-tuple-element.48), channel_id=1, source_target_pairs={{0,1},{1,2},{2,3},{3,4},{4,5},{5,6},{6,7},{8,9},{9,10},{10,11},{11... | collective-permute-start | bytes 9224 | tf_op jit(solution)/shard_map/ppermute | solution.py:23
  169.6 2.4 multiply_convert_fusion
  173.8 10.6 %fusion.28 = f32[2048,1536]{1,0:T(8,128)} fusion(bf16[2,768]{1,0:T(2,128)(2,1)} %collective-permute-done.2, bf16[2048,768]{1,0:T(8,128)(2,1)} %copy-done, bf16[5,768,1536]{2,1,0:T(8,128)(2,1)} %all-gather.4.cloned.1.call-done), kind=kOutput, calls=%fused_computation.41 | convolution fusion | flops 4838129664 | bytes 18091008 | tf_op jit(solution)/shard_map/dot_general | solution.py:86
  184.4 8.6 %fusion.32 = f32[2048,1536]{1,0:T(8,128)} fusion(bf16[2048,768]{1,0:T(8,128)(2,1)S(1)} %copy-done.1, bf16[2,768]{1,0:T(2,128)(2,1)} %collective-permute-done.2, bf16[5,768,1536]{2,1,0:T(8,128)(2,1)S(1)} %copy-done.7), kind=kOutput, calls=%fused_computation.46 | convolution fusion | flops 4838129664 | bytes 18091008 | tf_op jit(solution)/shard_map/dot_general | solution.py:88
  193.0 8.4 %fusion.25 = f32[2048,1536]{1,0:T(8,128)} fusion(bf16[2048,768]{1,0:T(8,128)(2,1)S(1)} %copy-done.1, bf16[2,768]{1,0:T(2,128)(2,1)S(1)} %collective-permute-done.3, bf16[5,768,1536]{2,1,0:T(8,128)(2,1)S(1)} %copy-done.7), kind=kOutput, calls=%fused_computation.39 | convolution fusion | flops 4838129664 | bytes 18091008 | tf_op jit(solution)/shard_map/dot_general | solution.py:88
  201.4 8.3 %fusion.35 = f32[2048,1536]{1,0:T(8,128)} fusion(bf16[2048,768]{1,0:T(8,128)(2,1)S(1)} %bitcast.117, bf16[5,768,1536]{2,1,0:T(8,128)(2,1)S(1)} %copy-done.7), kind=kOutput, calls=%fused_computation.53 | convolution fusion | flops 4831838208 | bytes 18087936 | tf_op jit(solution)/shard_map/dot_general | solution.py:88
  209.7 20.8 %bitcast_reduce_fusion.1 = bf16[128,1536]{1,0:T(8,128)(2,1)S(1)} fusion(f32[2048,1536]{1,0:T(8,128)} %fusion.25, f32[2048,1536]{1,0:T(8,128)} %fusion.35, f32[2048,1536]{1,0:T(8,128)} %fusion.28, f32[2048,1536]{1,0:T(8,128)} %fusion.32, f32[1536]{0:T(1024)S(1)} %copy-done.9, bf16[5,768,1536]{2,1,0:T(8,128)(2,1)} %all-gather.4.cloned.1.call-done, ...), kind=kOutput, calls=%fused_computation.21 | convolution fusion | flops 4881973248 | bytes 56239104 | tf_op jit(solution)/shard_map/dot_general | solution.py:88
  230.7 2.6 convolution_bitcast_fusion
  234.2 32.9 %all_gather.25 = bf16[1024,128]{0,1:T(8,128)(2,1)S(1)} all-gather(bf16[128,128]{0,1:T(8,128)(2,1)S(1)} %pad_maximum_fusion.9), channel_id=1, replica_groups=mesh['dp'=16,'seq'=8] {'seq'}, dimensions={0}, use_global_device_ids=true | all-gather | bytes 294912 | tf_op jit(solution)/shard_map/all_gather | solution.py:119
  267.5 30.7 %all_gather.23 = bf16[1024,192]{0,1:T(8,128)(2,1)S(1)} all-gather(bf16[128,192]{0,1:T(8,128)(2,1)S(1)} %convolution_convert_fusion), channel_id=1, replica_groups=mesh['dp'=16,'seq'=8] {'seq'}, dimensions={0}, use_global_device_ids=true | all-gather | bytes 442368 | tf_op jit(solution)/shard_map/all_gather | solution.py:120
  298.7 3.4 %fusion.79 = (f32[8,128]{1,0:T(8,128)S(1)}, f32[8,128,1024]{1,2,0:T(8,128)}) fusion(bf16[1024,128]{0,1:T(8,128)(2,1)S(1)} %all_gather.25, bf16[128,8,64]{2,0,1:T(8,128)(2,1)S(1)} %get-tuple-element.51, bf16[128,8,64]{2,0,1:T(8,128)(2,1)S(1)} %get-tuple-element.50), kind=kOutput, calls=%fused_computation.125 | convolution fusion | flops 272106496 | bytes 4722688 | tf_op jit(solution)/shard_map/sub | solution.py:125
  302.1 2.8 fusion.39
  304.9 3.9 %fusion.36 = bf16[1,128,1536]{2,1,0:T(8,128)(2,1)} fusion(bf16[128,1536]{0,1:T(8,128)(2,1)S(1)} %bitcast.119, bf16[1536,1536]{1,0:T(8,128)(2,1)} %all-gather.8.cloned.1.call-done, bf16[128,1536]{1,0:T(8,128)(2,1)S(1)} %bitcast_reduce_fusion.1), kind=kOutput, calls=%fused_computation.56 | convolution fusion | flops 604569600 | bytes 5898240 | tf_op jit(solution)/shard_map/dot_general | solution.py:131
  (120 shorter events, 64.1 us)
Async XLA Ops:
  6.5 167.3 %all-gather.4.cloned.1.call-start = ((), (), s32[]{:S(2)}) async-start(), calls=%async_computation | async-start | bytes 12533760 | tf_op jit(solution)/shard_map/all_gather | solution.py:85
  7.3 223.4 %all-gather.6.cloned.1.call-start = ((), (), s32[]{:S(2)}) async-start(), calls=%async_computation.1 | async-start | bytes 3342336 | tf_op jit(solution)/shard_map/all_gather | solution.py:100
  8.0 296.9 %all-gather.8.cloned.1.call-start = ((), (), s32[]{:S(2)}) async-start(), calls=%async_computation.2 | async-start | bytes 5013504 | tf_op jit(solution)/shard_map/all_gather | solution.py:132
  8.8 55.5 %collective-permute-start = (s32[1,7]{1,0:T(1,128)S(1)}, s32[1,7]{1,0:T(1,128)S(1)}, u32[]{:S(2)}, u32[]{:S(2)}) collective-permute-start(s32[1,7]{1,0:T(1,128)S(1)} %get-tuple-element.70), channel_id=1, source_target_pairs={{0,1},{1,2},{2,3},{3,4},{4,5},{5,6},{6,7},{8,9},{9,10},{10,11},{11... | collective-permute-start | bytes 92 | tf_op jit(solution)/shard_map/ppermute | solution.py:23
  14.0 53.1 %collective-permute-start.1 = (s32[1,7]{1,0:T(1,128)S(1)}, s32[1,7]{1,0:T(1,128)S(1)}, u32[]{:S(2)}, u32[]{:S(2)}) collective-permute-start(s32[1,7]{1,0:T(1,128)S(1)} %get-tuple-element.69), channel_id=1, source_target_pairs={{1,0},{2,1},{3,2},{4,3},{5,4},{6,5},{7,6},{9,8},{10,9},{11,10},{12... | collective-permute-start | bytes 92 | tf_op jit(solution)/shard_map/ppermute | solution.py:26
  84.7 3.8 %copy-start.8 = (bf16[60,768]{1,0:T(8,128)(2,1)S(1)}, bf16[60,768]{1,0:T(8,128)(2,1)}, u32[]{:S(2)}) copy-start(bf16[60,768]{1,0:T(8,128)(2,1)} %param.14) | copy-start | bytes 276484
  84.7 3.8 %copy-start.10 = (f32[768]{0:T(1024)S(1)}, f32[768]{0:T(1024)}, u32[]{:S(2)}) copy-start(f32[768]{0:T(1024)} %param.15) | copy-start | bytes 9220
  88.5 72.7 %copy-start.6 = (f32[768]{0:T(1024)S(1)}, f32[768]{0:T(1024)}, u32[]{:S(2)}) copy-start(f32[768]{0:T(1024)} %param.16) | copy-start | bytes 9220
  162.1 10.0 %copy-start = (bf16[2048,768]{1,0:T(8,128)(2,1)}, bf16[2048,768]{1,0:T(8,128)(2,1)S(1)}, u32[]{:S(2)}) copy-start(bf16[2048,768]{1,0:T(8,128)(2,1)S(1)} %fusion.18) | copy-start | bytes 9437188
  162.1 11.7 %collective-permute-start.2 = (bf16[2,768]{1,0:T(2,128)(2,1)S(1)}, bf16[2,768]{1,0:T(2,128)(2,1)}, u32[]{:S(2)}, u32[]{:S(2)}) collective-permute-start(bf16[2,768]{1,0:T(2,128)(2,1)S(1)} %get-tuple-element.48), channel_id=1, source_target_pairs={{0,1},{1,2},{2,3},{3,4},{4,5},{5,6},{6,7},{8,9},{9,10},{10,11},{11... | collective-permute-start | bytes 9224 | tf_op jit(solution)/shard_map/ppermute | solution.py:23
  172.0 12.4 %copy-start.1 = (bf16[2048,768]{1,0:T(8,128)(2,1)S(1)}, bf16[2048,768]{1,0:T(8,128)(2,1)}, u32[]{:S(2)}) copy-start(bf16[2048,768]{1,0:T(8,128)(2,1)} %copy-done) | copy-start | bytes 9437188
  172.0 20.9 %collective-permute-start.3 = (bf16[2,768]{1,0:T(2,128)(2,1)S(1)}, bf16[2,768]{1,0:T(2,128)(2,1)S(1)}, u32[]{:S(2)}, u32[]{:S(2)}) collective-permute-start(bf16[2,768]{1,0:T(2,128)(2,1)S(1)} %get-tuple-element.49), channel_id=1, source_target_pairs={{1,0},{2,1},{3,2},{4,3},{5,4},{6,5},{7,6},{9,8},{10,9},{11,10},{12... | collective-permute-start | bytes 9224 | tf_op jit(solution)/shard_map/ppermute | solution.py:26
  173.8 10.6 %copy-start.7 = (bf16[5,768,1536]{2,1,0:T(8,128)(2,1)S(1)}, bf16[5,768,1536]{2,1,0:T(8,128)(2,1)}, u32[]{:S(2)}) copy-start(bf16[5,768,1536]{2,1,0:T(8,128)(2,1)} %all-gather.4.cloned.1.call-done) | copy-start | bytes 35389444
  193.0 8.4 %copy-start.3 = (bf16[16,128,768]{2,1,0:T(8,128)(2,1)S(1)}, bf16[16,128,768]{2,1,0:T(8,128)(2,1)}, u32[]{:S(2)}) copy-start(bf16[16,128,768]{2,1,0:T(8,128)(2,1)} %multiply_convert_fusion) | copy-start | bytes 9437188
  193.0 8.4 %copy-start.11 = (bf16[2,768]{1,0:T(2,128)(2,1)}, bf16[2,768]{1,0:T(2,128)(2,1)S(1)}, u32[]{:S(2)}) copy-start(bf16[2,768]{1,0:T(2,128)(2,1)S(1)} %collective-permute-done.3) | copy-start | bytes 9220
  201.4 8.3 %copy-start.9 = (f32[1536]{0:T(1024)S(1)}, f32[1536]{0:T(1024)}, u32[]{:S(2)}) copy-start(f32[1536]{0:T(1024)} %param.18) | copy-start | bytes 18436
  201.4 8.3 %copy-start.12 = (bf16[2,768]{1,0:T(2,128)(2,1)S(1)}, bf16[2,768]{1,0:T(2,128)(2,1)}, u32[]{:S(2)}) copy-start(bf16[2,768]{1,0:T(2,128)(2,1)} %copy-done.11) | copy-start | bytes 9220
  209.7 21.0 %copy-start.5 = (f32[1536]{0:T(1024)S(1)}, f32[1536]{0:T(1024)}, u32[]{:S(2)}) copy-start(f32[1536]{0:T(1024)} %param.19) | copy-start | bytes 18436
  230.5 3.0 copy-start.4
  230.5 36.6 %copy-start.2 = (bf16[1536,192]{1,0:T(8,128)(2,1)S(1)}, bf16[1536,192]{1,0:T(8,128)(2,1)}, u32[]{:S(2)}) copy-start(bf16[1536,192]{1,0:T(8,128)(2,1)} %all_gather.22) | copy-start | bytes 1769476
Sparse Core Ops, SparseCore 0:
  9.0 74.6 all-gather.3
  85.5 38.0 all-gather.5
  125.3 38.3 all-gather.7
where the time goes:
time: 317 us; the launch traced here: 315 us
  blocking collectives  112 us (35%)
  matrix products  101 us (32%)
  local copies, waits for them, and re-layouts  55.5 us (18%)
  starting transfers between devices  15.8 us (5%)
  other arithmetic  14.9 us (5%)
  between operations  13.4 us (4%)
    dot_general x4, matrix products, body(): jnp.dot(padded_rows[tap_index:tap_index + rows_enc], full_weight[tap_inde...  46 us
    dynamic_slice x32, local copies, waits for them, and re-layouts, stem_pool(): lax.map(one_block, onehot).reshape(count // POOL_A, -1).astype(jnp.bfloat16)  38.2 us
    all_gather x1, blocking collectives, body(): lax.all_gather(keys, 'seq', axis=0, tiled=True)  32.9 us
    dot_general x16, matrix products, one_block(): jnp.dot(inputs, stem_weight, preferred_element_type=jnp.float32) + stem_bias  31.2 us
    all_gather x1, blocking collectives, body(): lax.all_gather(values, 'seq', axis=0, tiled=True)  30.7 us
    all_gather x1, blocking collectives, body(): lax.all_gather(w_value, 'dp', axis=0, tiled=True)  27.9 us
    all_gather x1, blocking collectives, body(): lax.all_gather(w_key, 'dp', axis=0, tiled=True)  21 us
    ppermute x2, starting transfers between devices, with_halo(): lax.ppermute(lax.slice_in_dim(block, block.shape[dim] - width, None, axis...  12.7 us
  transfers between devices with their start and end apart: 7, of which 0 were waited for; matrix products, arithmetic and copies ran while one was open for 53% of the time, Pallas kernels for 0%

commit v1 on v0

v1 whole, which is shorter than its diff:
```python
import functools

import jax
import jax.numpy as jnp
import numpy as np
from jax import lax
from jax.experimental import pallas as pl
from jax.experimental.pallas import tpu as pltpu
from jax.sharding import PartitionSpec as P

D_STEM = 768
D = 1536
HEADS = 8
HEAD_K = 128
HEAD_V = 192
KW_STEM = 15
KW = 5
POOL_A = 8
POOL_B = 16
SHARDS = 16
CONV_ROWS = D_STEM // SHARDS
PROJ_ROWS = D // SHARDS
OUT_AT = KW * CONV_ROWS
QKV_AT = OUT_AT + PROJ_ROWS
BLOCK_ROWS = QKV_AT + PROJ_ROWS
CHUNK = 256
ROWS = 128
HALO = 24
EPSILON = 1e-06
AXES = ("dp", "seq")
VMEM_LIMIT = 60 * 1024 * 1024


def device_of(x, y, z, core):
    x, y, z = x % 4, y % 4, z % 4
    return ((y % 2) * 8 + z * 2 + core) * 8 + (x * 2 + y // 2)


def received_from(source):
    pairs = []
    for x in range(4):
        for y in range(4):
            for z in range(4):
                for core in range(2):
                    pairs.append((device_of(*source(x, y, z, core)), device_of(x, y, z, core)))
    return sorted(pairs)


def side(core):
    return 1 - 2 * core


def turn(x, core):
    return 1 - 2 * ((x + core) % 2)


FROM_Y = received_from(lambda x, y, z, core: (x, y + side(core), z, core))
FROM_X = received_from(lambda x, y, z, core: (x + side(core), y, z, core))
FROM_Z = received_from(lambda x, y, z, core: (x, y, z + turn(x, core), core))
FROM_CORE = received_from(lambda x, y, z, core: (x, y, z, 1 - core))


def shard_order():
    orders = np.zeros((SHARDS, 8, SHARDS), np.int32)
    for dp in range(SHARDS):
        for seq in range(8):
            y_low, z, core, x = dp // 8, (dp // 2) % 4, dp % 2, seq // 2

            def names(c):
                turned = turn(x, c)

                def shard(other, dz):
                    return (y_low ^ other) * 8 + (z + dz) % 4 * 2 + c

                return dict(
                    own=shard(0, 0), y=shard(1, 0), za=shard(0, turned), zb=shard(0, -turned),
                    zz=shard(0, 2), yza=shard(1, turned), yzb=shard(1, -turned), yzz=shard(1, 2),
                )

            mine, other = names(core), names(1 - core)
            order = [mine["own"], other["own"], mine["y"], mine["za"], other["y"], other["za"]]
            order += [mine["zb"], mine["zz"], mine["yza"], other["zb"], other["zz"], other["yza"]]
            order += [mine["yzb"], mine["yzz"], other["yzb"], other["yzz"]]
            orders[dp, seq] = order
    return orders


ORDERS = shard_order()


def dot(a, b):
    return jnp.dot(a, b, preferred_element_type=jnp.float32)


def gelu(x):
    return jax.nn.gelu(x)


def stem_kernel(edges, tokens, taps, bias, gain, out, hits):
    held = tokens[...].astype(jnp.float32)
    before = pltpu.roll(held, 1, 0)
    after = pltpu.roll(held, held.shape[0] - 1, 0)
    wide = jnp.concatenate([before, held, after], axis=1).astype(jnp.bfloat16)
    width = wide.shape[1]
    for g in range(POOL_B):
        token = lax.broadcasted_iota(jnp.int32, (width, 128), 0)
        lane = lax.broadcasted_iota(jnp.int32, (width, 128), 1)
        pick = (token == 120 + 8 * g + lane // 4).astype(jnp.float32).astype(jnp.bfloat16)
        spread = dot(wide, pick)
        code = (lax.broadcasted_iota(jnp.int32, spread.shape, 1) % 4 + 1).astype(jnp.float32)
        hit = (spread == code).astype(jnp.float32)
        hits[g * ROWS : (g + 1) * ROWS] = hit[:ROWS].astype(jnp.bfloat16)
        if g == 0:
            row_0 = hit[ROWS : ROWS + 1]
        if g == 1:
            row_1 = hit[ROWS : ROWS + 1]
        if g == 14:
            row_2 = hit[-1:]
        if g == 15:
            row_3 = hit[-1:]
    tail = jnp.concatenate([row_0, row_1, row_2, row_3, jnp.zeros((12, 128), jnp.float32)], axis=0)
    hits[POOL_B * ROWS :] = tail.astype(jnp.bfloat16)

    def normed(rows):
        best = dot(rows, taps[0])
        for offset in range(1, POOL_A):
            best = jnp.maximum(best, dot(rows, taps[offset]))
        pooled = gelu(best + bias[...]).astype(jnp.bfloat16).astype(jnp.float32)
        scale = lax.rsqrt(jnp.mean(pooled * pooled, axis=-1, keepdims=True) + EPSILON)
        return pooled * scale * gain[...]

    edge = normed(hits[POOL_B * ROWS :])
    high = jnp.where(edges[1] == 1, 0.0, edge[0:2])
    low = jnp.where(edges[0] == 1, 0.0, edge[2:4])

    def one(g, _):
        start = pl.multiple_of(g * ROWS, ROWS)
        out[g + 2] = normed(hits[pl.ds(start, ROWS)]).astype(jnp.bfloat16)
        return 0

    lax.fori_loop(0, POOL_B, one, 0)
    row = lax.broadcasted_iota(jnp.int32, (ROWS, D_STEM), 0)
    for i in range(2):
        block = out[POOL_B + i].astype(jnp.float32)
        out[i] = jnp.where(row == 0, low[i : i + 1], pltpu.roll(block, 1, 0)).astype(jnp.bfloat16)
        block = out[2 + i].astype(jnp.float32)
        block = jnp.where(row == ROWS - 1, high[i : i + 1], pltpu.roll(block, ROWS - 1, 0))
        out[POOL_B + 2 + i] = block.astype(jnp.bfloat16)


def stem(edges, tokens, taps, bias, gain):
    return pl.pallas_call(
        stem_kernel,
        out_shape=jax.ShapeDtypeStruct((POOL_B + 4, ROWS, D_STEM), jnp.bfloat16),
        in_specs=[pl.BlockSpec(memory_space=pltpu.SMEM)]
        + [pl.BlockSpec(memory_space=pltpu.VMEM)] * 4,
        out_specs=pl.BlockSpec(memory_space=pltpu.VMEM),
        scratch_shapes=[pltpu.VMEM((POOL_B * ROWS + 16, 128), jnp.bfloat16)],
        compiler_params=pltpu.CompilerParams(vmem_limit_bytes=VMEM_LIMIT),
        cost_estimate=pl.CostEstimate(flops=7_000_000_000, bytes_accessed=5_000_000, transcendentals=1_600_000),
        name="stem",
    )(edges, tokens, taps, bias, gain)


def pieces_of(part):
    pieces = []
    at = part * CHUNK
    while at < (part + 1) * CHUNK:
        block, row = divmod(at, CONV_ROWS)
        rows = min(CONV_ROWS - row, (part + 1) * CHUNK - at)
        pieces.append((block, row, rows, at - part * CHUNK))
        at += rows
    return pieces


STEP_G = 4


def conv_kernel(part, count, rows, *refs):
    blocks = refs[:count]
    acc_in = None
    at = count
    if part > 0:
        acc_in = refs[at]
        at += 1
    if part == 2:
        bias = refs[at]
        at += 1
    out = refs[at]
    weight, sems = refs[at + 1], refs[at + 2]
    pieces = pieces_of(part)
    first = pieces[0][0]
    step = pl.program_id(0)

    def copies(tap):
        return [
            pltpu.make_async_copy(
                blocks[block - first].at[pl.ds(tap * CONV_ROWS + row, size)],
                weight.at[tap, pl.ds(to, size)],
                sems.at[tap * len(pieces) + i],
            )
            for i, (block, row, size, to) in enumerate(pieces)
        ]

    @pl.when(step == 0)
    def _():
        for tap in range(KW):
            for copy in copies(tap):
                copy.start()
        for tap in range(KW):
            for copy in copies(tap):
                copy.wait()

    base = step * STEP_G
    columns = 512
    for n in range(D // columns):
        here = slice(n * columns, (n + 1) * columns)
        total = None
        for tap in range(KW):
            lhs = rows[pl.ds(base + tap, STEP_G)].reshape(STEP_G * ROWS, CHUNK)
            term = dot(lhs, weight[tap, :, here])
            total = term if total is None else total + term
        if part > 0:
            total = total + acc_in[:, here]
        if part < 2:
            out[:, here] = total
        else:
            total = total.reshape(STEP_G, ROWS, columns)
            most, least = jnp.max(total, axis=0), jnp.min(total, axis=0)
            most_ref, least_ref = refs[at + 3], refs[at + 4]

            @pl.when(step == 0)
            def _():
                most_ref[:, here] = most
                least_ref[:, here] = least

            @pl.when(step > 0)
            def _():
                most_ref[:, here] = jnp.maximum(most_ref[:, here], most)
                least_ref[:, here] = jnp.minimum(least_ref[:, here], least)

            @pl.when(step == POOL_B // STEP_G - 1)
            def _():
                shift = bias[:, here]
                coarse = jnp.maximum(gelu(most_ref[:, here] + shift), gelu(least_ref[:, here] + shift))
                out[:, here] = coarse.astype(jnp.bfloat16)


def conv_part(part, rows, blocks, acc=None, bias=None):
    pieces = pieces_of(part)
    blocks = blocks[pieces[0][0] : pieces[-1][0] + 1]
    step_rows = STEP_G * ROWS
    args = [rows, *blocks]
    in_specs = [pl.BlockSpec((POOL_B + 4, ROWS, CHUNK), lambda i, part=part: (0, 0, part))]
    in_specs += [pl.BlockSpec(memory_space=pl.ANY)] * len(blocks)
    acc_spec = pl.BlockSpec((step_rows, D), lambda i: (i, 0))
    scratch = [
        pltpu.VMEM((KW, CHUNK, D), jnp.bfloat16),
        pltpu.SemaphoreType.DMA((KW * len(pieces),)),
    ]
    if part > 0:
        args.append(acc)
        in_specs.append(acc_spec)
    if part == 2:
        args.append(bias)
        in_specs.append(pl.BlockSpec((1, D), lambda i: (0, 0)))
        out_shape = jax.ShapeDtypeStruct((ROWS, D), jnp.bfloat16)
        out_spec = pl.BlockSpec((ROWS, D), lambda i: (0, 0))
        scratch += [pltpu.VMEM((ROWS, D), jnp.float32)] * 2
    else:
        out_shape = jax.ShapeDtypeStruct((POOL_B * ROWS, D), jnp.float32)
        out_spec = acc_spec
    return pl.pallas_call(
        functools.partial(conv_kernel, part, len(blocks)),
        grid=(POOL_B // STEP_G,),
        out_shape=out_shape,
        in_specs=in_specs,
        out_specs=out_spec,
        scratch_shapes=scratch,
        compiler_params=pltpu.CompilerParams(vmem_limit_bytes=VMEM_LIMIT),
        cost_estimate=pl.CostEstimate(flops=8_053_063_680, bytes_accessed=20_000_000, transcendentals=0),
        name="conv",
    )(*args)


def turned(values, cosine, sine):
    return values * cosine + pltpu.roll(values, HEAD_K // 2, 1) * sine


def load_rows(order, blocks, row, column, width, target, sems):
    copies = [
        pltpu.make_async_copy(
            block.at[pl.ds(row, PROJ_ROWS), pl.ds(column, width)],
            target.at[pl.ds(pl.multiple_of(order[i] * PROJ_ROWS, PROJ_ROWS), PROJ_ROWS)],
            sems.at[i],
        )
        for i, block in enumerate(blocks)
    ]
    for copy in copies:
        copy.start()
    return copies


KV_WIDTH = 384


def keys_kernel(order, coarse, gain, cosine, sine, *refs):
    blocks = refs[:SHARDS]
    hidden, pair, weight, sems = refs[SHARDS:]
    copies = load_rows(order, blocks, QKV_AT, HEADS * HEAD_K, KV_WIDTH, weight, sems)
    residual = coarse[...].astype(jnp.float32)
    scale = lax.rsqrt(jnp.mean(residual * residual, axis=-1, keepdims=True) + EPSILON)
    rows = (residual * scale * gain[...]).astype(jnp.bfloat16)
    hidden[...] = rows
    for copy in copies:
        copy.wait()
    both = dot(rows, weight[...])
    pair[:, :HEAD_K] = turned(both[:, :HEAD_K], cosine[...], sine[...]).astype(jnp.bfloat16)
    pair[:, HEAD_K:] = both[:, HEAD_K:].astype(jnp.bfloat16)


def keys_of(order, coarse, gain, cosine, sine, blocks):
    vmem = pl.BlockSpec(memory_space=pltpu.VMEM)
    return pl.pallas_call(
        keys_kernel,
        out_shape=(
            jax.ShapeDtypeStruct((ROWS, D), jnp.bfloat16),
            jax.ShapeDtypeStruct((ROWS, KV_WIDTH), jnp.bfloat16),
        ),
        in_specs=[pl.BlockSpec(memory_space=pltpu.SMEM)] + [vmem] * 4 + [pl.BlockSpec(memory_space=pl.ANY)] * SHARDS,
        out_specs=(vmem, vmem),
        scratch_shapes=[pltpu.VMEM((D, KV_WIDTH), jnp.bfloat16), pltpu.SemaphoreType.DMA((SHARDS,))],
        compiler_params=pltpu.CompilerParams(vmem_limit_bytes=VMEM_LIMIT),
        cost_estimate=pl.CostEstimate(flops=150_000_000, bytes_accessed=2_000_000, transcendentals=0),
        name="keys",
    )(order, coarse, gain, cosine, sine, *blocks)


def query_kernel(order, hidden, cosine, sine, *refs):
    blocks = refs[:SHARDS]
    out, weight, sems = refs[SHARDS:]
    for copy in load_rows(order, blocks, QKV_AT, 0, HEADS * HEAD_K, weight, sems):
        copy.wait()
    for head in range(HEADS):
        query = dot(hidden[...], weight[:, head * HEAD_K : (head + 1) * HEAD_K])
        out[head] = turned(query, cosine[...], sine[...]).astype(jnp.bfloat16)


def query_of(order, hidden, cosine, sine, blocks):
    vmem = pl.BlockSpec(memory_space=pltpu.VMEM)
    return pl.pallas_call(
        query_kernel,
        out_shape=jax.ShapeDtypeStruct((HEADS, ROWS, HEAD_K), jnp.bfloat16),
        in_specs=[pl.BlockSpec(memory_space=pltpu.SMEM)] + [vmem] * 3 + [pl.BlockSpec(memory_space=pl.ANY)] * SHARDS,
        out_specs=vmem,
        scratch_shapes=[pltpu.VMEM((D, HEADS * HEAD_K), jnp.bfloat16), pltpu.SemaphoreType.DMA((SHARDS,))],
        compiler_params=pltpu.CompilerParams(vmem_limit_bytes=VMEM_LIMIT),
        cost_estimate=pl.CostEstimate(flops=1_600_000_000, bytes_accessed=4_000_000, transcendentals=0),
        name="query",
    )(order, hidden, cosine, sine, *blocks)


def attention_kernel(order, coarse, query, *refs):
    pairs, blocks = refs[:8], refs[8 : 8 + SHARDS]
    out, weight, sems = refs[8 + SHARDS :]
    copies = load_rows(order, blocks, OUT_AT, 0, D, weight, sems)
    keys = jnp.concatenate([pair[:, :HEAD_K] for pair in pairs], axis=0)
    values = jnp.concatenate([pair[:, HEAD_K:] for pair in pairs], axis=0)
    mixed = []
    for head in range(HEADS):
        scores = lax.dot_general(
            query[head], keys, (((1,), (1,)), ((), ())), preferred_element_type=jnp.float32
        ) * HEAD_K ** (-0.5)
        raised = jnp.exp(scores - jnp.max(scores, axis=-1, keepdims=True))
        weights = raised / jnp.sum(raised, axis=-1, keepdims=True)
        mixed.append(dot(weights.astype(jnp.bfloat16), values).astype(jnp.bfloat16)[:, :HEAD_V])
    for copy in copies:
        copy.wait()
    total = coarse[...].astype(jnp.float32)
    for head in range(HEADS):
        total = total + dot(mixed[head], weight[head * HEAD_V : (head + 1) * HEAD_V])
    out[...] = total.astype(jnp.bfloat16)


def attention(order, coarse, query, pairs, blocks):
    vmem = pl.BlockSpec(memory_space=pltpu.VMEM)
    return pl.pallas_call(
        attention_kernel,
        out_shape=jax.ShapeDtypeStruct((ROWS, D), jnp.bfloat16),
        in_specs=[pl.BlockSpec(memory_space=pltpu.SMEM)] + [vmem] * 10 + [pl.BlockSpec(memory_space=pl.ANY)] * SHARDS,
        out_specs=vmem,
        scratch_shapes=[pltpu.VMEM((D, D), jnp.bfloat16), pltpu.SemaphoreType.DMA((SHARDS,))],
        compiler_params=pltpu.CompilerParams(vmem_limit_bytes=VMEM_LIMIT),
        cost_estimate=pl.CostEstimate(flops=3_000_000_000, bytes_accessed=6_000_000, transcendentals=1_000_000),
        name="attention",
    )(order, coarse, query, *pairs, *blocks)


def move(value, pairs):
    return lax.ppermute(value, AXES, pairs)


def body(
    tokens,
    stem_weight,
    stem_bias,
    conv_gain,
    conv_weight,
    conv_bias,
    attn_gain,
    w_query,
    w_key,
    w_value,
    w_out,
):
    seq = lax.axis_index("seq")
    line = tokens[0]
    up = [(i, i + 1) for i in range(7)]
    down = [(i + 1, i) for i in range(7)]
    low = lax.ppermute(line[-HALO:], "seq", up)
    high = lax.ppermute(line[:HALO], "seq", down)

    projections = jnp.pad(
        jnp.concatenate([w_query, w_key, w_value], axis=1), ((0, 0), (0, D - HEADS * HEAD_K - HEAD_K - HEAD_V))
    )
    own = jnp.concatenate([conv_weight.reshape(OUT_AT, D), w_out, projections], axis=0)
    own_o = move(own, FROM_CORE)
    y = move(own, FROM_Y)
    za = move(own, FROM_Z)
    order = jnp.asarray(ORDERS)[lax.axis_index("dp"), seq]
    source = (order[:, None] * CONV_ROWS + jnp.arange(CONV_ROWS)[None, :]).reshape(1, D_STEM)
    chosen = jnp.arange(D_STEM)[:, None] == source
    weight = dot(stem_weight, chosen.astype(jnp.bfloat16)).astype(jnp.bfloat16)
    bias, gain = (
        jnp.sum(jnp.where(chosen, vector[:, None], 0.0), axis=0, keepdims=True)
        for vector in (stem_bias, conv_gain)
    )
    taps = jnp.stack([jnp.pad(weight, ((4 * (j + 1), 128 - 60 - 4 * (j + 1)), (0, 0))) for j in range(POOL_A)])
    half = HEAD_K // 2
    freqs = 10000.0 ** (-jnp.arange(half, dtype=jnp.float32) / half)
    positions = seq * ROWS + jnp.arange(ROWS, dtype=jnp.int32)
    angles = positions.astype(jnp.float32)[:, None] * freqs[None, :]
    cosine = jnp.tile(jnp.cos(angles), (1, 2))
    sine = jnp.sin(angles)
    sine = jnp.concatenate([-sine, sine], axis=1)

    rows = jnp.concatenate(
        [
            line.reshape(ROWS, 128),
            jnp.pad(high, (0, 128 - HALO))[None],
            jnp.zeros((14, 128), jnp.int32),
            jnp.pad(low, (128 - HALO, 0))[None],
        ],
        axis=0,
    )
    edges = jnp.stack([seq == 0, seq == 7]).astype(jnp.int32)
    normed = stem(edges, rows, taps, bias, gain)

    zb = move(za, FROM_X)
    yza = move(za, FROM_Y)
    zz = move(za, FROM_Z)
    y_o, za_o = move(y, FROM_CORE), move(za, FROM_CORE)
    blocks = [own, own_o, y, za, y_o, za_o]
    total = conv_part(0, normed, blocks)
    yzb = move(yza, FROM_X)
    yzz = move(zz, FROM_Y)
    blocks += [zb, zz, yza] + [move(b, FROM_CORE) for b in (zb, zz, yza)]
    total = conv_part(1, normed, blocks, total)
    blocks += [yzb, yzz, move(yzb, FROM_CORE), move(yzz, FROM_CORE)]
    coarse = conv_part(2, normed, blocks, total, conv_bias[None])

    hidden, pair = keys_of(order, coarse, attn_gain[None], cosine, sine, blocks)
    pairs = [pair] + [
        lax.ppermute(pair, "seq", [(i, (i + shift) % 8) for i in range(8)]) for shift in range(1, 8)
    ]
    query = query_of(order, hidden, cosine, sine, blocks)
    return attention(order, coarse, query, pairs, blocks)[None]


def solution(mesh):
    in_specs = (
        P("dp", "seq"),
        P(),
        P(),
        P(),
        P(None, "dp", None),
        P(),
        P(),
        P("dp", None),
        P("dp", None),
        P("dp", None),
        P("dp", None),
    )
    out_specs = P("dp", "seq", None)
    return jax.shard_map(body, mesh=mesh, in_specs=in_specs, out_specs=out_specs, check_vma=False)
```

time: 317 us -> 164 us (0.52)
  blocking collectives: 112 us -> 0 us
  matrix products: 101 us -> 0.51 us
  Pallas kernels: 0 us -> 80.9 us
  local copies, waits for them, and re-layouts: 55.5 us -> 10.5 us
  starting transfers between devices: 15.8 us -> 43.4 us
  waiting for transfers between devices: 1.49 us -> 18 us
  between operations: 13.4 us -> 0.51 us
  other arithmetic: 14.9 us -> 7.61 us
    all_gather x4 -> x0, blocking collectives: 112 us -> none  [the longest x1 32.9 us: body(): lax.all_gather(keys, 'seq', axis=0, tiled=True)]
    dot_general x26 -> x1, matrix products: 97.9 us -> 0.51 us  [dot(): return jnp.dot(a, b, preferred_element_type=jnp.float32)]
    pallas_call x0 -> x7, Pallas kernels: none -> 80.9 us  [the longest x3 47.9 us: conv_part(): pl.pallas_call(functools.partial(conv_kernel, part, len(blocks)), grid=(P...]
    dynamic_slice x32 -> x0, local copies, waits for them, and re-layouts: 38.2 us -> none  [stem_pool(): lax.map(one_block, onehot).reshape(count // POOL_A, -1).astype(jnp.bfloat16)]
    ppermute x4 -> x24, starting transfers between devices: 15.7 us -> 43.4 us  [the longest x15 25.2 us: move(): return lax.ppermute(value, AXES, pairs)]
    ppermute x4 -> x24, waiting for transfers between devices: 0.01 us -> 18 us  [the longest x15 12.9 us: move(): return lax.ppermute(value, AXES, pairs)]
    eq x4 -> x0, local copies, waits for them, and re-layouts: 9.99 us -> none  [stem_pool(): columns[:, :, None] == codes]
    convert_element_type x3 -> x1, other arithmetic: 7.01 us -> 0.6 us  [body(): edges = jnp.stack([seq == 0, seq == 7]).astype(jnp.int32)]
  transfers between devices with their start and end apart: 7 -> 24, of which waited for: 0 -> 3; matrix products, arithmetic and copies ran while one was open for 53% -> 9% of each run, Pallas kernels for 0% -> 33%
where the time goes in v1:
time: 164 us; the launch traced here: 161 us
  Pallas kernels  80.9 us (49%)
  starting transfers between devices  43.4 us (26%)
  waiting for transfers between devices  18 us (11%)
  local copies, waits for them, and re-layouts  10.5 us (6%)
  other arithmetic  7.61 us (5%)
    pallas_call x3, Pallas kernels, conv_part(): pl.pallas_call(functools.partial(conv_kernel, part, len(blocks)), grid=(P...  47.9 us
    ppermute x15, starting transfers between devices, move(): return lax.ppermute(value, AXES, pairs)  25.2 us
    pallas_call x1, Pallas kernels, stem(): pl.pallas_call(stem_kernel, out_shape=jax.ShapeDtypeStruct((POOL_B + 4, R...  17.2 us
    ppermute x7, starting transfers between devices, body(): lax.ppermute(pair, 'seq', [(i, (i + shift) % 8) for i in range(8)])  14.4 us
    ppermute x15, waiting for transfers between devices, move(): return lax.ppermute(value, AXES, pairs)  12.9 us
    pallas_call x1, Pallas kernels, attention(): pl.pallas_call(attention_kernel, out_shape=jax.ShapeDtypeStruct((ROWS, D)...  7.1 us
    unnamed x37, local copies, waits for them, and re-layouts  6.32 us
    ppermute x1, waiting for transfers between devices, body(): high = lax.ppermute(line[:HALO], 'seq', down)  5.11 us
  transfers between devices with their start and end apart: 24, of which 3 were waited for; matrix products, arithmetic and copies ran while one was open for 9% of the time, Pallas kernels for 33%

profile of v1, /device:TPU:0, one launch (start us, length us, event | category | flops | bytes accessed | tf_op | source)
XLA Modules:
  0.0 161.4 jit_solution(11474027024825654385)
XLA Ops:
  0.0 1.0 fusion.8
  1.1 2.4 %pad_maximum_fusion.refs_0_.refs_8_ = bf16[432,1536]{1,0:T(8,128)(2,1)} fusion(bf16[96,1536]{1,0:T(8,128)(2,1)S(1)} %fusion.8, bf16[96,1536]{1,0:T(8,128)(2,1)} %param.22, bf16[240,1536]{1,0:T(8,128)(2,1)} %bitcast.36), kind=kLoop, calls=%fused_computation.4 | loop fusion | flops 3981312 | bytes 2654208 | tf_op jit(solution)/shard_map/concatenate | solution.py:426
  3.5 4.2 %collective-permute-start.2 = (bf16[432,1536]{1,0:T(8,128)(2,1)}, bf16[432,1536]{1,0:T(8,128)(2,1)}, u32[]{:S(2)}, u32[]{:S(2)}) collective-permute-start(bf16[432,1536]{1,0:T(8,128)(2,1)} %pad_maximum_fusion.refs_0_.refs_8_), channel_id=1, source_target_pairs={{0,48},{1,49},{2,18},{3,19},{4,52},{5,53},{6,22},{7,23},{8,24},{9,... | collective-permute-start | bytes 3981320 | tf_op jit(solution)/shard_map/ppermute | solution.py:400
  7.6 3.0 %collective-permute-start.15 = (bf16[432,1536]{1,0:T(8,128)(2,1)}, bf16[432,1536]{1,0:T(8,128)(2,1)}, u32[]{:S(2)}, u32[]{:S(2)}) collective-permute-start(bf16[432,1536]{1,0:T(8,128)(2,1)} %pad_maximum_fusion.refs_0_.refs_8_), channel_id=1, source_target_pairs={{0,65},{1,64},{2,67},{3,66},{4,69},{5,68},{6,71},{7,70},{8,72},{9,... | collective-permute-start | bytes 3981320 | tf_op jit(solution)/shard_map/ppermute | solution.py:400
  10.7 2.5 %collective-permute-start.1 = (s32[24]{0:T(128)S(1)}, s32[24]{0:T(128)S(1)}, u32[]{:S(2)}, u32[]{:S(2)}) collective-permute-start(s32[24]{0:T(128)S(1)} %get-tuple-element.14), channel_id=1, source_target_pairs={{0,1},{1,2},{2,3},{3,4},{4,5},{5,6},{6,7},{8,9},{9,10},{10,11},{11... | collective-permute-start | bytes 296 | tf_op jit(solution)/shard_map/ppermute | solution.py:420
  13.3 1.3 broadcast_multiply_fusion
  17.1 6.2 %collective-permute-done.2.refs_3_.refs_11_ = bf16[432,1536]{1,0:T(8,128)(2,1)} collective-permute-done((bf16[432,1536]{1,0:T(8,128)(2,1)}, bf16[432,1536]{1,0:T(8,128)(2,1)}, u32[]{:S(2)}, u32[]{:S(2)}) %collective-permute-start.2) | collective-permute-done | bytes 1327136 | tf_op jit(solution)/shard_map/ppermute | solution.py:400
  23.2 3.7 %collective-permute-start.3 = (bf16[432,1536]{1,0:T(8,128)(2,1)}, bf16[432,1536]{1,0:T(8,128)(2,1)S(1)}, u32[]{:S(2)}, u32[]{:S(2)}) collective-permute-start(bf16[432,1536]{1,0:T(8,128)(2,1)} %collective-permute-done.2.refs_3_.refs_11_), channel_id=1, source_target_pairs={{0,48},{1,49},{2,18},{3,19},{4,52},{5,53},{6,22},{7,23},{8,24},{9,... | collective-permute-start | bytes 3981320 | tf_op jit(solution)/shard_map/ppermute | solution.py:400
  26.9 3.0 %collective-permute-start.5 = (bf16[432,1536]{1,0:T(8,128)(2,1)}, bf16[432,1536]{1,0:T(8,128)(2,1)S(1)}, u32[]{:S(2)}, u32[]{:S(2)}) collective-permute-start(bf16[432,1536]{1,0:T(8,128)(2,1)} %collective-permute-done.2.refs_3_.refs_11_), channel_id=1, source_target_pairs={{0,65},{1,64},{2,67},{3,66},{4,69},{5,68},{6,71},{7,70},{8,72},{9,... | collective-permute-start | bytes 3981320 | tf_op jit(solution)/shard_map/ppermute | solution.py:400
  31.6 0.7 bitcast_dynamic-update-slice_fusion.6
  32.3 0.7 copy.21.cosine
  33.0 1.3 collective-permute-start
  34.9 5.1 %collective-permute-done = s32[24]{0:T(128)S(1)} collective-permute-done((s32[24]{0:T(128)S(1)}, s32[24]{0:T(128)S(1)}, u32[]{:S(2)}, u32[]{:S(2)}) %collective-permute-start) | collective-permute-done | bytes 128 | tf_op jit(solution)/shard_map/ppermute | solution.py:421
  40.0 2.2 %collective-permute-start.11 = (bf16[432,1536]{1,0:T(8,128)(2,1)}, bf16[432,1536]{1,0:T(8,128)(2,1)}, u32[]{:S(2)}, u32[]{:S(2)}) collective-permute-start(bf16[432,1536]{1,0:T(8,128)(2,1)} %collective-permute-done.2.refs_3_.refs_11_), channel_id=1, source_target_pairs={{0,8},{1,9},{2,10},{3,11},{4,12},{5,13},{6,14},{7,15},{8,0},{9,1},... | collective-permute-start | bytes 3981320 | tf_op jit(solution)/shard_map/ppermute | solution.py:400
  42.2 5.4 %collective-permute-start.12 = (bf16[432,1536]{1,0:T(8,128)(2,1)}, bf16[432,1536]{1,0:T(8,128)(2,1)}, u32[]{:S(2)}, u32[]{:S(2)}) collective-permute-start(bf16[432,1536]{1,0:T(8,128)(2,1)} %collective-permute-done.2.refs_3_.refs_11_), channel_id=1, source_target_pairs={{0,6},{1,7},{2,0},{3,1},{4,2},{5,3},{6,4},{7,5},{8,10},{9,11},{10,... | collective-permute-start | bytes 3981320 | tf_op jit(solution)/shard_map/ppermute | solution.py:400
  47.7 0.7 pad_maximum_fusion.1.sine
  52.0 2.2 %collective-permute-start.7 = (bf16[432,1536]{1,0:T(8,128)(2,1)S(1)}, bf16[432,1536]{1,0:T(8,128)(2,1)}, u32[]{:S(2)}, u32[]{:S(2)}) collective-permute-start(bf16[432,1536]{1,0:T(8,128)(2,1)S(1)} %collective-permute-done.5.refs_3_.refs_8_.refs_16_), channel_id=1, source_target_pairs={{0,6},{1,7},{2,0},{3,1},{4,2},{5,3},{6,4},{7,5},{8,10},{9,11},{10,... | collective-permute-start | bytes 3981320 | tf_op jit(solution)/shard_map/ppermute | solution.py:400
  55.6 0.7 pad_add_fusion.tokens
  56.6 6.7 %collective-permute-done.12.refs_1_.refs_6_.refs_14_ = bf16[432,1536]{1,0:T(8,128)(2,1)} collective-permute-done((bf16[432,1536]{1,0:T(8,128)(2,1)}, bf16[432,1536]{1,0:T(8,128)(2,1)}, u32[]{:S(2)}, u32[]{:S(2)}) %collective-permute-start.12) | collective-permute-done | bytes 1327136 | tf_op jit(solution)/shard_map/ppermute | solution.py:400
  63.3 17.2 %stem.1.rows = bf16[20,128,768]{2,1,0:T(8,128)(2,1)} custom-call(s32[2]{0:T(128)} %add_convert_fusion.edges, s32[144,128]{1,0:T(8,128)} %pad_add_fusion.tokens, bf16[8,128,768]{2,1,0:T(8,128)(2,1)} %bitcast_dynamic-update-slice_fusion.taps, f32[1,768]{1,0:T(1,128)} %broadcast_in_dim.53.bias, f32[1,768]{1,0:T(1,128)} %broadcast_in_dim.55.gain), custom_call_target="tpu_custom_call" | custom-call | flops 7000000000 | bytes 5000000 | tf_op jit(solution)/shard_map/stem/pallas_call | solution.py:152
  81.7 14.3 %conv.3.refs_6_ = f32[2048,1536]{1,0:T(8,128)} custom-call(bf16[20,128,768]{2,1,0:T(8,128)(2,1)} %stem.1.rows, bf16[432,1536]{1,0:T(8,128)(2,1)} %pad_maximum_fusion.refs_0_.refs_8_, bf16[432,1536]{1,0:T(8,128)(2,1)} %collective-permute-done.14.refs_1_.refs_9_, bf16[432,1536]{1,0:T(8,128)(2,1)} %collective-permute-done.15.refs_2_.refs_10_, ...), custom_call_target="tpu_custom_call" | custom-call | flops 8053063680 | bytes 20000000 | tf_op jit(solution)/shard_map/conv/pallas_call | solution.py:273
  96.0 16.3 %conv.4.refs_6_ = f32[2048,1536]{1,0:T(8,128)} custom-call(bf16[20,128,768]{2,1,0:T(8,128)(2,1)} %stem.1.rows, bf16[432,1536]{1,0:T(8,128)(2,1)} %collective-permute-done.11.refs_5_.refs_0_.refs_13_, bf16[432,1536]{1,0:T(8,128)(2,1)} %collective-permute-done.12.refs_1_.refs_6_.refs_14_, bf16[432,1536]{1,0:T(8,128)(2,1)} %copy-done.1, ...), custom_call_target="tpu_custom_call" | custom-call | flops 8053063680 | bytes 20000000 | tf_op jit(solution)/shard_map/conv/pallas_call | solution.py:273
  112.3 17.4 %conv.5.coarse = bf16[128,1536]{1,0:T(8,128)(2,1)} custom-call(bf16[20,128,768]{2,1,0:T(8,128)(2,1)} %stem.1.rows, bf16[432,1536]{1,0:T(8,128)(2,1)} %collective-permute-done.4.refs_5_.refs_0_.refs_10_.refs_18_, bf16[432,1536]{1,0:T(8,128)(2,1)} %collective-permute-done.6.refs_1_.refs_11_.refs_19_, ...), custom_call_target="tpu_custom_call" | custom-call | flops 8053063680 | bytes 20000000 | tf_op jit(solution)/shard_map/conv/pallas_call | solution.py:273
  129.7 3.6 %keys.1 = (bf16[128,1536]{1,0:T(8,128)(2,1)}, bf16[128,384]{1,0:T(8,128)(2,1)}) custom-call(s32[16]{0:T(128)} %get-tuple-element.12.order, bf16[128,1536]{1,0:T(8,128)(2,1)} %conv.5.coarse, f32[1,1536]{1,0:T(1,128)} %broadcast_in_dim.57.gain, f32[128,128]{1,0:T(8,128)} %copy.21.cosine, f32[128,128]{1,0:T(8,128)} %pad_maximum_fusion.1.sine, ...), custom_call_target="tpu_custom_call" | custom-call | flops 150000000 | bytes 2000000 | tf_op jit(solution)/shard_map/keys/pallas_call | solution.py:324
  133.4 1.3 collective-permute-start.18
  134.6 6.2 %collective-permute-start.19 = (bf16[128,384]{1,0:T(8,128)(2,1)}, bf16[128,384]{1,0:T(8,128)(2,1)S(1)}, u32[]{:S(2)}, u32[]{:S(2)}) collective-permute-start(bf16[128,384]{1,0:T(8,128)(2,1)} %get-tuple-element.8.refs_0_), channel_id=1, source_target_pairs={{0,3},{1,4},{2,5},{3,6},{4,7},{5,0},{6,1},{7,2},{8,11},{9,12},{10,... | collective-permute-start | bytes 294920 | tf_op jit(solution)/shard_map/ppermute | solution.py:474
  140.9 0.8 collective-permute-start.20
  141.7 2.9 %collective-permute-start.21 = (bf16[128,384]{1,0:T(8,128)(2,1)}, bf16[128,384]{1,0:T(8,128)(2,1)S(1)}, u32[]{:S(2)}, u32[]{:S(2)}) collective-permute-start(bf16[128,384]{1,0:T(8,128)(2,1)} %get-tuple-element.8.refs_0_), channel_id=1, source_target_pairs={{0,5},{1,6},{2,7},{3,0},{4,1},{5,2},{6,3},{7,4},{8,13},{9,14},{10,... | collective-permute-start | bytes 294920 | tf_op jit(solution)/shard_map/ppermute | solution.py:474
  144.5 1.2 collective-permute-start.22
  145.8 1.9 %collective-permute-start.23 = (bf16[128,384]{1,0:T(8,128)(2,1)}, bf16[128,384]{1,0:T(8,128)(2,1)S(1)}, u32[]{:S(2)}, u32[]{:S(2)}) collective-permute-start(bf16[128,384]{1,0:T(8,128)(2,1)} %get-tuple-element.8.refs_0_), channel_id=1, source_target_pairs={{0,7},{1,0},{2,1},{3,2},{4,3},{5,4},{6,5},{7,6},{8,15},{9,8},{10,9... | collective-permute-start | bytes 294920 | tf_op jit(solution)/shard_map/ppermute | solution.py:474
  147.7 5.0 %query.1 = bf16[8,128,128]{2,1,0:T(8,128)(2,1)} custom-call(s32[16]{0:T(128)} %get-tuple-element.12.order, bf16[128,1536]{1,0:T(8,128)(2,1)} %get-tuple-element.7.hidden, f32[128,128]{1,0:T(8,128)} %copy.21.cosine, f32[128,128]{1,0:T(8,128)} %pad_maximum_fusion.1.sine, bf16[432,1536]{1,0:T(8,128)(2,1)} %pad_maximum_fusion.refs_0_.refs_8_, ...), custom_call_target="tpu_custom_call" | custom-call | flops 1600000000 | bytes 4000000 | tf_op jit(solution)/shard_map/query/pallas_call | solution.py:351
  154.2 7.1 %attention.1 = bf16[128,1536]{1,0:T(8,128)(2,1)} custom-call(s32[16]{0:T(128)} %get-tuple-element.12.order, bf16[128,1536]{1,0:T(8,128)(2,1)} %conv.5.coarse, bf16[8,128,128]{2,1,0:T(8,128)(2,1)} %query.1, bf16[128,384]{1,0:T(8,128)(2,1)} %get-tuple-element.8.refs_0_, bf16[128,384]{1,0:T(8,128)(2,1)} %copy-done.3, bf16[128,384]{1,0:T(8,128)(2,1)} %copy-done.4, ...), custom_call_target="tpu_custom_call" | custom-call | flops 3000000000 | bytes 6000000 | tf_op jit(solution)/shard_map/attention/pallas_call | solution.py:387
  (86 shorter events, 12.6 us)
Async XLA Ops:
  0.0 30.3 %copy-start = (bf16[60,768]{1,0:T(8,128)(2,1)S(1)}, bf16[60,768]{1,0:T(8,128)(2,1)}, u32[]{:S(2)}) copy-start(bf16[60,768]{1,0:T(8,128)(2,1)} %param.13) | copy-start | bytes 276484
  0.0 10.6 %copy-start.10 = (s32[1,16384]{1,0:T(1,128)S(1)}, s32[1,16384]{1,0:T(1,128)}, u32[]{:S(2)}) copy-start(s32[1,16384]{1,0:T(1,128)} %param.12) | copy-start | bytes 196612
  0.0 14.7 %copy-start.14 = (f32[768]{0:T(1024)S(1)}, f32[768]{0:T(1024)}, u32[]{:S(2)}) copy-start(f32[768]{0:T(1024)} %param.14) | copy-start | bytes 9220
  0.0 14.7 %copy-start.13 = (f32[768]{0:T(1024)S(1)}, f32[768]{0:T(1024)}, u32[]{:S(2)}) copy-start(f32[768]{0:T(1024)} %param.15) | copy-start | bytes 9220
  0.0 16.5 %copy-start.11 = (f32[1536]{0:T(1024)S(1)}, f32[1536]{0:T(1024)}, u32[]{:S(2)}) copy-start(f32[1536]{0:T(1024)} %param.17) | copy-start | bytes 18436
  3.4 30.9 %copy-start.12 = (f32[1536]{0:T(1024)S(1)}, f32[1536]{0:T(1024)}, u32[]{:S(2)}) copy-start(f32[1536]{0:T(1024)} %param.18) | copy-start | bytes 18436
  3.5 19.8 %collective-permute-start.2 = (bf16[432,1536]{1,0:T(8,128)(2,1)}, bf16[432,1536]{1,0:T(8,128)(2,1)}, u32[]{:S(2)}, u32[]{:S(2)}) collective-permute-start(bf16[432,1536]{1,0:T(8,128)(2,1)} %pad_maximum_fusion.refs_0_.refs_8_), channel_id=1, source_target_pairs={{0,48},{1,49},{2,18},{3,19},{4,52},{5,53},{6,22},{7,23},{8,24},{9,... | collective-permute-start | bytes 3981320 | tf_op jit(solution)/shard_map/ppermute | solution.py:400
  7.6 34.6 %collective-permute-start.15 = (bf16[432,1536]{1,0:T(8,128)(2,1)}, bf16[432,1536]{1,0:T(8,128)(2,1)}, u32[]{:S(2)}, u32[]{:S(2)}) collective-permute-start(bf16[432,1536]{1,0:T(8,128)(2,1)} %pad_maximum_fusion.refs_0_.refs_8_), channel_id=1, source_target_pairs={{0,65},{1,64},{2,67},{3,66},{4,69},{5,68},{6,71},{7,70},{8,72},{9,... | collective-permute-start | bytes 3981320 | tf_op jit(solution)/shard_map/ppermute | solution.py:400
  10.6 41.3 %collective-permute-start.14 = (bf16[432,1536]{1,0:T(8,128)(2,1)}, bf16[432,1536]{1,0:T(8,128)(2,1)}, u32[]{:S(2)}, u32[]{:S(2)}) collective-permute-start(bf16[432,1536]{1,0:T(8,128)(2,1)} %pad_maximum_fusion.refs_0_.refs_8_), channel_id=1, source_target_pairs={{0,8},{1,9},{2,10},{3,11},{4,12},{5,13},{6,14},{7,15},{8,0},{9,1},... | collective-permute-start | bytes 3981320 | tf_op jit(solution)/shard_map/ppermute | solution.py:400
  10.7 22.3 %collective-permute-start.1 = (s32[24]{0:T(128)S(1)}, s32[24]{0:T(128)S(1)}, u32[]{:S(2)}, u32[]{:S(2)}) collective-permute-start(s32[24]{0:T(128)S(1)} %get-tuple-element.14), channel_id=1, source_target_pairs={{0,1},{1,2},{2,3},{3,4},{4,5},{5,6},{6,7},{8,9},{9,10},{10,11},{11... | collective-permute-start | bytes 296 | tf_op jit(solution)/shard_map/ppermute | solution.py:420
  23.2 28.7 %collective-permute-start.3 = (bf16[432,1536]{1,0:T(8,128)(2,1)}, bf16[432,1536]{1,0:T(8,128)(2,1)S(1)}, u32[]{:S(2)}, u32[]{:S(2)}) collective-permute-start(bf16[432,1536]{1,0:T(8,128)(2,1)} %collective-permute-done.2.refs_3_.refs_11_), channel_id=1, source_target_pairs={{0,48},{1,49},{2,18},{3,19},{4,52},{5,53},{6,22},{7,23},{8,24},{9,... | collective-permute-start | bytes 3981320 | tf_op jit(solution)/shard_map/ppermute | solution.py:400
  26.9 25.1 %collective-permute-start.5 = (bf16[432,1536]{1,0:T(8,128)(2,1)}, bf16[432,1536]{1,0:T(8,128)(2,1)S(1)}, u32[]{:S(2)}, u32[]{:S(2)}) collective-permute-start(bf16[432,1536]{1,0:T(8,128)(2,1)} %collective-permute-done.2.refs_3_.refs_11_), channel_id=1, source_target_pairs={{0,65},{1,64},{2,67},{3,66},{4,69},{5,68},{6,71},{7,70},{8,72},{9,... | collective-permute-start | bytes 3981320 | tf_op jit(solution)/shard_map/ppermute | solution.py:400
  33.0 7.0 %collective-permute-start = (s32[24]{0:T(128)S(1)}, s32[24]{0:T(128)S(1)}, u32[]{:S(2)}, u32[]{:S(2)}) collective-permute-start(s32[24]{0:T(128)S(1)} %get-tuple-element.13), channel_id=1, source_target_pairs={{1,0},{2,1},{3,2},{4,3},{5,4},{6,5},{7,6},{9,8},{10,9},{11,10},{12... | collective-permute-start | bytes 296 | tf_op jit(solution)/shard_map/ppermute | solution.py:421
  40.0 16.3 %collective-permute-start.11 = (bf16[432,1536]{1,0:T(8,128)(2,1)}, bf16[432,1536]{1,0:T(8,128)(2,1)}, u32[]{:S(2)}, u32[]{:S(2)}) collective-permute-start(bf16[432,1536]{1,0:T(8,128)(2,1)} %collective-permute-done.2.refs_3_.refs_11_), channel_id=1, source_target_pairs={{0,8},{1,9},{2,10},{3,11},{4,12},{5,13},{6,14},{7,15},{8,0},{9,1},... | collective-permute-start | bytes 3981320 | tf_op jit(solution)/shard_map/ppermute | solution.py:400
  42.2 21.0 %collective-permute-start.12 = (bf16[432,1536]{1,0:T(8,128)(2,1)}, bf16[432,1536]{1,0:T(8,128)(2,1)}, u32[]{:S(2)}, u32[]{:S(2)}) collective-permute-start(bf16[432,1536]{1,0:T(8,128)(2,1)} %collective-permute-done.2.refs_3_.refs_11_), channel_id=1, source_target_pairs={{0,6},{1,7},{2,0},{3,1},{4,2},{5,3},{6,4},{7,5},{8,10},{9,11},{10,... | collective-permute-start | bytes 3981320 | tf_op jit(solution)/shard_map/ppermute | solution.py:400
  51.9 28.6 %collective-permute-start.16 = (bf16[432,1536]{1,0:T(8,128)(2,1)}, bf16[432,1536]{1,0:T(8,128)(2,1)}, u32[]{:S(2)}, u32[]{:S(2)}) collective-permute-start(bf16[432,1536]{1,0:T(8,128)(2,1)} %collective-permute-done.15.refs_2_.refs_10_), channel_id=1, source_target_pairs={{0,8},{1,9},{2,10},{3,11},{4,12},{5,13},{6,14},{7,15},{8,0},{9,1},... | collective-permute-start | bytes 3981320 | tf_op jit(solution)/shard_map/ppermute | solution.py:400
  51.9 28.6 %copy-start.1 = (bf16[432,1536]{1,0:T(8,128)(2,1)}, bf16[432,1536]{1,0:T(8,128)(2,1)S(1)}, u32[]{:S(2)}) copy-start(bf16[432,1536]{1,0:T(8,128)(2,1)S(1)} %collective-permute-done.3.refs_2_.refs_7_.refs_15_) | copy-start | bytes 3981316
  51.9 29.2 %collective-permute-start.8 = (bf16[432,1536]{1,0:T(8,128)(2,1)S(1)}, bf16[432,1536]{1,0:T(8,128)(2,1)}, u32[]{:S(2)}, u32[]{:S(2)}) collective-permute-start(bf16[432,1536]{1,0:T(8,128)(2,1)S(1)} %collective-permute-done.3.refs_2_.refs_7_.refs_15_), channel_id=1, source_target_pairs={{0,65},{1,64},{2,67},{3,66},{4,69},{5,68},{6,71},{7,70},{8,72},{9,... | collective-permute-start | bytes 3981320 | tf_op jit(solution)/shard_map/ppermute | solution.py:400
  52.0 28.5 %copy-start.2 = (bf16[432,1536]{1,0:T(8,128)(2,1)}, bf16[432,1536]{1,0:T(8,128)(2,1)S(1)}, u32[]{:S(2)}) copy-start(bf16[432,1536]{1,0:T(8,128)(2,1)S(1)} %collective-permute-done.5.refs_3_.refs_8_.refs_16_) | copy-start | bytes 3981316
  52.0 29.2 %collective-permute-start.7 = (bf16[432,1536]{1,0:T(8,128)(2,1)S(1)}, bf16[432,1536]{1,0:T(8,128)(2,1)}, u32[]{:S(2)}, u32[]{:S(2)}) collective-permute-start(bf16[432,1536]{1,0:T(8,128)(2,1)S(1)} %collective-permute-done.5.refs_3_.refs_8_.refs_16_), channel_id=1, source_target_pairs={{0,6},{1,7},{2,0},{3,1},{4,2},{5,3},{6,4},{7,5},{8,10},{9,11},{10,... | collective-permute-start | bytes 3981320 | tf_op jit(solution)/shard_map/ppermute | solution.py:400
  56.3 39.6 %collective-permute-start.4 = (bf16[432,1536]{1,0:T(8,128)(2,1)S(1)}, bf16[432,1536]{1,0:T(8,128)(2,1)}, u32[]{:S(2)}, u32[]{:S(2)}) collective-permute-start(bf16[432,1536]{1,0:T(8,128)(2,1)S(1)} %collective-permute-done.3.refs_2_.refs_7_.refs_15_), channel_id=1, source_target_pairs={{0,8},{1,9},{2,10},{3,11},{4,12},{5,13},{6,14},{7,15},{8,0},{9,1},... | collective-permute-start | bytes 3981320 | tf_op jit(solution)/shard_map/ppermute | solution.py:400
  63.3 32.6 %collective-permute-start.13 = (bf16[432,1536]{1,0:T(8,128)(2,1)}, bf16[432,1536]{1,0:T(8,128)(2,1)}, u32[]{:S(2)}, u32[]{:S(2)}) collective-permute-start(bf16[432,1536]{1,0:T(8,128)(2,1)} %collective-permute-done.12.refs_1_.refs_6_.refs_14_), channel_id=1, source_target_pairs={{0,8},{1,9},{2,10},{3,11},{4,12},{5,13},{6,14},{7,15},{8,0},{9,1},... | collective-permute-start | bytes 3981320 | tf_op jit(solution)/shard_map/ppermute | solution.py:400
  80.5 31.7 %collective-permute-start.6 = (bf16[432,1536]{1,0:T(8,128)(2,1)S(1)}, bf16[432,1536]{1,0:T(8,128)(2,1)}, u32[]{:S(2)}, u32[]{:S(2)}) collective-permute-start(bf16[432,1536]{1,0:T(8,128)(2,1)S(1)} %collective-permute-done.5.refs_3_.refs_8_.refs_16_), channel_id=1, source_target_pairs={{0,8},{1,9},{2,10},{3,11},{4,12},{5,13},{6,14},{7,15},{8,0},{9,1},... | collective-permute-start | bytes 3981320 | tf_op jit(solution)/shard_map/ppermute | solution.py:400
  81.1 31.1 %collective-permute-start.10 = (bf16[432,1536]{1,0:T(8,128)(2,1)}, bf16[432,1536]{1,0:T(8,128)(2,1)}, u32[]{:S(2)}, u32[]{:S(2)}) collective-permute-start(bf16[432,1536]{1,0:T(8,128)(2,1)} %collective-permute-done.8.refs_3_.refs_13_.refs_21_), channel_id=1, source_target_pairs={{0,8},{1,9},{2,10},{3,11},{4,12},{5,13},{6,14},{7,15},{8,0},{9,1},... | collective-permute-start | bytes 3981320 | tf_op jit(solution)/shard_map/ppermute | solution.py:400
  81.2 31.0 %collective-permute-start.9 = (bf16[432,1536]{1,0:T(8,128)(2,1)}, bf16[432,1536]{1,0:T(8,128)(2,1)}, u32[]{:S(2)}, u32[]{:S(2)}) collective-permute-start(bf16[432,1536]{1,0:T(8,128)(2,1)} %collective-permute-done.7.refs_2_.refs_12_.refs_20_), channel_id=1, source_target_pairs={{0,8},{1,9},{2,10},{3,11},{4,12},{5,13},{6,14},{7,15},{8,0},{9,1},... | collective-permute-start | bytes 3981320 | tf_op jit(solution)/shard_map/ppermute | solution.py:400
  133.3 11.2 %collective-permute-start.17 = (bf16[128,384]{1,0:T(8,128)(2,1)}, bf16[128,384]{1,0:T(8,128)(2,1)S(1)}, u32[]{:S(2)}, u32[]{:S(2)}) collective-permute-start(bf16[128,384]{1,0:T(8,128)(2,1)} %get-tuple-element.8.refs_0_), channel_id=1, source_target_pairs={{0,1},{1,2},{2,3},{3,4},{4,5},{5,6},{6,7},{7,0},{8,9},{9,10},{10,1... | collective-permute-start | bytes 294920 | tf_op jit(solution)/shard_map/ppermute | solution.py:474
  133.4 12.4 %collective-permute-start.18 = (bf16[128,384]{1,0:T(8,128)(2,1)}, bf16[128,384]{1,0:T(8,128)(2,1)S(1)}, u32[]{:S(2)}, u32[]{:S(2)}) collective-permute-start(bf16[128,384]{1,0:T(8,128)(2,1)} %get-tuple-element.8.refs_0_), channel_id=1, source_target_pairs={{0,2},{1,3},{2,4},{3,5},{4,6},{5,7},{6,0},{7,1},{8,10},{9,11},{10,... | collective-permute-start | bytes 294920 | tf_op jit(solution)/shard_map/ppermute | solution.py:474
  134.6 18.1 %collective-permute-start.19 = (bf16[128,384]{1,0:T(8,128)(2,1)}, bf16[128,384]{1,0:T(8,128)(2,1)S(1)}, u32[]{:S(2)}, u32[]{:S(2)}) collective-permute-start(bf16[128,384]{1,0:T(8,128)(2,1)} %get-tuple-element.8.refs_0_), channel_id=1, source_target_pairs={{0,3},{1,4},{2,5},{3,6},{4,7},{5,0},{6,1},{7,2},{8,11},{9,12},{10,... | collective-permute-start | bytes 294920 | tf_op jit(solution)/shard_map/ppermute | solution.py:474
  140.9 11.9 %collective-permute-start.20 = (bf16[128,384]{1,0:T(8,128)(2,1)}, bf16[128,384]{1,0:T(8,128)(2,1)S(1)}, u32[]{:S(2)}, u32[]{:S(2)}) collective-permute-start(bf16[128,384]{1,0:T(8,128)(2,1)} %get-tuple-element.8.refs_0_), channel_id=1, source_target_pairs={{0,4},{1,5},{2,6},{3,7},{4,0},{5,1},{6,2},{7,3},{8,12},{9,13},{10,... | collective-permute-start | bytes 294920 | tf_op jit(solution)/shard_map/ppermute | solution.py:474
  141.7 11.1 %collective-permute-start.21 = (bf16[128,384]{1,0:T(8,128)(2,1)}, bf16[128,384]{1,0:T(8,128)(2,1)S(1)}, u32[]{:S(2)}, u32[]{:S(2)}) collective-permute-start(bf16[128,384]{1,0:T(8,128)(2,1)} %get-tuple-element.8.refs_0_), channel_id=1, source_target_pairs={{0,5},{1,6},{2,7},{3,0},{4,1},{5,2},{6,3},{7,4},{8,13},{9,14},{10,... | collective-permute-start | bytes 294920 | tf_op jit(solution)/shard_map/ppermute | solution.py:474
  144.5 8.3 %collective-permute-start.22 = (bf16[128,384]{1,0:T(8,128)(2,1)}, bf16[128,384]{1,0:T(8,128)(2,1)S(1)}, u32[]{:S(2)}, u32[]{:S(2)}) collective-permute-start(bf16[128,384]{1,0:T(8,128)(2,1)} %get-tuple-element.8.refs_0_), channel_id=1, source_target_pairs={{0,6},{1,7},{2,0},{3,1},{4,2},{5,3},{6,4},{7,5},{8,14},{9,15},{10,... | collective-permute-start | bytes 294920 | tf_op jit(solution)/shard_map/ppermute | solution.py:474
  145.8 7.0 %collective-permute-start.23 = (bf16[128,384]{1,0:T(8,128)(2,1)}, bf16[128,384]{1,0:T(8,128)(2,1)S(1)}, u32[]{:S(2)}, u32[]{:S(2)}) collective-permute-start(bf16[128,384]{1,0:T(8,128)(2,1)} %get-tuple-element.8.refs_0_), channel_id=1, source_target_pairs={{0,7},{1,0},{2,1},{3,2},{4,3},{5,4},{6,5},{7,6},{8,15},{9,8},{10,9... | collective-permute-start | bytes 294920 | tf_op jit(solution)/shard_map/ppermute | solution.py:474
  (7 other events, 18.5 us)

commit v2 on v1

v2 whole, which is shorter than its diff:
```python
import functools

import jax
import jax.numpy as jnp
import numpy as np
from jax import lax
from jax.experimental import pallas as pl
from jax.experimental.pallas import tpu as pltpu
from jax.sharding import PartitionSpec as P

D_STEM = 768
D = 1536
HEADS = 8
HEAD_K = 128
HEAD_V = 192
KW_STEM = 15
KW = 5
POOL_A = 8
POOL_B = 16
SHARDS = 16
CONV_ROWS = D_STEM // SHARDS
PROJ_ROWS = D // SHARDS
OUT_AT = KW * CONV_ROWS
QKV_AT = OUT_AT + PROJ_ROWS
BLOCK_ROWS = QKV_AT + PROJ_ROWS
CHUNK = 256
ROWS = 128
HALO = 24
EPSILON = 1e-06
AXES = ("dp", "seq")
VMEM_LIMIT = 60 * 1024 * 1024


def device_of(x, y, z, core):
    x, y, z = x % 4, y % 4, z % 4
    return ((y % 2) * 8 + z * 2 + core) * 8 + (x * 2 + y // 2)


def received_from(source):
    pairs = []
    for x in range(4):
        for y in range(4):
            for z in range(4):
                for core in range(2):
                    pairs.append((device_of(*source(x, y, z, core)), device_of(x, y, z, core)))
    return sorted(pairs)


def side(core):
    return 1 - 2 * core


def turn(x, core):
    return 1 - 2 * ((x + core) % 2)


FROM_Y = received_from(lambda x, y, z, core: (x, y + side(core), z, core))
FROM_X = received_from(lambda x, y, z, core: (x + side(core), y, z, core))
FROM_Z = received_from(lambda x, y, z, core: (x, y, z + turn(x, core), core))
FROM_CORE = received_from(lambda x, y, z, core: (x, y, z, 1 - core))


def shard_order():
    orders = np.zeros((SHARDS, 8, SHARDS), np.int32)
    for dp in range(SHARDS):
        for seq in range(8):
            y_low, z, core, x = dp // 8, (dp // 2) % 4, dp % 2, seq // 2

            def names(c):
                turned = turn(x, c)

                def shard(other, dz):
                    return (y_low ^ other) * 8 + (z + dz) % 4 * 2 + c

                return dict(
                    own=shard(0, 0), y=shard(1, 0), za=shard(0, turned), zb=shard(0, -turned),
                    zz=shard(0, 2), yza=shard(1, turned), yzb=shard(1, -turned), yzz=shard(1, 2),
                )

            mine, other = names(core), names(1 - core)
            order = [mine["own"], other["own"], mine["y"], mine["za"], other["y"], other["za"]]
            order += [mine["zb"], mine["zz"], mine["yza"], other["zb"], other["zz"], other["yza"]]
            order += [mine["yzb"], mine["yzz"], other["yzb"], other["yzz"]]
            orders[dp, seq] = order
    return orders


def trig():
    half = HEAD_K // 2
    freqs = np.float32(10000.0) ** (-np.arange(half, dtype=np.float32) / np.float32(half))
    angles = np.arange(8 * ROWS, dtype=np.float32)[:, None] * freqs[None, :]
    cosine, sine = np.cos(angles.astype(np.float64)), np.sin(angles.astype(np.float64))
    table = [np.concatenate([cosine, cosine], axis=1), np.concatenate([-sine, sine], axis=1)]
    return np.stack([t.reshape(8, ROWS, HEAD_K) for t in table], axis=1).astype(np.float32)


PLACES = np.concatenate(
    [shard_order(), np.broadcast_to(np.arange(8, dtype=np.int32)[None, :, None], (SHARDS, 8, 1))], axis=2
)
ANGLES = trig()


def dot(a, b):
    return jnp.dot(a, b, preferred_element_type=jnp.float32)


def gelu(x):
    return jax.nn.gelu(x)


STEM_ROWS = 512
FULL = POOL_B * ROWS


def hits_of(wide, g):
    width = wide.shape[1]
    token = lax.broadcasted_iota(jnp.int32, (width, 128), 0)
    lane = lax.broadcasted_iota(jnp.int32, (width, 128), 1)
    pick = (token == 120 + 8 * g + lane // 4).astype(jnp.float32).astype(jnp.bfloat16)
    spread = dot(wide, pick)
    code = (lax.broadcasted_iota(jnp.int32, spread.shape, 1) % 4 + 1).astype(jnp.float32)
    return (spread == code).astype(jnp.float32)


def strongest(rows, taps, columns):
    most = dot(rows, taps[0:128, columns])
    for offset in range(1, POOL_A):
        most = jnp.maximum(most, dot(rows, taps[offset * 128 : (offset + 1) * 128, columns]))
    return most


def stem_norm(most, bias, gain):
    pooled = gelu(most + bias).astype(jnp.bfloat16).astype(jnp.float32)
    scale = lax.rsqrt(jnp.mean(pooled * pooled, axis=-1, keepdims=True) + EPSILON)
    return pooled * scale * gain


def stem_kernel(order, tokens, weight, bias, gain, out, taps, vectors, hits, best):
    lane = lax.broadcasted_iota(jnp.int32, (D_STEM, D_STEM), 1)
    source = lax.broadcasted_iota(jnp.int32, (1, D_STEM), 1)
    for i in range(SHARDS):
        here = lax.broadcasted_iota(jnp.int32, (1, D_STEM), 1)
        source = jnp.where(here >= i * CONV_ROWS, here + (order[i] - i) * CONV_ROWS, source)
    channel = lax.broadcasted_iota(jnp.int32, (D_STEM, D_STEM), 0)
    chosen = (channel == source).astype(jnp.float32).astype(jnp.bfloat16)
    parts = []
    for vector in (bias[...], gain[...]):
        for _ in range(3):
            parts.append(vector.astype(jnp.bfloat16).astype(jnp.float32))
            vector = vector - parts[-1]
    parts = jnp.concatenate(parts + [jnp.zeros((10, D_STEM), jnp.float32)], axis=0)
    parts = dot(parts.astype(jnp.bfloat16), chosen)
    vectors[0:1] = parts[0:1] + parts[1:2] + parts[2:3]
    vectors[1:2] = parts[3:4] + parts[4:5] + parts[5:6]
    vectors[2:] = jnp.zeros((6, D_STEM), jnp.float32)
    moved = dot(weight[...], chosen).astype(jnp.bfloat16)
    row = lax.broadcasted_iota(jnp.int32, (POOL_A * 128, 4 * KW_STEM), 0)
    tap = lax.broadcasted_iota(jnp.int32, (POOL_A * 128, 4 * KW_STEM), 1)
    place = (row % 128 == tap + 4 * (row // 128 + 1)).astype(jnp.float32).astype(jnp.bfloat16)
    taps[...] = dot(place, moved).astype(jnp.bfloat16)

    held = tokens[...].astype(jnp.float32)
    before, after = pltpu.roll(held, 1, 0), pltpu.roll(held, ROWS - 1, 0)
    wide = jnp.concatenate([before, held, after], axis=1).astype(jnp.bfloat16)
    for g in range(POOL_B):
        hits[g * ROWS : (g + 1) * ROWS] = hits_of(wide, g).astype(jnp.bfloat16)

    def one(i, _):
        rows = hits[pl.ds(pl.multiple_of(i * STEM_ROWS, STEM_ROWS), STEM_ROWS)]
        for n in range(D_STEM // 256):
            here = slice(n * 256, (n + 1) * 256)
            best[:, here] = strongest(rows, taps, here)
        for k in range(STEM_ROWS // ROWS):
            block = stem_norm(best[k * ROWS : (k + 1) * ROWS], vectors[0:1], vectors[1:2])
            out[i * (STEM_ROWS // ROWS) + k + 2] = block.astype(jnp.bfloat16)
        return 0

    lax.fori_loop(0, FULL // STEM_ROWS, one, 0)
    for i in range(2):
        block = out[POOL_B + i].astype(jnp.float32)
        out[i] = pltpu.roll(block, 1, 0).astype(jnp.bfloat16)
        block = out[2 + i].astype(jnp.float32)
        out[POOL_B + 2 + i] = pltpu.roll(block, ROWS - 1, 0).astype(jnp.bfloat16)


def stem(order, tokens, weight, bias, gain):
    vmem = pl.BlockSpec(memory_space=pltpu.VMEM)
    return pl.pallas_call(
        stem_kernel,
        out_shape=(
            jax.ShapeDtypeStruct((POOL_B + 4, ROWS, D_STEM), jnp.bfloat16),
            jax.ShapeDtypeStruct((POOL_A * 128, D_STEM), jnp.bfloat16),
            jax.ShapeDtypeStruct((8, D_STEM), jnp.float32),
        ),
        in_specs=[pl.BlockSpec(memory_space=pltpu.SMEM)] + [vmem] * 4,
        out_specs=(vmem, vmem, vmem),
        scratch_shapes=[
            pltpu.VMEM((FULL, 128), jnp.bfloat16),
            pltpu.VMEM((STEM_ROWS, D_STEM), jnp.float32),
        ],
        compiler_params=pltpu.CompilerParams(vmem_limit_bytes=VMEM_LIMIT),
        cost_estimate=pl.CostEstimate(flops=7_000_000_000, bytes_accessed=5_000_000, transcendentals=1_600_000),
        name="stem",
    )(order, tokens, weight, bias, gain)


def edge_kernel(order, tokens, low_row, high_row, taps, vectors, out):
    at_start = order[SHARDS] == 0
    at_end = order[SHARDS] == 7
    low = jnp.where(at_start, 0, low_row[...])
    high = jnp.where(at_end, 0, high_row[...])
    first, last = tokens[0:1], tokens[ROWS - 1 : ROWS]
    lines = [(low, low, first), (low, first, first), (last, last, high), (last, high, high)]
    wide = jnp.concatenate([jnp.concatenate(line, axis=1) for line in lines] + [jnp.zeros((12, 384), jnp.int32)], axis=0)
    wide = wide.astype(jnp.float32).astype(jnp.bfloat16)
    by_row = {g: hits_of(wide, g) for g in (0, 1, 14, 15)}
    wanted = [(14, 0), (15, 0), (0, 1), (15, 2), (0, 3), (1, 3)]
    rows = [by_row[g][line : line + 1] for g, line in wanted] + [jnp.zeros((10, 128), jnp.float32)]
    rows = jnp.concatenate(rows, axis=0).astype(jnp.bfloat16)
    normed = stem_norm(strongest(rows, taps, slice(0, D_STEM)), vectors[0:1], vectors[1:2])
    row = lax.broadcasted_iota(jnp.int32, normed.shape, 0)
    outside = ((row < 2) & at_start) | ((row > 3) & at_end)
    out[...] = jnp.where(outside, 0.0, normed)


def edges(order, tokens, low, high, taps, vectors):
    vmem = pl.BlockSpec(memory_space=pltpu.VMEM)
    return pl.pallas_call(
        edge_kernel,
        out_shape=jax.ShapeDtypeStruct((16, D_STEM), jnp.float32),
        in_specs=[pl.BlockSpec(memory_space=pltpu.SMEM)] + [vmem] * 5,
        out_specs=vmem,
        compiler_params=pltpu.CompilerParams(vmem_limit_bytes=VMEM_LIMIT),
        cost_estimate=pl.CostEstimate(flops=30_000_000, bytes_accessed=2_000_000, transcendentals=10_000),
        name="edges",
    )(order, tokens, low, high, taps, vectors)


def pack_kernel(conv, w_out, w_query, w_key, w_value, out):
    for tap in range(KW):
        out[tap * CONV_ROWS : (tap + 1) * CONV_ROWS] = conv[tap]
    out[OUT_AT:QKV_AT] = w_out[...]
    at = 0
    for piece in (w_query, w_key, w_value):
        width = piece.shape[1]
        out[QKV_AT:, at : at + width] = piece[...]
        at += width
    out[QKV_AT:, at:] = jnp.zeros((PROJ_ROWS, D - at), jnp.bfloat16)


def pack(*pieces):
    vmem = pl.BlockSpec(memory_space=pltpu.VMEM)
    return pl.pallas_call(
        pack_kernel,
        out_shape=jax.ShapeDtypeStruct((BLOCK_ROWS, D), jnp.bfloat16),
        in_specs=[vmem] * 5,
        out_specs=vmem,
        compiler_params=pltpu.CompilerParams(vmem_limit_bytes=VMEM_LIMIT),
        name="pack",
    )(*pieces)


def pieces_of(part):
    pieces = []
    at = part * CHUNK
    while at < (part + 1) * CHUNK:
        block, row = divmod(at, CONV_ROWS)
        rows = min(CONV_ROWS - row, (part + 1) * CHUNK - at)
        pieces.append((block, row, rows, at - part * CHUNK))
        at += rows
    return pieces


COLUMNS = 512
PAIRS = 4
KV_WIDTH = 384


def conv_kernel(part, count, order, rows, patch, *refs):
    blocks, refs = refs[:count], refs[count:]
    if part > 0:
        acc_in, refs = refs[0], refs[1:]
    if part == 2:
        bias, gain, angles = refs[:3]
        coarse, pair, query = refs[3:6]
        refs = refs[6:]
    else:
        out, refs = refs[0], refs[1:]
    held, lhs_a, lhs_b, lhs_c, lhs_d, w_a, w_b, w_c, w_d, w_1, sems, held_sem = refs[:12]
    if part == 2:
        most_ref, least_ref, weight, weight_sems = refs[12:]
    pieces = pieces_of(part)
    first = pieces[0][0]
    third, step = pl.program_id(0), pl.program_id(1)
    homes = [(w_a, 0), (w_1, 0), (w_d, 0), (w_a, CHUNK), (w_d, CHUNK)]

    def copies(n):
        here = pl.ds(n * COLUMNS, COLUMNS)
        return [
            pltpu.make_async_copy(
                blocks[block - first].at[pl.ds(tap * CONV_ROWS + row, size), here],
                homes[tap][0].at[n, pl.ds(homes[tap][1] + to, size)],
                sems.at[(n * KW + tap) * len(pieces) + i],
            )
            for tap in range(KW)
            for i, (block, row, size, to) in enumerate(pieces)
        ]

    def projection_copies():
        return [
            pltpu.make_async_copy(
                block.at[pl.ds(QKV_AT, PROJ_ROWS), pl.ds(0, D - 128)],
                weight.at[pl.ds(pl.multiple_of(order[(first + i) % SHARDS] * PROJ_ROWS, PROJ_ROWS), PROJ_ROWS)],
                weight_sems.at[i],
            )
            for i, block in enumerate(blocks)
        ]

    @pl.when((third == 0) & (step == 0))
    def _():
        load = pltpu.make_async_copy(rows.at[:, :, pl.ds(part * CHUNK, CHUNK)], held, held_sem)
        load.start()
        for n in range(D // COLUMNS):
            for copy in copies(n):
                copy.start()
        if part == 2:
            for copy in projection_copies():
                copy.start()
        load.wait()
        row = lax.broadcasted_iota(jnp.int32, (16, CHUNK), 0)
        edge = patch[...]
        for i, block in enumerate((0, 1, 2, POOL_B + 1, POOL_B + 2, POOL_B + 3)):
            at, which = (0, 0) if i < 3 else (ROWS - 16, 15)
            old = held[block, at : at + 16].astype(jnp.float32)
            held[block, at : at + 16] = jnp.where(row == which, edge[i : i + 1], old).astype(jnp.bfloat16)
        for m in range(POOL_B // 2):
            even, odd = [held[2 * m + 2 * k] for k in range(3)], [held[2 * m + 2 * k + 1] for k in range(3)]
            lhs_a[m, :, :CHUNK] = even[0] - even[1]
            lhs_a[m, :, CHUNK:] = odd[1] - even[2]
            lhs_b[m, :, :CHUNK] = odd[0] + even[1]
            lhs_b[m, :, CHUNK:] = even[2]
            lhs_c[m] = even[1] - odd[0]
            lhs_d[m, :, :CHUNK] = odd[0] - odd[1]
            lhs_d[m, :, CHUNK:] = even[2] - odd[2]

    @pl.when(step == 0)
    def _():
        for n in range(D // COLUMNS):

            @pl.when(third == n)
            def _():
                for copy in copies(n):
                    copy.wait()

        outer = (w_a[third, :CHUNK].astype(jnp.float32) + w_d[third, :CHUNK].astype(jnp.float32)) * 0.5
        inner = w_1[third].astype(jnp.float32) * 0.5
        w_b[:CHUNK] = (outer + inner).astype(jnp.bfloat16)
        w_c[...] = (outer - inner).astype(jnp.bfloat16)
        w_b[CHUNK:] = w_a[third, CHUNK:] + w_d[third, CHUNK:]

    def part_of(lhs):
        return lhs[pl.ds(step * PAIRS, PAIRS)].reshape(PAIRS * ROWS, -1)

    a = dot(part_of(lhs_a), w_a[third])
    b = dot(part_of(lhs_b), w_b[...])
    c = dot(part_of(lhs_c), w_c[...])
    d = dot(part_of(lhs_d), w_d[third])
    even = (a + (b + c)).reshape(PAIRS, ROWS, COLUMNS)
    odd = ((b - c) - d).reshape(PAIRS, ROWS, COLUMNS)
    if part > 0:
        even = even + acc_in[0]
        odd = odd + acc_in[1]
    if part < 2:
        out[0] = even
        out[1] = odd
        return
    most = jnp.max(jnp.maximum(even, odd), axis=0)
    least = jnp.min(jnp.minimum(even, odd), axis=0)

    @pl.when(step == 0)
    def _():
        most_ref[...] = most
        least_ref[...] = least

    last = POOL_B // 2 // PAIRS - 1
    for n in range(D // COLUMNS):

        @pl.when((step == last) & (third == n))
        def _():
            here = slice(n * COLUMNS, (n + 1) * COLUMNS)
            shift = bias[:, here]
            high = jnp.maximum(most_ref[...], most) + shift
            low = jnp.minimum(least_ref[...], least) + shift
            coarse[:, here] = jnp.maximum(gelu(high), gelu(low)).astype(jnp.bfloat16)

    @pl.when((step == last) & (third == D // COLUMNS - 1))
    def _():
        residual = coarse[...].astype(jnp.float32)
        scale = lax.rsqrt(jnp.mean(residual * residual, axis=-1, keepdims=True) + EPSILON)
        hidden = (residual * scale * gain[...]).astype(jnp.bfloat16)
        for copy in projection_copies():
            copy.wait()
        made = dot(hidden, weight[...])
        cosine, sine = angles[0], angles[1]
        for head in range(HEADS):
            one = made[:, head * HEAD_K : (head + 1) * HEAD_K]
            query[head * ROWS : (head + 1) * ROWS] = turned(one, cosine, sine).astype(jnp.bfloat16)
        at = HEADS * HEAD_K
        pair[:, :HEAD_K] = turned(made[:, at : at + HEAD_K], cosine, sine).astype(jnp.bfloat16)
        pair[:, HEAD_K:] = made[:, at + HEAD_K : at + KV_WIDTH].astype(jnp.bfloat16)


def conv_part(part, order, rows, patch, blocks, acc=None, rest=()):
    pieces = pieces_of(part)
    if part < 2:
        blocks = blocks[pieces[0][0] : pieces[-1][0] + 1]
        used = blocks
    else:
        used = blocks[pieces[0][0] :] + blocks[: pieces[0][0]]
    args = [order, rows, patch, *used]
    whole = pl.BlockSpec(memory_space=pltpu.VMEM)
    in_specs = [
        pl.BlockSpec(memory_space=pltpu.SMEM),
        pl.BlockSpec(memory_space=pl.ANY),
        pl.BlockSpec((16, CHUNK), lambda i, j, part=part: (0, part)),
    ]
    in_specs += [pl.BlockSpec(memory_space=pl.ANY)] * len(used)
    acc_shape = (2, POOL_B // 2, ROWS, D)
    acc_spec = pl.BlockSpec((2, PAIRS, ROWS, COLUMNS), lambda i, j: (0, j, 0, i))
    lhs = (POOL_B // 2, ROWS)
    thirds = D // COLUMNS
    scratch = [
        pltpu.VMEM((POOL_B + 4, ROWS, CHUNK), jnp.bfloat16),
        pltpu.VMEM((*lhs, 2 * CHUNK), jnp.bfloat16),
        pltpu.VMEM((*lhs, 2 * CHUNK), jnp.bfloat16),
        pltpu.VMEM((*lhs, CHUNK), jnp.bfloat16),
        pltpu.VMEM((*lhs, 2 * CHUNK), jnp.bfloat16),
        pltpu.VMEM((thirds, 2 * CHUNK, COLUMNS), jnp.bfloat16),
        pltpu.VMEM((2 * CHUNK, COLUMNS), jnp.bfloat16),
        pltpu.VMEM((CHUNK, COLUMNS), jnp.bfloat16),
        pltpu.VMEM((thirds, 2 * CHUNK, COLUMNS), jnp.bfloat16),
        pltpu.VMEM((thirds, CHUNK, COLUMNS), jnp.bfloat16),
        pltpu.SemaphoreType.DMA((thirds * KW * len(pieces),)),
        pltpu.SemaphoreType.DMA,
    ]
    if part > 0:
        args.append(acc)
        in_specs.append(acc_spec)
    if part == 2:
        args += rest
        in_specs += [whole] * 3
        out_shape = (
            jax.ShapeDtypeStruct((ROWS, D), jnp.bfloat16),
            jax.ShapeDtypeStruct((ROWS, KV_WIDTH), jnp.bfloat16),
            jax.ShapeDtypeStruct((HEADS * ROWS, HEAD_K), jnp.bfloat16),
        )
        out_spec = (whole, whole, whole)
        scratch += [pltpu.VMEM((ROWS, COLUMNS), jnp.float32)] * 2
        scratch += [pltpu.VMEM((D, D - 128), jnp.bfloat16), pltpu.SemaphoreType.DMA((SHARDS,))]
    else:
        out_shape = jax.ShapeDtypeStruct(acc_shape, jnp.float32)
        out_spec = acc_spec
    return pl.pallas_call(
        functools.partial(conv_kernel, part, len(used)),
        grid=(thirds, POOL_B // 2 // PAIRS),
        out_shape=out_shape,
        in_specs=in_specs,
        out_specs=out_spec,
        scratch_shapes=scratch,
        compiler_params=pltpu.CompilerParams(vmem_limit_bytes=VMEM_LIMIT),
        cost_estimate=pl.CostEstimate(flops=8_053_063_680, bytes_accessed=20_000_000, transcendentals=0),
        name="conv",
    )(*args)


def turned(values, cosine, sine):
    return values * cosine + pltpu.roll(values, HEAD_K // 2, 1) * sine


def load_rows(order, blocks, row, column, width, target, sems):
    copies = [
        pltpu.make_async_copy(
            block.at[pl.ds(row, PROJ_ROWS), pl.ds(column, width)],
            target.at[pl.ds(pl.multiple_of(order[i] * PROJ_ROWS, PROJ_ROWS), PROJ_ROWS)],
            sems.at[i],
        )
        for i, block in enumerate(blocks)
    ]
    for copy in copies:
        copy.start()
    return copies


def attention_kernel(order, coarse, *refs):
    queries, pairs, blocks = refs[0], refs[1:5], refs[5 : 5 + SHARDS]
    out, weight, sems = refs[5 + SHARDS :]
    copies = load_rows(order, blocks, OUT_AT, 0, D, weight, sems)
    keys = jnp.concatenate([pair[:, :HEAD_K] for pair in pairs], axis=0)
    values = jnp.concatenate([pair[:, HEAD_K:] for pair in pairs], axis=0)
    mixed = []
    for head in range(HEADS):
        query = queries[head * ROWS : (head + 1) * ROWS]
        scores = lax.dot_general(query, keys, (((1,), (1,)), ((), ())), preferred_element_type=jnp.float32)
        scores = scores * HEAD_K ** (-0.5)
        raised = jnp.exp(scores - jnp.max(scores, axis=-1, keepdims=True))
        weights = raised * (1.0 / jnp.sum(raised, axis=-1, keepdims=True))
        mixed.append(dot(weights.astype(jnp.bfloat16), values).astype(jnp.bfloat16)[:, :HEAD_V])
    for copy in copies:
        copy.wait()
    total = coarse[...].astype(jnp.float32)
    for head in range(HEADS):
        total = total + dot(mixed[head], weight[head * HEAD_V : (head + 1) * HEAD_V])
    out[...] = total.astype(jnp.bfloat16)


def attention(order, coarse, query, pairs, blocks):
    vmem = pl.BlockSpec(memory_space=pltpu.VMEM)
    return pl.pallas_call(
        attention_kernel,
        out_shape=jax.ShapeDtypeStruct((ROWS, D), jnp.bfloat16),
        in_specs=[pl.BlockSpec(memory_space=pltpu.SMEM)] + [vmem] * 6 + [pl.BlockSpec(memory_space=pl.ANY)] * SHARDS,
        out_specs=vmem,
        scratch_shapes=[pltpu.VMEM((D, D), jnp.bfloat16), pltpu.SemaphoreType.DMA((SHARDS,))],
        compiler_params=pltpu.CompilerParams(vmem_limit_bytes=VMEM_LIMIT),
        cost_estimate=pl.CostEstimate(flops=3_000_000_000, bytes_accessed=6_000_000, transcendentals=1_000_000),
        name="attention",
    )(order, coarse, query, *pairs, *blocks)


def move(value, pairs):
    return lax.ppermute(value, AXES, pairs)


def body(
    tokens,
    stem_weight,
    stem_bias,
    conv_gain,
    conv_weight,
    conv_bias,
    attn_gain,
    w_query,
    w_key,
    w_value,
    w_out,
):
    seq = lax.axis_index("seq")
    line = tokens.reshape(ROWS, 128)
    own = pack(conv_weight, w_out, w_query, w_key, w_value)
    own_o = move(own, FROM_CORE)
    y = move(own, FROM_Y)
    za = move(own, FROM_Z)
    low = lax.ppermute(line[-1:], "seq", [(i, (i + 1) % 8) for i in range(8)])
    high = lax.ppermute(line[:1], "seq", [(i, (i - 1) % 8) for i in range(8)])
    order = jnp.asarray(PLACES)[lax.axis_index("dp"), seq]
    normed, taps, vectors = stem(order, line, stem_weight, stem_bias[None], conv_gain[None])
    y, za, own_o, low, high, normed = lax.optimization_barrier((y, za, own_o, low, high, normed))

    y_o, za_o = move(y, FROM_CORE), move(za, FROM_CORE)
    zb = move(za, FROM_X)
    yza = move(za, FROM_Y)
    zz = move(za, FROM_Z)
    patch = edges(order, line, low, high, taps, vectors)
    blocks = [own, own_o, y, za, y_o, za_o]
    total = conv_part(0, order, normed, patch, blocks)
    zb, yza, zz, total = lax.optimization_barrier((zb, yza, zz, total))
    yzb = move(yza, FROM_X)
    yzz = move(zz, FROM_Y)
    blocks += [zb, zz, yza] + [move(b, FROM_CORE) for b in (zb, zz, yza)]
    total = conv_part(1, order, normed, patch, blocks, total)
    yzb, yzz, total = lax.optimization_barrier((yzb, yzz, total))
    blocks += [yzb, yzz, move(yzb, FROM_CORE), move(yzz, FROM_CORE)]
    angles = jnp.asarray(ANGLES)[seq]
    rest = (conv_bias[None], attn_gain[None], angles)
    coarse, pair, query = conv_part(2, order, normed, patch, blocks, total, rest)

    near = lax.ppermute(pair, "seq", [(i, i ^ 1) for i in range(8)])
    both = jnp.concatenate([pair, near], axis=0)
    pairs = [both] + [
        lax.ppermute(both, "seq", [(i, (i + shift) % 8) for i in range(8)]) for shift in (2, 6, 4)
    ]
    return attention(order, coarse, query, pairs, blocks)[None]


def solution(mesh):
    in_specs = (
        P("dp", "seq"),
        P(),
        P(),
        P(),
        P(None, "dp", None),
        P(),
        P(),
        P("dp", None),
        P("dp", None),
        P("dp", None),
        P("dp", None),
    )
    out_specs = P("dp", "seq", None)
    return jax.shard_map(body, mesh=mesh, in_specs=in_specs, out_specs=out_specs, check_vma=False)
```

time: 164 us -> 130 us (0.79)
  starting transfers between devices: 43.4 us -> 25.2 us
  other arithmetic: 7.61 us -> 0 us
  Pallas kernels: 80.9 us -> 76.8 us
  waiting for transfers between devices: 18 us -> 14.8 us
    ppermute x15, waiting for transfers between devices: 12.9 us -> 2 us  [move(): return lax.ppermute(value, AXES, pairs)]
    ppermute x15, starting transfers between devices: 25.2 us -> 14.6 us  [move(): return lax.ppermute(value, AXES, pairs)]
    ppermute x9 -> x6, waiting for transfers between devices: 5.13 us -> 12.8 us  [the longest x3 8.42 us: body(): lax.ppermute(both, 'seq', [(i, (i + shift) % 8) for i in range(8)])]
    ppermute x9 -> x6, starting transfers between devices: 18.2 us -> 10.6 us  [the longest x1 5.01 us: body(): high = lax.ppermute(line[:1], 'seq', [(i, (i - 1) % 8) for i in range(8)])]
    concatenate x4 -> x0, other arithmetic: 4.85 us -> none  [the longest x1 2.39 us: body(): jnp.concatenate([conv_weight.reshape(OUT_AT, D), w_out, projections], axi...]
    pallas_call x6, Pallas kernels: 73.8 us -> 69.8 us  [the longest x3 51 us: conv_part(): pl.pallas_call(functools.partial(conv_kernel, part, len(used)), grid=(thi...]
    squeeze x0 -> x2, local copies, waits for them, and re-layouts: none -> 2.8 us  [the longest x1 1.57 us: body(): angles = jnp.asarray(ANGLES)[seq]]
    unnamed x37 -> x35, local copies, waits for them, and re-layouts: 6.32 us -> 5.87 us
  transfers between devices with their start and end apart: 24 -> 21, of which waited for: 3 -> 3; matrix products, arithmetic and copies ran while one was open for 9% -> 5% of each run, Pallas kernels for 33% -> 38%
where the time goes in v2:
time: 130 us; the launch traced here: 129 us
  Pallas kernels  76.8 us (59%)
  starting transfers between devices  25.2 us (19%)
  waiting for transfers between devices  14.8 us (11%)
  local copies, waits for them, and re-layouts  11.7 us (9%)
    pallas_call x3, Pallas kernels, conv_part(): pl.pallas_call(functools.partial(conv_kernel, part, len(used)), grid=(thi...  51 us
    ppermute x15, starting transfers between devices, move(): return lax.ppermute(value, AXES, pairs)  14.6 us
    pallas_call x1, Pallas kernels, stem(): pl.pallas_call(stem_kernel, out_shape=(jax.ShapeDtypeStruct((POOL_B + 4,...  13.6 us
    ppermute x3, waiting for transfers between devices, body(): lax.ppermute(both, 'seq', [(i, (i + shift) % 8) for i in range(8)])  8.42 us
    pallas_call x1, Pallas kernels, attention(): pl.pallas_call(attention_kernel, out_shape=jax.ShapeDtypeStruct((ROWS, D)...  7.09 us
    unnamed x35, local copies, waits for them, and re-layouts  5.87 us
    ppermute x1, starting transfers between devices, body(): high = lax.ppermute(line[:1], 'seq', [(i, (i - 1) % 8) for i in range(8)])  5.01 us
    ppermute x1, waiting for transfers between devices, body(): near = lax.ppermute(pair, 'seq', [(i, i ^ 1) for i in range(8)])  4.4 us
  transfers between devices with their start and end apart: 21, of which 3 were waited for; matrix products, arithmetic and copies ran while one was open for 5% of the time, Pallas kernels for 38%

profile of v2, /device:TPU:0, one launch (start us, length us, event | category | flops | bytes accessed | tf_op | source)
XLA Modules:
  0.0 129.1 jit_solution(1389280292937272201)
XLA Ops:
  0.0 2.5 %pack.1.refs_0_.refs_6_.refs_5_ = bf16[432,1536]{1,0:T(8,128)(2,1)} custom-call(bf16[5,48,1536]{2,1,0:T(8,128)(2,1)} %conv.4, bf16[96,1536]{1,0:T(8,128)(2,1)} %w_out.1, bf16[96,1024]{1,0:T(8,128)(2,1)} %w_query.1, bf16[96,128]{1,0:T(8,128)(2,1)} %w_key.1, bf16[96,192]{1,0:T(8,128)(2,1)} %w_value.1), custom_call_target="tpu_custom_call" | custom-call | tf_op jit(solution)/shard_map/pack/pallas_call | solution.py:253
  2.5 3.1 %collective-permute-start = (bf16[432,1536]{1,0:T(8,128)(2,1)}, bf16[432,1536]{1,0:T(8,128)(2,1)}, u32[]{:S(2)}, u32[]{:S(2)}) collective-permute-start(bf16[432,1536]{1,0:T(8,128)(2,1)} %pack.1.refs_0_.refs_6_.refs_5_), channel_id=1, source_target_pairs={{0,65},{1,64},{2,67},{3,66},{4,69},{5,68},{6,71},{7,70},{8,72},{9,... | collective-permute-start | bytes 3981320 | tf_op jit(solution)/shard_map/ppermute | solution.py:531
  5.6 4.0 %collective-permute-start.1 = (bf16[432,1536]{1,0:T(8,128)(2,1)}, bf16[432,1536]{1,0:T(8,128)(2,1)}, u32[]{:S(2)}, u32[]{:S(2)}) collective-permute-start(bf16[432,1536]{1,0:T(8,128)(2,1)} %pack.1.refs_0_.refs_6_.refs_5_), channel_id=1, source_target_pairs={{0,48},{1,49},{2,18},{3,19},{4,52},{5,53},{6,22},{7,23},{8,24},{9,... | collective-permute-start | bytes 3981320 | tf_op jit(solution)/shard_map/ppermute | solution.py:531
  9.6 0.7 fusion
  10.3 0.6 collective-permute-start.3
  10.9 5.0 %collective-permute-start.4 = (s32[1,128]{1,0:T(1,128)S(1)}, s32[1,128]{1,0:T(1,128)S(1)}, u32[]{:S(2)}, u32[]{:S(2)}) collective-permute-start(s32[1,128]{1,0:T(1,128)S(1)} %get-tuple-element.43), channel_id=1, source_target_pairs={{0,7},{1,0},{2,1},{3,2},{4,3},{5,4},{6,5},{7,6},{8,15},{9,8},{10,9... | collective-permute-start | bytes 1544 | tf_op jit(solution)/shard_map/ppermute | solution.py:554
  16.5 0.6 broadcast_in_dim.16.gain
  17.1 1.2 dynamic-slice_bitcast_fusion.1.order
  18.3 13.6 %stem.1 = (bf16[20,128,768]{2,1,0:T(8,128)(2,1)}, bf16[1024,768]{1,0:T(8,128)(2,1)}, f32[8,768]{1,0:T(8,128)}) custom-call(s32[17]{0:T(128)} %dynamic-slice_bitcast_fusion.1.order, s32[128,128]{1,0:T(8,128)} %bitcast.6, bf16[60,768]{1,0:T(8,128)(2,1)} %weight.1, f32[1,768]{1,0:T(1,128)} %broadcast_in_dim.15.bias, f32[1,768]{1,0:T(1,128)} %broadcast_in_dim.16.gain), custom_call_target="tpu_custom_call" | custom-call | flops 7000000000 | bytes 5000000 | tf_op jit(solution)/shard_map/stem/pallas_call | solution.py:188
  32.1 1.0 copy-done.4
  33.2 1.4 %collective-permute-start.7 = (bf16[432,1536]{1,0:T(8,128)(2,1)}, bf16[432,1536]{1,0:T(8,128)(2,1)}, u32[]{:S(2)}, u32[]{:S(2)}) collective-permute-start(bf16[432,1536]{1,0:T(8,128)(2,1)} %collective-permute-done.1.refs_3_.refs_9_.refs_8_), channel_id=1, source_target_pairs={{0,48},{1,49},{2,18},{3,19},{4,52},{5,53},{6,22},{7,23},{8,24},{9,... | collective-permute-start | bytes 3981320 | tf_op jit(solution)/shard_map/ppermute | solution.py:531
  34.6 2.7 %edges.1.patch = f32[16,768]{1,0:T(8,128)} custom-call(s32[17]{0:T(128)} %dynamic-slice_bitcast_fusion.1.order, s32[128,128]{1,0:T(8,128)} %bitcast.7, s32[1,128]{1,0:T(1,128)} %copy-done.15, s32[1,128]{1,0:T(1,128)} %copy-done.16, bf16[1024,768]{1,0:T(8,128)(2,1)} %get-tuple-element.28.taps, f32[8,768]{1,0:T(8,128)} %get-tuple-element.29.vectors), custom_call_target="tpu_custom_call" | custom-call | flops 30000000 | bytes 2000000 | tf_op jit(solution)/shard_map/edges/pallas_call | solution.py:228
  37.4 1.0 copy-done
  38.4 14.3 %conv.5.refs_6_ = f32[2,8,128,1536]{3,2,1,0:T(8,128)} custom-call(s32[17]{0:T(128)} %dynamic-slice_bitcast_fusion.1.order, bf16[20,128,768]{2,1,0:T(8,128)(2,1)} %get-tuple-element.25.rows, f32[16,768]{1,0:T(8,128)} %edges.1.patch, bf16[432,1536]{1,0:T(8,128)(2,1)} %pack.1.refs_0_.refs_6_.refs_5_, bf16[432,1536]{1,0:T(8,128)(2,1)} %copy-done.4, ...), custom_call_target="tpu_custom_call" | custom-call | flops 8053063680 | bytes 20000000 | tf_op jit(solution)/shard_map/conv/pallas_call | solution.py:463
  53.3 1.9 %collective-permute-start.12 = (bf16[432,1536]{1,0:T(8,128)(2,1)S(1)}, bf16[432,1536]{1,0:T(8,128)(2,1)}, u32[]{:S(2)}, u32[]{:S(2)}) collective-permute-start(bf16[432,1536]{1,0:T(8,128)(2,1)S(1)} %collective-permute-done.6.refs_3_.refs_14_.refs_13_), channel_id=1, source_target_pairs={{0,6},{1,7},{2,0},{3,1},{4,2},{5,3},{6,4},{7,5},{8,10},{9,11},{10,... | collective-permute-start | bytes 3981320 | tf_op jit(solution)/shard_map/ppermute | solution.py:531
  55.2 2.7 %collective-permute-start.13 = (bf16[432,1536]{1,0:T(8,128)(2,1)}, bf16[432,1536]{1,0:T(8,128)(2,1)}, u32[]{:S(2)}, u32[]{:S(2)}) collective-permute-start(bf16[432,1536]{1,0:T(8,128)(2,1)} %collective-permute-done.7.refs_2_.refs_13_.refs_12_), channel_id=1, source_target_pairs={{0,65},{1,64},{2,67},{3,66},{4,69},{5,68},{6,71},{7,70},{8,72},{9,... | collective-permute-start | bytes 3981320 | tf_op jit(solution)/shard_map/ppermute | solution.py:531
  57.9 1.0 copy-done.3
  59.0 18.1 %conv.6.refs_16_ = f32[2,8,128,1536]{3,2,1,0:T(8,128)} custom-call(s32[17]{0:T(128)} %dynamic-slice_bitcast_fusion.1.order, bf16[20,128,768]{2,1,0:T(8,128)(2,1)} %get-tuple-element.25.rows, f32[16,768]{1,0:T(8,128)} %edges.1.patch, bf16[432,1536]{1,0:T(8,128)(2,1)} %copy-done, bf16[432,1536]{1,0:T(8,128)(2,1)} %copy-done.1, ...), custom_call_target="tpu_custom_call" | custom-call | flops 8053063680 | bytes 20000000 | tf_op jit(solution)/shard_map/conv/pallas_call | solution.py:463
  77.8 0.6 broadcast_in_dim.17.refs_17_
  78.4 0.6 broadcast_in_dim.18.refs_18_
  79.0 1.6 %dynamic-slice_bitcast_fusion.refs_19_ = f32[2,128,128]{2,1,0:T(8,128)} fusion(f32[8,2,128,128]{3,2,1,0:T(8,128)} %constant.20.clone, s32[]{:T(128)S(6)} %select_n.8), kind=kLoop, calls=%fused_computation | loop fusion | bytes 262148 | tf_op jit(solution)/shard_map/squeeze | solution.py:573
  80.6 1.9 %collective-permute-done.16.refs_5_.refs_20_ = bf16[432,1536]{1,0:T(8,128)(2,1)S(1)} collective-permute-done((bf16[432,1536]{1,0:T(8,128)(2,1)}, bf16[432,1536]{1,0:T(8,128)(2,1)S(1)}, u32[]{:S(2)}, u32[]{:S(2)}) %collective-permute-start.16) | collective-permute-done | bytes 1327136 | tf_op jit(solution)/shard_map/ppermute | solution.py:531
  82.5 1.1 copy-done.6
  83.6 18.6 %conv.7 = (bf16[128,1536]{1,0:T(8,128)(2,1)}, bf16[128,384]{1,0:T(8,128)(2,1)}, bf16[1024,128]{1,0:T(8,128)(2,1)}) custom-call(s32[17]{0:T(128)} %dynamic-slice_bitcast_fusion.1.order, bf16[20,128,768]{2,1,0:T(8,128)(2,1)} %get-tuple-element.25.rows, f32[16,768]{1,0:T(8,128)} %edges.1.patch, bf16[432,1536]{1,0:T(8,128)(2,1)} %copy-done.3, ...), custom_call_target="tpu_custom_call" | custom-call | flops 8053063680 | bytes 20000000 | tf_op jit(solution)/shard_map/conv/pallas_call | solution.py:463
  102.2 1.5 %collective-permute-start.17 = (bf16[128,384]{1,0:T(8,128)(2,1)}, bf16[128,384]{1,0:T(8,128)(2,1)S(1)}, u32[]{:S(2)}, u32[]{:S(2)}) collective-permute-start(bf16[128,384]{1,0:T(8,128)(2,1)} %get-tuple-element.42), channel_id=1, source_target_pairs={{0,1},{1,0},{2,3},{3,2},{4,5},{5,4},{6,7},{7,6},{8,9},{9,8},{10,11... | collective-permute-start | bytes 294920 | tf_op jit(solution)/shard_map/ppermute | solution.py:577
  103.7 0.9 constant_dynamic-update-slice_fusion.1
  104.7 4.4 %collective-permute-done.17 = bf16[128,384]{1,0:T(8,128)(2,1)S(1)} collective-permute-done((bf16[128,384]{1,0:T(8,128)(2,1)}, bf16[128,384]{1,0:T(8,128)(2,1)S(1)}, u32[]{:S(2)}, u32[]{:S(2)}) %collective-permute-start.17) | collective-permute-done | bytes 98336 | tf_op jit(solution)/shard_map/ppermute | solution.py:577
  109.1 1.3 %collective-permute-start.18 = (bf16[256,384]{1,0:T(8,128)(2,1)S(1)}, bf16[256,384]{1,0:T(8,128)(2,1)S(1)}, u32[]{:S(2)}, u32[]{:S(2)}) collective-permute-start(bf16[256,384]{1,0:T(8,128)(2,1)S(1)} %constant_dynamic-update-slice_fusion.refs_1_), channel_id=1, source_target_pairs={{0,2},{1,3},{2,4},{3,5},{4,6},{5,7},{6,0},{7,1},{8,10},{9,11},{10,... | collective-permute-start | bytes 589832 | tf_op jit(solution)/shard_map/ppermute | solution.py:580
  110.4 2.0 %collective-permute-start.19 = (bf16[256,384]{1,0:T(8,128)(2,1)S(1)}, bf16[256,384]{1,0:T(8,128)(2,1)S(1)}, u32[]{:S(2)}, u32[]{:S(2)}) collective-permute-start(bf16[256,384]{1,0:T(8,128)(2,1)S(1)} %constant_dynamic-update-slice_fusion.refs_1_), channel_id=1, source_target_pairs={{0,6},{1,7},{2,0},{3,1},{4,2},{5,3},{6,4},{7,5},{8,14},{9,15},{10,... | collective-permute-start | bytes 589832 | tf_op jit(solution)/shard_map/ppermute | solution.py:580
  112.6 8.4 %collective-permute-done.18.refs_2_ = bf16[256,384]{1,0:T(8,128)(2,1)S(1)} collective-permute-done((bf16[256,384]{1,0:T(8,128)(2,1)S(1)}, bf16[256,384]{1,0:T(8,128)(2,1)S(1)}, u32[]{:S(2)}, u32[]{:S(2)}) %collective-permute-start.18) | collective-permute-done | bytes 196640 | tf_op jit(solution)/shard_map/ppermute | solution.py:580
  121.0 0.6 copy-done.8
  121.8 7.1 %attention.1 = bf16[128,1536]{1,0:T(8,128)(2,1)} custom-call(s32[17]{0:T(128)} %dynamic-slice_bitcast_fusion.1.order, bf16[128,1536]{1,0:T(8,128)(2,1)} %get-tuple-element.40.coarse, bf16[1024,128]{1,0:T(8,128)(2,1)} %get-tuple-element.41.refs_0_, bf16[256,384]{1,0:T(8,128)(2,1)} %copy-done.7, bf16[256,384]{1,0:T(8,128)(2,1)} %copy-done.8, ...), custom_call_target="tpu_custom_call" | custom-call | flops 3000000000 | bytes 6000000 | tf_op jit(solution)/shard_map/attention/pallas_call | solution.py:518
  (60 shorter events, 2.6 us)
Async XLA Ops:
  0.0 15.9 %copy-start.13 = (f32[768]{0:T(1024)S(1)}, f32[768]{0:T(1024)}, u32[]{:S(2)}) copy-start(f32[768]{0:T(1024)} %param.15) | copy-start | bytes 9220
  0.0 16.5 %copy-start.14 = (f32[768]{0:T(1024)S(1)}, f32[768]{0:T(1024)}, u32[]{:S(2)}) copy-start(f32[768]{0:T(1024)} %param.16) | copy-start | bytes 9220
  2.5 29.5 %collective-permute-start = (bf16[432,1536]{1,0:T(8,128)(2,1)}, bf16[432,1536]{1,0:T(8,128)(2,1)}, u32[]{:S(2)}, u32[]{:S(2)}) collective-permute-start(bf16[432,1536]{1,0:T(8,128)(2,1)} %pack.1.refs_0_.refs_6_.refs_5_), channel_id=1, source_target_pairs={{0,65},{1,64},{2,67},{3,66},{4,69},{5,68},{6,71},{7,70},{8,72},{9,... | collective-permute-start | bytes 3981320 | tf_op jit(solution)/shard_map/ppermute | solution.py:531
  5.6 26.4 %collective-permute-start.1 = (bf16[432,1536]{1,0:T(8,128)(2,1)}, bf16[432,1536]{1,0:T(8,128)(2,1)}, u32[]{:S(2)}, u32[]{:S(2)}) collective-permute-start(bf16[432,1536]{1,0:T(8,128)(2,1)} %pack.1.refs_0_.refs_6_.refs_5_), channel_id=1, source_target_pairs={{0,48},{1,49},{2,18},{3,19},{4,52},{5,53},{6,22},{7,23},{8,24},{9,... | collective-permute-start | bytes 3981320 | tf_op jit(solution)/shard_map/ppermute | solution.py:531
  9.6 22.4 %collective-permute-start.2 = (bf16[432,1536]{1,0:T(8,128)(2,1)}, bf16[432,1536]{1,0:T(8,128)(2,1)S(1)}, u32[]{:S(2)}, u32[]{:S(2)}) collective-permute-start(bf16[432,1536]{1,0:T(8,128)(2,1)} %pack.1.refs_0_.refs_6_.refs_5_), channel_id=1, source_target_pairs={{0,8},{1,9},{2,10},{3,11},{4,12},{5,13},{6,14},{7,15},{8,0},{9,1},... | collective-permute-start | bytes 3981320 | tf_op jit(solution)/shard_map/ppermute | solution.py:531
  10.3 21.6 %collective-permute-start.3 = (s32[1,128]{1,0:T(1,128)S(1)}, s32[1,128]{1,0:T(1,128)S(1)}, u32[]{:S(2)}, u32[]{:S(2)}) collective-permute-start(s32[1,128]{1,0:T(1,128)S(1)} %get-tuple-element.44), channel_id=1, source_target_pairs={{0,1},{1,2},{2,3},{3,4},{4,5},{5,6},{6,7},{7,0},{8,9},{9,10},{10,1... | collective-permute-start | bytes 1544 | tf_op jit(solution)/shard_map/ppermute | solution.py:553
  10.9 21.0 %collective-permute-start.4 = (s32[1,128]{1,0:T(1,128)S(1)}, s32[1,128]{1,0:T(1,128)S(1)}, u32[]{:S(2)}, u32[]{:S(2)}) collective-permute-start(s32[1,128]{1,0:T(1,128)S(1)} %get-tuple-element.43), channel_id=1, source_target_pairs={{0,7},{1,0},{2,1},{3,2},{4,3},{5,4},{6,5},{7,6},{8,15},{9,8},{10,9... | collective-permute-start | bytes 1544 | tf_op jit(solution)/shard_map/ppermute | solution.py:554
  31.9 2.7 %copy-start.15 = (s32[1,128]{1,0:T(1,128)}, s32[1,128]{1,0:T(1,128)S(1)}, u32[]{:S(2)}) copy-start(s32[1,128]{1,0:T(1,128)S(1)} %collective-permute-done.3.low_row) | copy-start | bytes 1540
  31.9 2.7 %copy-start.16 = (s32[1,128]{1,0:T(1,128)}, s32[1,128]{1,0:T(1,128)S(1)}, u32[]{:S(2)}) copy-start(s32[1,128]{1,0:T(1,128)S(1)} %collective-permute-done.4.high_row) | copy-start | bytes 1540
  32.0 5.3 %collective-permute-start.9 = (bf16[432,1536]{1,0:T(8,128)(2,1)}, bf16[432,1536]{1,0:T(8,128)(2,1)S(1)}, u32[]{:S(2)}, u32[]{:S(2)}) collective-permute-start(bf16[432,1536]{1,0:T(8,128)(2,1)} %collective-permute-done.1.refs_3_.refs_9_.refs_8_), channel_id=1, source_target_pairs={{0,8},{1,9},{2,10},{3,11},{4,12},{5,13},{6,14},{7,15},{8,0},{9,1},... | collective-permute-start | bytes 3981320 | tf_op jit(solution)/shard_map/ppermute | solution.py:531
  33.0 4.3 %collective-permute-start.8 = (bf16[432,1536]{1,0:T(8,128)(2,1)}, bf16[432,1536]{1,0:T(8,128)(2,1)}, u32[]{:S(2)}, u32[]{:S(2)}) collective-permute-start(bf16[432,1536]{1,0:T(8,128)(2,1)} %collective-permute-done.refs_2_.refs_8_.refs_7_), channel_id=1, source_target_pairs={{0,8},{1,9},{2,10},{3,11},{4,12},{5,13},{6,14},{7,15},{8,0},{9,1},... | collective-permute-start | bytes 3981320 | tf_op jit(solution)/shard_map/ppermute | solution.py:531
  33.0 19.7 %collective-permute-start.5 = (bf16[432,1536]{1,0:T(8,128)(2,1)}, bf16[432,1536]{1,0:T(8,128)(2,1)S(1)}, u32[]{:S(2)}, u32[]{:S(2)}) collective-permute-start(bf16[432,1536]{1,0:T(8,128)(2,1)} %collective-permute-done.1.refs_3_.refs_9_.refs_8_), channel_id=1, source_target_pairs={{0,6},{1,7},{2,0},{3,1},{4,2},{5,3},{6,4},{7,5},{8,10},{9,11},{10,... | collective-permute-start | bytes 3981320 | tf_op jit(solution)/shard_map/ppermute | solution.py:531
  33.0 19.7 %collective-permute-start.6 = (bf16[432,1536]{1,0:T(8,128)(2,1)}, bf16[432,1536]{1,0:T(8,128)(2,1)S(1)}, u32[]{:S(2)}, u32[]{:S(2)}) collective-permute-start(bf16[432,1536]{1,0:T(8,128)(2,1)} %collective-permute-done.1.refs_3_.refs_9_.refs_8_), channel_id=1, source_target_pairs={{0,65},{1,64},{2,67},{3,66},{4,69},{5,68},{6,71},{7,70},{8,72},{9,... | collective-permute-start | bytes 3981320 | tf_op jit(solution)/shard_map/ppermute | solution.py:531
  33.2 19.5 %collective-permute-start.7 = (bf16[432,1536]{1,0:T(8,128)(2,1)}, bf16[432,1536]{1,0:T(8,128)(2,1)}, u32[]{:S(2)}, u32[]{:S(2)}) collective-permute-start(bf16[432,1536]{1,0:T(8,128)(2,1)} %collective-permute-done.1.refs_3_.refs_9_.refs_8_), channel_id=1, source_target_pairs={{0,48},{1,49},{2,18},{3,19},{4,52},{5,53},{6,22},{7,23},{8,24},{9,... | collective-permute-start | bytes 3981320 | tf_op jit(solution)/shard_map/ppermute | solution.py:531
  37.3 1.1 copy-start
  52.7 25.1 %copy-start.11 = (f32[1536]{0:T(1024)S(1)}, f32[1536]{0:T(1024)}, u32[]{:S(2)}) copy-start(f32[1536]{0:T(1024)} %param.18) | copy-start | bytes 18436
  52.7 25.7 %copy-start.12 = (f32[1536]{0:T(1024)S(1)}, f32[1536]{0:T(1024)}, u32[]{:S(2)}) copy-start(f32[1536]{0:T(1024)} %param.19) | copy-start | bytes 18436
  52.7 5.2 %copy-start.1 = (bf16[432,1536]{1,0:T(8,128)(2,1)}, bf16[432,1536]{1,0:T(8,128)(2,1)S(1)}, u32[]{:S(2)}) copy-start(bf16[432,1536]{1,0:T(8,128)(2,1)S(1)} %collective-permute-done.5.refs_1_.refs_12_.refs_11_) | copy-start | bytes 3981316
  52.7 5.2 %copy-start.2 = (bf16[432,1536]{1,0:T(8,128)(2,1)}, bf16[432,1536]{1,0:T(8,128)(2,1)S(1)}, u32[]{:S(2)}) copy-start(bf16[432,1536]{1,0:T(8,128)(2,1)S(1)} %collective-permute-done.6.refs_3_.refs_14_.refs_13_) | copy-start | bytes 3981316
  52.7 5.2 %collective-permute-start.10 = (bf16[432,1536]{1,0:T(8,128)(2,1)}, bf16[432,1536]{1,0:T(8,128)(2,1)S(1)}, u32[]{:S(2)}, u32[]{:S(2)}) collective-permute-start(bf16[432,1536]{1,0:T(8,128)(2,1)} %collective-permute-done.7.refs_2_.refs_13_.refs_12_), channel_id=1, source_target_pairs={{0,8},{1,9},{2,10},{3,11},{4,12},{5,13},{6,14},{7,15},{8,0},{9,1},... | collective-permute-start | bytes 3981320 | tf_op jit(solution)/shard_map/ppermute | solution.py:531
  52.8 5.1 %collective-permute-start.14 = (bf16[432,1536]{1,0:T(8,128)(2,1)S(1)}, bf16[432,1536]{1,0:T(8,128)(2,1)}, u32[]{:S(2)}, u32[]{:S(2)}) collective-permute-start(bf16[432,1536]{1,0:T(8,128)(2,1)S(1)} %collective-permute-done.5.refs_1_.refs_12_.refs_11_), channel_id=1, source_target_pairs={{0,8},{1,9},{2,10},{3,11},{4,12},{5,13},{6,14},{7,15},{8,0},{9,1},... | collective-permute-start | bytes 3981320 | tf_op jit(solution)/shard_map/ppermute | solution.py:531
  53.3 23.8 %collective-permute-start.12 = (bf16[432,1536]{1,0:T(8,128)(2,1)S(1)}, bf16[432,1536]{1,0:T(8,128)(2,1)}, u32[]{:S(2)}, u32[]{:S(2)}) collective-permute-start(bf16[432,1536]{1,0:T(8,128)(2,1)S(1)} %collective-permute-done.6.refs_3_.refs_14_.refs_13_), channel_id=1, source_target_pairs={{0,6},{1,7},{2,0},{3,1},{4,2},{5,3},{6,4},{7,5},{8,10},{9,11},{10,... | collective-permute-start | bytes 3981320 | tf_op jit(solution)/shard_map/ppermute | solution.py:531
  55.2 21.9 %collective-permute-start.13 = (bf16[432,1536]{1,0:T(8,128)(2,1)}, bf16[432,1536]{1,0:T(8,128)(2,1)}, u32[]{:S(2)}, u32[]{:S(2)}) collective-permute-start(bf16[432,1536]{1,0:T(8,128)(2,1)} %collective-permute-done.7.refs_2_.refs_13_.refs_12_), channel_id=1, source_target_pairs={{0,65},{1,64},{2,67},{3,66},{4,69},{5,68},{6,71},{7,70},{8,72},{9,... | collective-permute-start | bytes 3981320 | tf_op jit(solution)/shard_map/ppermute | solution.py:531
  57.9 22.7 %collective-permute-start.11 = (bf16[432,1536]{1,0:T(8,128)(2,1)S(1)}, bf16[432,1536]{1,0:T(8,128)(2,1)}, u32[]{:S(2)}, u32[]{:S(2)}) collective-permute-start(bf16[432,1536]{1,0:T(8,128)(2,1)S(1)} %collective-permute-done.6.refs_3_.refs_14_.refs_13_), channel_id=1, source_target_pairs={{0,8},{1,9},{2,10},{3,11},{4,12},{5,13},{6,14},{7,15},{8,0},{9,1},... | collective-permute-start | bytes 3981320 | tf_op jit(solution)/shard_map/ppermute | solution.py:531
  77.1 3.5 %collective-permute-start.15 = (bf16[432,1536]{1,0:T(8,128)(2,1)}, bf16[432,1536]{1,0:T(8,128)(2,1)S(1)}, u32[]{:S(2)}, u32[]{:S(2)}) collective-permute-start(bf16[432,1536]{1,0:T(8,128)(2,1)} %collective-permute-done.12.refs_2_.refs_17_), channel_id=1, source_target_pairs={{0,8},{1,9},{2,10},{3,11},{4,12},{5,13},{6,14},{7,15},{8,0},{9,1},... | collective-permute-start | bytes 3981320 | tf_op jit(solution)/shard_map/ppermute | solution.py:531
  77.7 4.8 %collective-permute-start.16 = (bf16[432,1536]{1,0:T(8,128)(2,1)}, bf16[432,1536]{1,0:T(8,128)(2,1)S(1)}, u32[]{:S(2)}, u32[]{:S(2)}) collective-permute-start(bf16[432,1536]{1,0:T(8,128)(2,1)} %collective-permute-done.13.refs_3_.refs_18_), channel_id=1, source_target_pairs={{0,8},{1,9},{2,10},{3,11},{4,12},{5,13},{6,14},{7,15},{8,0},{9,1},... | collective-permute-start | bytes 3981320 | tf_op jit(solution)/shard_map/ppermute | solution.py:531
  80.6 1.9 %copy-start.5 = (bf16[432,1536]{1,0:T(8,128)(2,1)}, bf16[432,1536]{1,0:T(8,128)(2,1)S(1)}, u32[]{:S(2)}) copy-start(bf16[432,1536]{1,0:T(8,128)(2,1)S(1)} %collective-permute-done.15.refs_4_.refs_19_) | copy-start | bytes 3981316
  102.2 6.9 %collective-permute-start.17 = (bf16[128,384]{1,0:T(8,128)(2,1)}, bf16[128,384]{1,0:T(8,128)(2,1)S(1)}, u32[]{:S(2)}, u32[]{:S(2)}) collective-permute-start(bf16[128,384]{1,0:T(8,128)(2,1)} %get-tuple-element.42), channel_id=1, source_target_pairs={{0,1},{1,0},{2,3},{3,2},{4,5},{5,4},{6,7},{7,6},{8,9},{9,8},{10,11... | collective-permute-start | bytes 294920 | tf_op jit(solution)/shard_map/ppermute | solution.py:577
  109.1 11.9 %copy-start.7 = (bf16[256,384]{1,0:T(8,128)(2,1)}, bf16[256,384]{1,0:T(8,128)(2,1)S(1)}, u32[]{:S(2)}) copy-start(bf16[256,384]{1,0:T(8,128)(2,1)S(1)} %constant_dynamic-update-slice_fusion.refs_1_) | copy-start | bytes 589828
  109.1 11.9 %collective-permute-start.18 = (bf16[256,384]{1,0:T(8,128)(2,1)S(1)}, bf16[256,384]{1,0:T(8,128)(2,1)S(1)}, u32[]{:S(2)}, u32[]{:S(2)}) collective-permute-start(bf16[256,384]{1,0:T(8,128)(2,1)S(1)} %constant_dynamic-update-slice_fusion.refs_1_), channel_id=1, source_target_pairs={{0,2},{1,3},{2,4},{3,5},{4,6},{5,7},{6,0},{7,1},{8,10},{9,11},{10,... | collective-permute-start | bytes 589832 | tf_op jit(solution)/shard_map/ppermute | solution.py:580
  110.4 10.6 %collective-permute-start.19 = (bf16[256,384]{1,0:T(8,128)(2,1)S(1)}, bf16[256,384]{1,0:T(8,128)(2,1)S(1)}, u32[]{:S(2)}, u32[]{:S(2)}) collective-permute-start(bf16[256,384]{1,0:T(8,128)(2,1)S(1)} %constant_dynamic-update-slice_fusion.refs_1_), channel_id=1, source_target_pairs={{0,6},{1,7},{2,0},{3,1},{4,2},{5,3},{6,4},{7,5},{8,14},{9,15},{10,... | collective-permute-start | bytes 589832 | tf_op jit(solution)/shard_map/ppermute | solution.py:580
  112.4 8.6 %collective-permute-start.20 = (bf16[256,384]{1,0:T(8,128)(2,1)S(1)}, bf16[256,384]{1,0:T(8,128)(2,1)S(1)}, u32[]{:S(2)}, u32[]{:S(2)}) collective-permute-start(bf16[256,384]{1,0:T(8,128)(2,1)S(1)} %constant_dynamic-update-slice_fusion.refs_1_), channel_id=1, source_target_pairs={{0,4},{1,5},{2,6},{3,7},{4,0},{5,1},{6,2},{7,3},{8,12},{9,13},{10,... | collective-permute-start | bytes 589832 | tf_op jit(solution)/shard_map/ppermute | solution.py:580
  (6 other events, 5.4 us)

commit v3 on v2

--- a/solution.py
+++ b/solution.py
@@ -23,7 +23,6 @@
 OUT_AT = KW * CONV_ROWS
 QKV_AT = OUT_AT + PROJ_ROWS
 BLOCK_ROWS = QKV_AT + PROJ_ROWS
-CHUNK = 256
 ROWS = 128
 HALO = 24
 EPSILON = 1e-06
@@ -159,11 +158,15 @@
     place = (row % 128 == tap + 4 * (row // 128 + 1)).astype(jnp.float32).astype(jnp.bfloat16)
     taps[...] = dot(place, moved).astype(jnp.bfloat16)
 
+    stem_rows(0, tokens, taps, vectors, out, hits, best)
+
+
+def stem_rows(half, tokens, taps, vectors, out, hits, best):
     held = tokens[...].astype(jnp.float32)
     before, after = pltpu.roll(held, 1, 0), pltpu.roll(held, ROWS - 1, 0)
     wide = jnp.concatenate([before, held, after], axis=1).astype(jnp.bfloat16)
-    for g in range(POOL_B):
-        hits[g * ROWS : (g + 1) * ROWS] = hits_of(wide, g).astype(jnp.bfloat16)
+    for k in range(POOL_B // 2):
+        hits[k * ROWS : (k + 1) * ROWS] = hits_of(wide, half * (POOL_B // 2) + k).astype(jnp.bfloat16)
 
     def one(i, _):
         rows = hits[pl.ds(pl.multiple_of(i * STEM_ROWS, STEM_ROWS), STEM_ROWS)]
@@ -172,36 +175,51 @@
             best[:, here] = strongest(rows, taps, here)
         for k in range(STEM_ROWS // ROWS):
             block = stem_norm(best[k * ROWS : (k + 1) * ROWS], vectors[0:1], vectors[1:2])
-            out[i * (STEM_ROWS // ROWS) + k + 2] = block.astype(jnp.bfloat16)
+            out[i * (STEM_ROWS // ROWS) + k + 2 * half] = block.astype(jnp.bfloat16)
         return 0
 
-    lax.fori_loop(0, FULL // STEM_ROWS, one, 0)
+    lax.fori_loop(0, FULL // 2 // STEM_ROWS, one, 0)
     for i in range(2):
-        block = out[POOL_B + i].astype(jnp.float32)
-        out[i] = pltpu.roll(block, 1, 0).astype(jnp.bfloat16)
-        block = out[2 + i].astype(jnp.float32)
-        out[POOL_B + 2 + i] = pltpu.roll(block, ROWS - 1, 0).astype(jnp.bfloat16)
-
-
-def stem(order, tokens, weight, bias, gain):
+        source, to, by = (i, 8 + i, ROWS - 1) if half == 0 else (8 + i, i, 1)
+        out[to] = pltpu.roll(out[source].astype(jnp.float32), by, 0).astype(jnp.bfloat16)
+
+
+def stem_front(order, tokens, weight, bias, gain):
     vmem = pl.BlockSpec(memory_space=pltpu.VMEM)
     return pl.pallas_call(
         stem_kernel,
         out_shape=(
-            jax.ShapeDtypeStruct((POOL_B + 4, ROWS, D_STEM), jnp.bfloat16),
+            jax.ShapeDtypeStruct((POOL_B // 2 + 2, ROWS, D_STEM), jnp.bfloat16),
             jax.ShapeDtypeStruct((POOL_A * 128, D_STEM), jnp.bfloat16),
             jax.ShapeDtypeStruct((8, D_STEM), jnp.float32),
         ),
         in_specs=[pl.BlockSpec(memory_space=pltpu.SMEM)] + [vmem] * 4,
         out_specs=(vmem, vmem, vmem),
         scratch_shapes=[
-            pltpu.VMEM((FULL, 128), jnp.bfloat16),
+            pltpu.VMEM((FULL // 2, 128), jnp.bfloat16),
             pltpu.VMEM((STEM_ROWS, D_STEM), jnp.float32),
         ],
         compiler_params=pltpu.CompilerParams(vmem_limit_bytes=VMEM_LIMIT),
-        cost_estimate=pl.CostEstimate(flops=7_000_000_000, bytes_accessed=5_000_000, transcendentals=1_600_000),
-        name="stem",
+        cost_estimate=pl.CostEstimate(flops=4_000_000_000, bytes_accessed=5_000_000, transcendentals=800_000),
+        name="stem_front",
     )(order, tokens, weight, bias, gain)
+
+
+def stem_back(tokens, taps, vectors):
+    vmem = pl.BlockSpec(memory_space=pltpu.VMEM)
+    return pl.pallas_call(
+        functools.partial(stem_rows, 1),
+        out_shape=jax.ShapeDtypeStruct((POOL_B // 2 + 2, ROWS, D_STEM), jnp.bfloat16),
+        in_specs=[vmem] * 3,
+        out_specs=vmem,
+        scratch_shapes=[
+            pltpu.VMEM((FULL // 2, 128), jnp.bfloat16),
+            pltpu.VMEM((STEM_ROWS, D_STEM), jnp.float32),
+        ],
+        compiler_params=pltpu.CompilerParams(vmem_limit_bytes=VMEM_LIMIT),
+        cost_estimate=pl.CostEstimate(flops=3_500_000_000, bytes_accessed=4_000_000, transcendentals=800_000),
+        name="stem_back",
+    )(tokens, taps, vectors)
 
 
 def edge_kernel(order, tokens, low_row, high_row, taps, vectors, out):
@@ -260,13 +278,17 @@
     )(*pieces)
 
 
+PARTS = ((0, 512), (512, 256))
+
+
 def pieces_of(part):
+    start, size = PARTS[part]
     pieces = []
-    at = part * CHUNK
-    while at < (part + 1) * CHUNK:
+    at = start
+    while at < start + size:
         block, row = divmod(at, CONV_ROWS)
-        rows = min(CONV_ROWS - row, (part + 1) * CHUNK - at)
-        pieces.append((block, row, rows, at - part * CHUNK))
+        rows = min(CONV_ROWS - row, start + size - at)
+        pieces.append((block, row, rows, at - start))
         at += rows
     return pieces
 
@@ -276,40 +298,51 @@
 KV_WIDTH = 384
 
 
-def conv_kernel(part, count, order, rows, patch, *refs):
+def conv_kernel(part, count, order, front, back, patch, *refs):
     blocks, refs = refs[:count], refs[count:]
-    if part > 0:
-        acc_in, refs = refs[0], refs[1:]
-    if part == 2:
-        bias, gain, angles = refs[:3]
-        coarse, pair, query = refs[3:6]
-        refs = refs[6:]
+    if part == 1:
+        acc_in, bias, gain, angles = refs[:4]
+        coarse, hidden, pair = refs[4:7]
+        refs = refs[7:]
     else:
         out, refs = refs[0], refs[1:]
-    held, lhs_a, lhs_b, lhs_c, lhs_d, w_a, w_b, w_c, w_d, w_1, sems, held_sem = refs[:12]
-    if part == 2:
+    held, lhs_a, lhs_b, lhs_c, lhs_d, w_a, w_b, w_c, w_d, w_1, sems, held_sems = refs[:12]
+    if part == 1:
         most_ref, least_ref, weight, weight_sems = refs[12:]
     pieces = pieces_of(part)
     first = pieces[0][0]
+    start, size = PARTS[part]
     third, step = pl.program_id(0), pl.program_id(1)
-    homes = [(w_a, 0), (w_1, 0), (w_d, 0), (w_a, CHUNK), (w_d, CHUNK)]
-
-    def copies(n):
-        here = pl.ds(n * COLUMNS, COLUMNS)
+    columns = pl.ds(pl.multiple_of(third * COLUMNS, COLUMNS), COLUMNS)
+    homes = [(w_a, 0), (w_1, 0), (w_d, 0), (w_a, size), (w_d, size)]
+
+    def copies():
         return [
             pltpu.make_async_copy(
-                blocks[block - first].at[pl.ds(tap * CONV_ROWS + row, size), here],
-                homes[tap][0].at[n, pl.ds(homes[tap][1] + to, size)],
-                sems.at[(n * KW + tap) * len(pieces) + i],
+                blocks[block - first].at[pl.ds(tap * CONV_ROWS + row, rows)],
+                homes[tap][0].at[pl.ds(homes[tap][1] + to, rows)],
+                sems.at[tap * len(pieces) + i],
             )
             for tap in range(KW)
-            for i, (block, row, size, to) in enumerate(pieces)
+            for i, (block, row, rows, to) in enumerate(pieces)
+        ]
+
+    def row_copies():
+        return [
+            pltpu.make_async_copy(
+                source.at[pl.ds(at, rows), :, pl.ds(start, size)],
+                held.at[pl.ds(to, rows)],
+                held_sems.at[i],
+            )
+            for i, (source, at, rows, to) in enumerate(
+                ((front, 0, 8, 2), (back, 0, 2, 0), (back, 2, 8, 10), (front, 8, 2, 18))
+            )
         ]
 
     def projection_copies():
         return [
             pltpu.make_async_copy(
-                block.at[pl.ds(QKV_AT, PROJ_ROWS), pl.ds(0, D - 128)],
+                block.at[pl.ds(QKV_AT, PROJ_ROWS), pl.ds(HEADS * HEAD_K, KV_WIDTH)],
                 weight.at[pl.ds(pl.multiple_of(order[(first + i) % SHARDS] * PROJ_ROWS, PROJ_ROWS), PROJ_ROWS)],
                 weight_sems.at[i],
             )
@@ -318,16 +351,14 @@
 
     @pl.when((third == 0) & (step == 0))
     def _():
-        load = pltpu.make_async_copy(rows.at[:, :, pl.ds(part * CHUNK, CHUNK)], held, held_sem)
-        load.start()
-        for n in range(D // COLUMNS):
-            for copy in copies(n):
-                copy.start()
-        if part == 2:
+        for copy in row_copies() + copies():
+            copy.start()
+        if part == 1:
             for copy in projection_copies():
                 copy.start()
-        load.wait()
-        row = lax.broadcasted_iota(jnp.int32, (16, CHUNK), 0)
+        for copy in row_copies():
+            copy.wait()
+        row = lax.broadcasted_iota(jnp.int32, (16, size), 0)
         edge = patch[...]
         for i, block in enumerate((0, 1, 2, POOL_B + 1, POOL_B + 2, POOL_B + 3)):
             at, which = (0, 0) if i < 3 else (ROWS - 16, 15)
@@ -335,42 +366,37 @@
             held[block, at : at + 16] = jnp.where(row == which, edge[i : i + 1], old).astype(jnp.bfloat16)
         for m in range(POOL_B // 2):
             even, odd = [held[2 * m + 2 * k] for k in range(3)], [held[2 * m + 2 * k + 1] for k in range(3)]
-            lhs_a[m, :, :CHUNK] = even[0] - even[1]
-            lhs_a[m, :, CHUNK:] = odd[1] - even[2]
-            lhs_b[m, :, :CHUNK] = odd[0] + even[1]
-            lhs_b[m, :, CHUNK:] = even[2]
+            lhs_a[m, :, :size] = even[0] - even[1]
+            lhs_a[m, :, size:] = odd[1] - even[2]
+            lhs_b[m, :, :size] = odd[0] + even[1]
+            lhs_b[m, :, size:] = even[2]
             lhs_c[m] = even[1] - odd[0]
-            lhs_d[m, :, :CHUNK] = odd[0] - odd[1]
-            lhs_d[m, :, CHUNK:] = even[2] - odd[2]
+            lhs_d[m, :, :size] = odd[0] - odd[1]
+            lhs_d[m, :, size:] = even[2] - odd[2]
+        for copy in copies():
+            copy.wait()
 
     @pl.when(step == 0)
     def _():
-        for n in range(D // COLUMNS):
-
-            @pl.when(third == n)
-            def _():
-                for copy in copies(n):
-                    copy.wait()
-
-        outer = (w_a[third, :CHUNK].astype(jnp.float32) + w_d[third, :CHUNK].astype(jnp.float32)) * 0.5
-        inner = w_1[third].astype(jnp.float32) * 0.5
-        w_b[:CHUNK] = (outer + inner).astype(jnp.bfloat16)
+        outer = (w_a[:size, columns].astype(jnp.float32) + w_d[:size, columns].astype(jnp.float32)) * 0.5
+        inner = w_1[:, columns].astype(jnp.float32) * 0.5
+        w_b[:size] = (outer + inner).astype(jnp.bfloat16)
         w_c[...] = (outer - inner).astype(jnp.bfloat16)
-        w_b[CHUNK:] = w_a[third, CHUNK:] + w_d[third, CHUNK:]
+        w_b[size:] = w_a[size:, columns] + w_d[size:, columns]
 
     def part_of(lhs):
         return lhs[pl.ds(step * PAIRS, PAIRS)].reshape(PAIRS * ROWS, -1)
 
-    a = dot(part_of(lhs_a), w_a[third])
+    a = dot(part_of(lhs_a), w_a[:, columns])
     b = dot(part_of(lhs_b), w_b[...])
     c = dot(part_of(lhs_c), w_c[...])
-    d = dot(part_of(lhs_d), w_d[third])
+    d = dot(part_of(lhs_d), w_d[:, columns])
     even = (a + (b + c)).reshape(PAIRS, ROWS, COLUMNS)
     odd = ((b - c) - d).reshape(PAIRS, ROWS, COLUMNS)
-    if part > 0:
+    if part == 1:
         even = even + acc_in[0]
         odd = odd + acc_in[1]
-    if part < 2:
+    else:
         out[0] = even
         out[1] = odd
         return
@@ -397,78 +423,66 @@
     def _():
         residual = coarse[...].astype(jnp.float32)
         scale = lax.rsqrt(jnp.mean(residual * residual, axis=-1, keepdims=True) + EPSILON)
-        hidden = (residual * scale * gain[...]).astype(jnp.bfloat16)
+        hidden[...] = (residual * scale * gain[...]).astype(jnp.bfloat16)
         for copy in projection_copies():
             copy.wait()
-        made = dot(hidden, weight[...])
-        cosine, sine = angles[0], angles[1]
-        for head in range(HEADS):
-            one = made[:, head * HEAD_K : (head + 1) * HEAD_K]
-            query[head * ROWS : (head + 1) * ROWS] = turned(one, cosine, sine).astype(jnp.bfloat16)
-        at = HEADS * HEAD_K
-        pair[:, :HEAD_K] = turned(made[:, at : at + HEAD_K], cosine, sine).astype(jnp.bfloat16)
-        pair[:, HEAD_K:] = made[:, at + HEAD_K : at + KV_WIDTH].astype(jnp.bfloat16)
-
-
-def conv_part(part, order, rows, patch, blocks, acc=None, rest=()):
+        made = dot(hidden[...], weight[...])
+        pair[:, :HEAD_K] = turned(made[:, :HEAD_K], angles[0], angles[1]).astype(jnp.bfloat16)
+        pair[:, HEAD_K:] = made[:, HEAD_K:].astype(jnp.bfloat16)
+
+
+def conv_part(part, order, front, back, patch, blocks, rest=()):
     pieces = pieces_of(part)
-    if part < 2:
-        blocks = blocks[pieces[0][0] : pieces[-1][0] + 1]
-        used = blocks
-    else:
-        used = blocks[pieces[0][0] :] + blocks[: pieces[0][0]]
-    args = [order, rows, patch, *used]
+    start, size = PARTS[part]
+    used = blocks[: pieces[-1][0] + 1] if part == 0 else blocks[pieces[0][0] :] + blocks[: pieces[0][0]]
+    args = [order, front, back, patch, *used]
     whole = pl.BlockSpec(memory_space=pltpu.VMEM)
     in_specs = [
         pl.BlockSpec(memory_space=pltpu.SMEM),
         pl.BlockSpec(memory_space=pl.ANY),
-        pl.BlockSpec((16, CHUNK), lambda i, j, part=part: (0, part)),
+        pl.BlockSpec(memory_space=pl.ANY),
+        pl.BlockSpec((16, size), lambda i, j: (0, start // size)),
     ]
     in_specs += [pl.BlockSpec(memory_space=pl.ANY)] * len(used)
-    acc_shape = (2, POOL_B // 2, ROWS, D)
     acc_spec = pl.BlockSpec((2, PAIRS, ROWS, COLUMNS), lambda i, j: (0, j, 0, i))
     lhs = (POOL_B // 2, ROWS)
-    thirds = D // COLUMNS
     scratch = [
-        pltpu.VMEM((POOL_B + 4, ROWS, CHUNK), jnp.bfloat16),
-        pltpu.VMEM((*lhs, 2 * CHUNK), jnp.bfloat16),
-        pltpu.VMEM((*lhs, 2 * CHUNK), jnp.bfloat16),
-        pltpu.VMEM((*lhs, CHUNK), jnp.bfloat16),
-        pltpu.VMEM((*lhs, 2 * CHUNK), jnp.bfloat16),
-        pltpu.VMEM((thirds, 2 * CHUNK, COLUMNS), jnp.bfloat16),
-        pltpu.VMEM((2 * CHUNK, COLUMNS), jnp.bfloat16),
-        pltpu.VMEM((CHUNK, COLUMNS), jnp.bfloat16),
-        pltpu.VMEM((thirds, 2 * CHUNK, COLUMNS), jnp.bfloat16),
-        pltpu.VMEM((thirds, CHUNK, COLUMNS), jnp.bfloat16),
-        pltpu.SemaphoreType.DMA((thirds * KW * len(pieces),)),
-        pltpu.SemaphoreType.DMA,
+        pltpu.VMEM((POOL_B + 4, ROWS, size), jnp.bfloat16),
+        pltpu.VMEM((*lhs, 2 * size), jnp.bfloat16),
+        pltpu.VMEM((*lhs, 2 * size), jnp.bfloat16),
+        pltpu.VMEM((*lhs, size), jnp.bfloat16),
+        pltpu.VMEM((*lhs, 2 * size), jnp.bfloat16),
+        pltpu.VMEM((2 * size, D), jnp.bfloat16),
+        pltpu.VMEM((2 * size, COLUMNS), jnp.bfloat16),
+        pltpu.VMEM((size, COLUMNS), jnp.bfloat16),
+        pltpu.VMEM((2 * size, D), jnp.bfloat16),
+        pltpu.VMEM((size, D), jnp.bfloat16),
+        pltpu.SemaphoreType.DMA((KW * len(pieces),)),
+        pltpu.SemaphoreType.DMA((4,)),
     ]
-    if part > 0:
-        args.append(acc)
-        in_specs.append(acc_spec)
-    if part == 2:
+    if part == 1:
         args += rest
-        in_specs += [whole] * 3
+        in_specs += [acc_spec] + [whole] * 3
         out_shape = (
             jax.ShapeDtypeStruct((ROWS, D), jnp.bfloat16),
+            jax.ShapeDtypeStruct((ROWS, D), jnp.bfloat16),
             jax.ShapeDtypeStruct((ROWS, KV_WIDTH), jnp.bfloat16),
-            jax.ShapeDtypeStruct((HEADS * ROWS, HEAD_K), jnp.bfloat16),
         )
         out_spec = (whole, whole, whole)
         scratch += [pltpu.VMEM((ROWS, COLUMNS), jnp.float32)] * 2
-        scratch += [pltpu.VMEM((D, D - 128), jnp.bfloat16), pltpu.SemaphoreType.DMA((SHARDS,))]
+        scratch += [pltpu.VMEM((D, KV_WIDTH), jnp.bfloat16), pltpu.SemaphoreType.DMA((SHARDS,))]
     else:
-        out_shape = jax.ShapeDtypeStruct(acc_shape, jnp.float32)
+        out_shape = jax.ShapeDtypeStruct((2, POOL_B // 2, ROWS, D), jnp.float32)
         out_spec = acc_spec
     return pl.pallas_call(
         functools.partial(conv_kernel, part, len(used)),
-        grid=(thirds, POOL_B // 2 // PAIRS),
+        grid=(D // COLUMNS, POOL_B // 2 // PAIRS),
         out_shape=out_shape,
         in_specs=in_specs,
         out_specs=out_spec,
         scratch_shapes=scratch,
         compiler_params=pltpu.CompilerParams(vmem_limit_bytes=VMEM_LIMIT),
-        cost_estimate=pl.CostEstimate(flops=8_053_063_680, bytes_accessed=20_000_000, transcendentals=0),
+        cost_estimate=pl.CostEstimate(flops=size * 22_020_096, bytes_accessed=20_000_000, transcendentals=0),
         name="conv",
     )(*args)
 
@@ -489,6 +503,31 @@
     for copy in copies:
         copy.start()
     return copies
+
+
+def query_kernel(order, hidden, angles, *refs):
+    blocks = refs[:SHARDS]
+    out, weight, sems = refs[SHARDS:]
+    for copy in load_rows(order, blocks, QKV_AT, 0, HEADS * HEAD_K, weight, sems):
+        copy.wait()
+    query = dot(hidden[...], weight[...])
+    for head in range(HEADS):
+        one = query[:, head * HEAD_K : (head + 1) * HEAD_K]
+        out[head * ROWS : (head + 1) * ROWS] = turned(one, angles[0], angles[1]).astype(jnp.bfloat16)
+
+
+def query_of(order, hidden, angles, blocks):
+    vmem = pl.BlockSpec(memory_space=pltpu.VMEM)
+    return pl.pallas_call(
+        query_kernel,
+        out_shape=jax.ShapeDtypeStruct((HEADS * ROWS, HEAD_K), jnp.bfloat16),
+        in_specs=[pl.BlockSpec(memory_space=pltpu.SMEM)] + [vmem] * 2 + [pl.BlockSpec(memory_space=pl.ANY)] * SHARDS,
+        out_specs=vmem,
+        scratch_shapes=[pltpu.VMEM((D, HEADS * HEAD_K), jnp.bfloat16), pltpu.SemaphoreType.DMA((SHARDS,))],
+        compiler_params=pltpu.CompilerParams(vmem_limit_bytes=VMEM_LIMIT),
+        cost_estimate=pl.CostEstimate(flops=1_600_000_000, bytes_accessed=4_000_000, transcendentals=0),
+        name="query",
+    )(order, hidden, angles, *blocks)
 
 
 def attention_kernel(order, coarse, *refs):
@@ -553,32 +592,31 @@
     low = lax.ppermute(line[-1:], "seq", [(i, (i + 1) % 8) for i in range(8)])
     high = lax.ppermute(line[:1], "seq", [(i, (i - 1) % 8) for i in range(8)])
     order = jnp.asarray(PLACES)[lax.axis_index("dp"), seq]
-    normed, taps, vectors = stem(order, line, stem_weight, stem_bias[None], conv_gain[None])
-    y, za, own_o, low, high, normed = lax.optimization_barrier((y, za, own_o, low, high, normed))
+    front, taps, vectors = stem_front(order, line, stem_weight, stem_bias[None], conv_gain[None])
+    y, za, own_o, low, high, front = lax.optimization_barrier((y, za, own_o, low, high, front))
 
     y_o, za_o = move(y, FROM_CORE), move(za, FROM_CORE)
     zb = move(za, FROM_X)
     yza = move(za, FROM_Y)
     zz = move(za, FROM_Z)
+    back = stem_back(line, taps, vectors)
     patch = edges(order, line, low, high, taps, vectors)
-    blocks = [own, own_o, y, za, y_o, za_o]
-    total = conv_part(0, order, normed, patch, blocks)
-    zb, yza, zz, total = lax.optimization_barrier((zb, yza, zz, total))
+    rest = (conv_bias[None], attn_gain[None], jnp.asarray(ANGLES)[seq])
+    zb, yza, zz, back, patch, *rest = lax.optimization_barrier((zb, yza, zz, back, patch, *rest))
     yzb = move(yza, FROM_X)
     yzz = move(zz, FROM_Y)
-    blocks += [zb, zz, yza] + [move(b, FROM_CORE) for b in (zb, zz, yza)]
-    total = conv_part(1, order, normed, patch, blocks, total)
+    blocks = [own, own_o, y, za, y_o, za_o, zb, zz, yza] + [move(b, FROM_CORE) for b in (zb, zz, yza)]
+    total = conv_part(0, order, front, back, patch, blocks)
     yzb, yzz, total = lax.optimization_barrier((yzb, yzz, total))
     blocks += [yzb, yzz, move(yzb, FROM_CORE), move(yzz, FROM_CORE)]
-    angles = jnp.asarray(ANGLES)[seq]
-    rest = (conv_bias[None], attn_gain[None], angles)
-    coarse, pair, query = conv_part(2, order, normed, patch, blocks, total, rest)
+    coarse, hidden, pair = conv_part(1, order, front, back, patch, blocks, (total, *rest))
 
     near = lax.ppermute(pair, "seq", [(i, i ^ 1) for i in range(8)])
     both = jnp.concatenate([pair, near], axis=0)
     pairs = [both] + [
         lax.ppermute(both, "seq", [(i, (i + shift) % 8) for i in range(8)]) for shift in (2, 6, 4)
     ]
+    query = query_of(order, hidden, rest[2], blocks)
     return attention(order, coarse, query, pairs, blocks)[None]
 
 

time: 130 us -> 125 us (0.962)
  Pallas kernels: 76.8 us -> 70.1 us
  starting transfers between devices: 25.2 us -> 27.6 us
  waiting for transfers between devices: 14.8 us -> 17.2 us
  local copies, waits for them, and re-layouts: 11.7 us -> 9.55 us
    ppermute x15, waiting for transfers between devices: 2 us -> 9.01 us  [move(): return lax.ppermute(value, AXES, pairs)]
    pallas_call x4 -> x5, Pallas kernels: 64.6 us -> 57.9 us  [the longest x2 37.7 us: conv_part(): pl.pallas_call(functools.partial(conv_kernel, part, len(used)), grid=(D /...]
    ppermute x3, waiting for transfers between devices: 8.42 us -> 2.99 us  [body(): lax.ppermute(both, 'seq', [(i, (i + shift) % 8) for i in range(8)])]
    ppermute x1, starting transfers between devices: 5.01 us -> 0.7 us  [body(): high = lax.ppermute(line[:1], 'seq', [(i, (i - 1) % 8) for i in range(8)])]
    ppermute x15, starting transfers between devices: 14.6 us -> 18.4 us  [move(): return lax.ppermute(value, AXES, pairs)]
    ppermute x1, starting transfers between devices: 0.63 us -> 2.83 us  [body(): low = lax.ppermute(line[-1:], 'seq', [(i, (i + 1) % 8) for i in range(8)])]
    unnamed x35 -> x33, local copies, waits for them, and re-layouts: 5.87 us -> 3.75 us
    ppermute x3, starting transfers between devices: 3.44 us -> 5.13 us  [body(): lax.ppermute(both, 'seq', [(i, (i + shift) % 8) for i in range(8)])]
  transfers between devices with their start and end apart: 21 -> 21, of which waited for: 3 -> 8; matrix products, arithmetic and copies ran while one was open for 5% -> 5% of each run, Pallas kernels for 38% -> 35%
where the time goes in v3:
time: 125 us
  Pallas kernels  70.1 us (56%)
  starting transfers between devices  27.6 us (22%)
  waiting for transfers between devices  17.2 us (14%)
  local copies, waits for them, and re-layouts  9.55 us (8%)
    pallas_call x2, Pallas kernels, conv_part(): pl.pallas_call(functools.partial(conv_kernel, part, len(used)), grid=(D /...  37.7 us
    ppermute x15, starting transfers between devices, move(): return lax.ppermute(value, AXES, pairs)  18.4 us
    ppermute x15, waiting for transfers between devices, move(): return lax.ppermute(value, AXES, pairs)  9.01 us
    pallas_call x1, Pallas kernels, stem_front(): pl.pallas_call(stem_kernel, out_shape=(jax.ShapeDtypeStruct((POOL_B // 2...  8.14 us
    pallas_call x1, Pallas kernels, stem_back(): pl.pallas_call(functools.partial(stem_rows, 1), out_shape=jax.ShapeDtypeS...  7.58 us
    pallas_call x1, Pallas kernels, attention(): pl.pallas_call(attention_kernel, out_shape=jax.ShapeDtypeStruct((ROWS, D)...  7.09 us
    ppermute x1, waiting for transfers between devices, body(): near = lax.ppermute(pair, 'seq', [(i, i ^ 1) for i in range(8)])  5.19 us
    ppermute x3, starting transfers between devices, body(): lax.ppermute(both, 'seq', [(i, (i + shift) % 8) for i in range(8)])  5.13 us
  transfers between devices with their start and end apart: 21, of which 8 were waited for; matrix products, arithmetic and copies ran while one was open for 5% of the time, Pallas kernels for 35%

profile of v3, /device:TPU:0, one launch (start us, length us, event | category | flops | bytes accessed | tf_op | source)
XLA Modules:
  0.0 124.8 jit_solution(3750443238959690338)
XLA Ops:
  0.0 2.4 %pack.1.refs_0_.refs_6_.refs_5_ = bf16[432,1536]{1,0:T(8,128)(2,1)} custom-call(bf16[5,48,1536]{2,1,0:T(8,128)(2,1)} %conv.3, bf16[96,1536]{1,0:T(8,128)(2,1)} %w_out.1, bf16[96,1024]{1,0:T(8,128)(2,1)} %w_query.1, bf16[96,128]{1,0:T(8,128)(2,1)} %w_key.1, bf16[96,192]{1,0:T(8,128)(2,1)} %w_value.1), custom_call_target="tpu_custom_call" | custom-call | tf_op jit(solution)/shard_map/pack/pallas_call | solution.py:271
  2.5 4.1 %collective-permute-start.1 = (bf16[432,1536]{1,0:T(8,128)(2,1)}, bf16[432,1536]{1,0:T(8,128)(2,1)S(1)}, u32[]{:S(2)}, u32[]{:S(2)}) collective-permute-start(bf16[432,1536]{1,0:T(8,128)(2,1)} %pack.1.refs_0_.refs_6_.refs_5_), channel_id=1, source_target_pairs={{0,48},{1,49},{2,18},{3,19},{4,52},{5,53},{6,22},{7,23},{8,24},{9,... | collective-permute-start | bytes 3981320 | tf_op jit(solution)/shard_map/ppermute | solution.py:570
  6.6 3.0 %collective-permute-start = (bf16[432,1536]{1,0:T(8,128)(2,1)}, bf16[432,1536]{1,0:T(8,128)(2,1)}, u32[]{:S(2)}, u32[]{:S(2)}) collective-permute-start(bf16[432,1536]{1,0:T(8,128)(2,1)} %pack.1.refs_0_.refs_6_.refs_5_), channel_id=1, source_target_pairs={{0,65},{1,64},{2,67},{3,66},{4,69},{5,68},{6,71},{7,70},{8,72},{9,... | collective-permute-start | bytes 3981320 | tf_op jit(solution)/shard_map/ppermute | solution.py:570
  9.6 0.7 fusion
  10.3 0.7 collective-permute-start.4
  11.0 2.8 %collective-permute-start.3 = (s32[1,128]{1,0:T(1,128)S(1)}, s32[1,128]{1,0:T(1,128)S(1)}, u32[]{:S(2)}, u32[]{:S(2)}) collective-permute-start(s32[1,128]{1,0:T(1,128)S(1)} %get-tuple-element.52), channel_id=1, source_target_pairs={{0,1},{1,2},{2,3},{3,4},{4,5},{5,6},{6,7},{7,0},{8,9},{9,10},{10,1... | collective-permute-start | bytes 1544 | tf_op jit(solution)/shard_map/ppermute | solution.py:592
  15.0 1.2 dynamic-slice_bitcast_fusion.1.order
  16.2 8.1 %stem_front.1 = (bf16[10,128,768]{2,1,0:T(8,128)(2,1)}, bf16[1024,768]{1,0:T(8,128)(2,1)}, f32[8,768]{1,0:T(8,128)}) custom-call(s32[17]{0:T(128)} %dynamic-slice_bitcast_fusion.1.order, s32[128,128]{1,0:T(8,128)} %bitcast.6, bf16[60,768]{1,0:T(8,128)(2,1)} %weight.1, f32[1,768]{1,0:T(1,128)} %broadcast_in_dim.15.bias, f32[1,768]{1,0:T(1,128)} %broadcast_in_dim.16.gain), custom_call_target="tpu_custom_call" | custom-call | flops 4000000000 | bytes 5000000 | tf_op jit(solution)/shard_map/stem_front/pallas_call | solution.py:189
  24.4 0.9 collective-permute-done.refs_2_.refs_8_.refs_7_
  25.8 3.5 %collective-permute-start.6 = (bf16[432,1536]{1,0:T(8,128)(2,1)S(1)}, bf16[432,1536]{1,0:T(8,128)(2,1)}, u32[]{:S(2)}, u32[]{:S(2)}) collective-permute-start(bf16[432,1536]{1,0:T(8,128)(2,1)S(1)} %collective-permute-done.1.refs_3_.refs_9_.refs_8_), channel_id=1, source_target_pairs={{0,65},{1,64},{2,67},{3,66},{4,69},{5,68},{6,71},{7,70},{8,72},{9,... | collective-permute-start | bytes 3981320 | tf_op jit(solution)/shard_map/ppermute | solution.py:570
  29.3 2.2 %collective-permute-start.5 = (bf16[432,1536]{1,0:T(8,128)(2,1)S(1)}, bf16[432,1536]{1,0:T(8,128)(2,1)}, u32[]{:S(2)}, u32[]{:S(2)}) collective-permute-start(bf16[432,1536]{1,0:T(8,128)(2,1)S(1)} %collective-permute-done.1.refs_3_.refs_9_.refs_8_), channel_id=1, source_target_pairs={{0,6},{1,7},{2,0},{3,1},{4,2},{5,3},{6,4},{7,5},{8,10},{9,11},{10,... | collective-permute-start | bytes 3981320 | tf_op jit(solution)/shard_map/ppermute | solution.py:570
  32.7 1.6 %dynamic-slice_bitcast_fusion.refs_19_.angles = f32[2,128,128]{2,1,0:T(8,128)} fusion(f32[8,2,128,128]{3,2,1,0:T(8,128)} %constant.20.clone, s32[]{:T(128)S(6)} %select_n.8), kind=kLoop, calls=%fused_computation | loop fusion | bytes 262148 | tf_op jit(solution)/shard_map/squeeze | solution.py:604
  34.2 7.6 %stem_back.1.back = bf16[10,128,768]{2,1,0:T(8,128)(2,1)} custom-call(s32[128,128]{1,0:T(8,128)} %bitcast.7, bf16[1024,768]{1,0:T(8,128)(2,1)} %get-tuple-element.31.taps, f32[8,768]{1,0:T(8,128)} %get-tuple-element.32.vectors), custom_call_target="tpu_custom_call" | custom-call | flops 3500000000 | bytes 4000000 | tf_op jit(solution)/shard_map/stem_back/pallas_call | solution.py:210
  42.4 2.7 %edges.1.patch = f32[16,768]{1,0:T(8,128)} custom-call(s32[17]{0:T(128)} %dynamic-slice_bitcast_fusion.1.order, s32[128,128]{1,0:T(8,128)} %bitcast.8, s32[1,128]{1,0:T(1,128)} %copy-done.15, s32[1,128]{1,0:T(1,128)} %copy-done.14, bf16[1024,768]{1,0:T(8,128)(2,1)} %get-tuple-element.31.taps, f32[8,768]{1,0:T(8,128)} %get-tuple-element.32.vectors), custom_call_target="tpu_custom_call" | custom-call | flops 30000000 | bytes 2000000 | tf_op jit(solution)/shard_map/edges/pallas_call | solution.py:246
  45.1 2.1 %collective-permute-done.5.refs_6_.refs_12_.refs_11_ = bf16[432,1536]{1,0:T(8,128)(2,1)} collective-permute-done((bf16[432,1536]{1,0:T(8,128)(2,1)S(1)}, bf16[432,1536]{1,0:T(8,128)(2,1)}, u32[]{:S(2)}, u32[]{:S(2)}) %collective-permute-start.5) | collective-permute-done | bytes 1327136 | tf_op jit(solution)/shard_map/ppermute | solution.py:570
  47.7 1.2 collective-permute-start.11
  48.9 2.2 %collective-permute-start.10 = (bf16[432,1536]{1,0:T(8,128)(2,1)}, bf16[432,1536]{1,0:T(8,128)(2,1)}, u32[]{:S(2)}, u32[]{:S(2)}) collective-permute-start(bf16[432,1536]{1,0:T(8,128)(2,1)} %collective-permute-done.6.refs_8_.refs_14_.refs_13_), channel_id=1, source_target_pairs={{0,6},{1,7},{2,0},{3,1},{4,2},{5,3},{6,4},{7,5},{8,10},{9,11},{10,... | collective-permute-start | bytes 3981320 | tf_op jit(solution)/shard_map/ppermute | solution.py:570
  51.1 1.2 collective-permute-done.14.refs_9_.refs_15_.refs_14_
  52.5 0.9 copy-done.2
  53.4 21.2 %conv.4.refs_16_ = f32[2,8,128,1536]{3,2,1,0:T(8,128)} custom-call(s32[17]{0:T(128)} %dynamic-slice_bitcast_fusion.1.order, bf16[10,128,768]{2,1,0:T(8,128)(2,1)} %get-tuple-element.29.front, bf16[10,128,768]{2,1,0:T(8,128)(2,1)} %stem_back.1.back, f32[16,768]{1,0:T(8,128)} %edges.1.patch, bf16[432,1536]{1,0:T(8,128)(2,1)} %pack.1.refs_0_.refs_6_.refs_5_, ...), custom_call_target="tpu_custom_call" | custom-call | flops 11274289152 | bytes 20000000 | tf_op jit(solution)/shard_map/conv/pallas_call | solution.py:477
  75.3 2.8 %collective-permute-done.15.refs_4_.refs_14_.refs_19_ = bf16[432,1536]{1,0:T(8,128)(2,1)S(1)} collective-permute-done((bf16[432,1536]{1,0:T(8,128)(2,1)}, bf16[432,1536]{1,0:T(8,128)(2,1)S(1)}, u32[]{:S(2)}, u32[]{:S(2)}) %collective-permute-start.15) | collective-permute-done | bytes 1327136 | tf_op jit(solution)/shard_map/ppermute | solution.py:570
  78.1 1.9 %collective-permute-done.16.refs_5_.refs_15_.refs_20_ = bf16[432,1536]{1,0:T(8,128)(2,1)S(1)} collective-permute-done((bf16[432,1536]{1,0:T(8,128)(2,1)}, bf16[432,1536]{1,0:T(8,128)(2,1)S(1)}, u32[]{:S(2)}, u32[]{:S(2)}) %collective-permute-start.16) | collective-permute-done | bytes 1327136 | tf_op jit(solution)/shard_map/ppermute | solution.py:570
  80.0 1.1 copy-done.5
  81.1 16.4 %conv.5 = (bf16[128,1536]{1,0:T(8,128)(2,1)}, bf16[128,1536]{1,0:T(8,128)(2,1)}, bf16[128,384]{1,0:T(8,128)(2,1)}) custom-call(s32[17]{0:T(128)} %dynamic-slice_bitcast_fusion.1.order, bf16[10,128,768]{2,1,0:T(8,128)(2,1)} %get-tuple-element.29.front, bf16[10,128,768]{2,1,0:T(8,128)(2,1)} %stem_back.1.back, f32[16,768]{1,0:T(8,128)} %edges.1.patch, ...), custom_call_target="tpu_custom_call" | custom-call | flops 5637144576 | bytes 20000000 | tf_op jit(solution)/shard_map/conv/pallas_call | solution.py:477
  98.0 0.9 constant_dynamic-update-slice_fusion.1
  98.9 5.2 %collective-permute-done.17 = bf16[128,384]{1,0:T(8,128)(2,1)S(1)} collective-permute-done((bf16[128,384]{1,0:T(8,128)(2,1)}, bf16[128,384]{1,0:T(8,128)(2,1)S(1)}, u32[]{:S(2)}, u32[]{:S(2)}) %collective-permute-start.17) | collective-permute-done | bytes 98336 | tf_op jit(solution)/shard_map/ppermute | solution.py:614
  104.1 3.1 %collective-permute-start.20 = (bf16[256,384]{1,0:T(8,128)(2,1)S(1)}, bf16[256,384]{1,0:T(8,128)(2,1)S(1)}, u32[]{:S(2)}, u32[]{:S(2)}) collective-permute-start(bf16[256,384]{1,0:T(8,128)(2,1)S(1)} %constant_dynamic-update-slice_fusion.refs_1_), channel_id=1, source_target_pairs={{0,4},{1,5},{2,6},{3,7},{4,0},{5,1},{6,2},{7,3},{8,12},{9,13},{10,... | collective-permute-start | bytes 589832 | tf_op jit(solution)/shard_map/ppermute | solution.py:617
  107.9 1.4 %collective-permute-start.18 = (bf16[256,384]{1,0:T(8,128)(2,1)S(1)}, bf16[256,384]{1,0:T(8,128)(2,1)S(1)}, u32[]{:S(2)}, u32[]{:S(2)}) collective-permute-start(bf16[256,384]{1,0:T(8,128)(2,1)S(1)} %constant_dynamic-update-slice_fusion.refs_1_), channel_id=1, source_target_pairs={{0,2},{1,3},{2,4},{3,5},{4,6},{5,7},{6,0},{7,1},{8,10},{9,11},{10,... | collective-permute-start | bytes 589832 | tf_op jit(solution)/shard_map/ppermute | solution.py:617
  109.3 4.5 %query.1.refs_0_ = bf16[1024,128]{1,0:T(8,128)(2,1)} custom-call(s32[17]{0:T(128)} %dynamic-slice_bitcast_fusion.1.order, bf16[128,1536]{1,0:T(8,128)(2,1)} %get-tuple-element.49.hidden, f32[2,128,128]{2,1,0:T(8,128)} %dynamic-slice_bitcast_fusion.refs_19_.angles, bf16[432,1536]{1,0:T(8,128)(2,1)} %pack.1.refs_0_.refs_6_.refs_5_, bf16[432,1536]{1,0:T(8,128)(2,1)} %copy-done, ...), custom_call_target="tpu_custom_call" | custom-call | flops 1600000000 | bytes 4000000 | tf_op jit(solution)/shard_map/query/pallas_call | solution.py:521
  113.8 3.0 %collective-permute-done.19.refs_3_ = bf16[256,384]{1,0:T(8,128)(2,1)S(1)} collective-permute-done((bf16[256,384]{1,0:T(8,128)(2,1)S(1)}, bf16[256,384]{1,0:T(8,128)(2,1)S(1)}, u32[]{:S(2)}, u32[]{:S(2)}) %collective-permute-start.19) | collective-permute-done | bytes 196640 | tf_op jit(solution)/shard_map/ppermute | solution.py:617
  116.8 0.7 copy-done.8
  117.6 7.1 %attention.1 = bf16[128,1536]{1,0:T(8,128)(2,1)} custom-call(s32[17]{0:T(128)} %dynamic-slice_bitcast_fusion.1.order, bf16[128,1536]{1,0:T(8,128)(2,1)} %get-tuple-element.48.coarse, bf16[1024,128]{1,0:T(8,128)(2,1)} %query.1.refs_0_, bf16[256,384]{1,0:T(8,128)(2,1)} %copy-done.6, bf16[256,384]{1,0:T(8,128)(2,1)} %copy-done.9, bf16[256,384]{1,0:T(8,128)(2,1)} %copy-done.8, ...), custom_call_target="tpu_custom_call" | custom-call | flops 3000000000 | bytes 6000000 | tf_op jit(solution)/shard_map/attention/pallas_call | solution.py:557
  (59 shorter events, 6.1 us)
Async XLA Ops:
  0.0 13.8 %copy-start.12 = (f32[768]{0:T(1024)S(1)}, f32[768]{0:T(1024)}, u32[]{:S(2)}) copy-start(f32[768]{0:T(1024)} %param.15) | copy-start | bytes 9220
  0.0 14.4 %copy-start.13 = (f32[768]{0:T(1024)S(1)}, f32[768]{0:T(1024)}, u32[]{:S(2)}) copy-start(f32[768]{0:T(1024)} %param.16) | copy-start | bytes 9220
  2.4 21.9 %collective-permute-start.2 = (bf16[432,1536]{1,0:T(8,128)(2,1)}, bf16[432,1536]{1,0:T(8,128)(2,1)S(1)}, u32[]{:S(2)}, u32[]{:S(2)}) collective-permute-start(bf16[432,1536]{1,0:T(8,128)(2,1)} %pack.1.refs_0_.refs_6_.refs_5_), channel_id=1, source_target_pairs={{0,8},{1,9},{2,10},{3,11},{4,12},{5,13},{6,14},{7,15},{8,0},{9,1},... | collective-permute-start | bytes 3981320 | tf_op jit(solution)/shard_map/ppermute | solution.py:570
  2.5 21.9 %collective-permute-start.1 = (bf16[432,1536]{1,0:T(8,128)(2,1)}, bf16[432,1536]{1,0:T(8,128)(2,1)S(1)}, u32[]{:S(2)}, u32[]{:S(2)}) collective-permute-start(bf16[432,1536]{1,0:T(8,128)(2,1)} %pack.1.refs_0_.refs_6_.refs_5_), channel_id=1, source_target_pairs={{0,48},{1,49},{2,18},{3,19},{4,52},{5,53},{6,22},{7,23},{8,24},{9,... | collective-permute-start | bytes 3981320 | tf_op jit(solution)/shard_map/ppermute | solution.py:570
  6.6 18.7 %collective-permute-start = (bf16[432,1536]{1,0:T(8,128)(2,1)}, bf16[432,1536]{1,0:T(8,128)(2,1)}, u32[]{:S(2)}, u32[]{:S(2)}) collective-permute-start(bf16[432,1536]{1,0:T(8,128)(2,1)} %pack.1.refs_0_.refs_6_.refs_5_), channel_id=1, source_target_pairs={{0,65},{1,64},{2,67},{3,66},{4,69},{5,68},{6,71},{7,70},{8,72},{9,... | collective-permute-start | bytes 3981320 | tf_op jit(solution)/shard_map/ppermute | solution.py:570
  10.3 14.0 %collective-permute-start.4 = (s32[1,128]{1,0:T(1,128)S(1)}, s32[1,128]{1,0:T(1,128)S(1)}, u32[]{:S(2)}, u32[]{:S(2)}) collective-permute-start(s32[1,128]{1,0:T(1,128)S(1)} %get-tuple-element.51), channel_id=1, source_target_pairs={{0,7},{1,0},{2,1},{3,2},{4,3},{5,4},{6,5},{7,6},{8,15},{9,8},{10,9... | collective-permute-start | bytes 1544 | tf_op jit(solution)/shard_map/ppermute | solution.py:593
  11.0 13.3 %collective-permute-start.3 = (s32[1,128]{1,0:T(1,128)S(1)}, s32[1,128]{1,0:T(1,128)S(1)}, u32[]{:S(2)}, u32[]{:S(2)}) collective-permute-start(s32[1,128]{1,0:T(1,128)S(1)} %get-tuple-element.52), channel_id=1, source_target_pairs={{0,1},{1,2},{2,3},{3,4},{4,5},{5,6},{6,7},{7,0},{8,9},{9,10},{10,1... | collective-permute-start | bytes 1544 | tf_op jit(solution)/shard_map/ppermute | solution.py:592
  16.2 15.3 %copy-start.10 = (f32[1536]{0:T(1024)S(1)}, f32[1536]{0:T(1024)}, u32[]{:S(2)}) copy-start(f32[1536]{0:T(1024)} %param.18) | copy-start | bytes 18436
  16.2 15.9 %copy-start.11 = (f32[1536]{0:T(1024)S(1)}, f32[1536]{0:T(1024)}, u32[]{:S(2)}) copy-start(f32[1536]{0:T(1024)} %param.19) | copy-start | bytes 18436
  24.3 17.5 %copy-start.14 = (s32[1,128]{1,0:T(1,128)}, s32[1,128]{1,0:T(1,128)S(1)}, u32[]{:S(2)}) copy-start(s32[1,128]{1,0:T(1,128)S(1)} %collective-permute-done.4.high_row) | copy-start | bytes 1540
  24.3 17.5 %copy-start.15 = (s32[1,128]{1,0:T(1,128)}, s32[1,128]{1,0:T(1,128)S(1)}, u32[]{:S(2)}) copy-start(s32[1,128]{1,0:T(1,128)S(1)} %collective-permute-done.3.low_row) | copy-start | bytes 1540
  24.3 17.5 %copy-start = (bf16[432,1536]{1,0:T(8,128)(2,1)}, bf16[432,1536]{1,0:T(8,128)(2,1)S(1)}, u32[]{:S(2)}) copy-start(bf16[432,1536]{1,0:T(8,128)(2,1)S(1)} %collective-permute-done.2.refs_1_.refs_7_.refs_6_) | copy-start | bytes 3981316
  24.4 17.5 %copy-start.1 = (bf16[432,1536]{1,0:T(8,128)(2,1)}, bf16[432,1536]{1,0:T(8,128)(2,1)S(1)}, u32[]{:S(2)}) copy-start(bf16[432,1536]{1,0:T(8,128)(2,1)S(1)} %collective-permute-done.1.refs_3_.refs_9_.refs_8_) | copy-start | bytes 3981316
  25.2 19.9 %collective-permute-start.7 = (bf16[432,1536]{1,0:T(8,128)(2,1)S(1)}, bf16[432,1536]{1,0:T(8,128)(2,1)}, u32[]{:S(2)}, u32[]{:S(2)}) collective-permute-start(bf16[432,1536]{1,0:T(8,128)(2,1)S(1)} %collective-permute-done.1.refs_3_.refs_9_.refs_8_), channel_id=1, source_target_pairs={{0,48},{1,49},{2,18},{3,19},{4,52},{5,53},{6,22},{7,23},{8,24},{9,... | collective-permute-start | bytes 3981320 | tf_op jit(solution)/shard_map/ppermute | solution.py:570
  25.8 19.4 %collective-permute-start.6 = (bf16[432,1536]{1,0:T(8,128)(2,1)S(1)}, bf16[432,1536]{1,0:T(8,128)(2,1)}, u32[]{:S(2)}, u32[]{:S(2)}) collective-permute-start(bf16[432,1536]{1,0:T(8,128)(2,1)S(1)} %collective-permute-done.1.refs_3_.refs_9_.refs_8_), channel_id=1, source_target_pairs={{0,65},{1,64},{2,67},{3,66},{4,69},{5,68},{6,71},{7,70},{8,72},{9,... | collective-permute-start | bytes 3981320 | tf_op jit(solution)/shard_map/ppermute | solution.py:570
  29.3 17.9 %collective-permute-start.5 = (bf16[432,1536]{1,0:T(8,128)(2,1)S(1)}, bf16[432,1536]{1,0:T(8,128)(2,1)}, u32[]{:S(2)}, u32[]{:S(2)}) collective-permute-start(bf16[432,1536]{1,0:T(8,128)(2,1)S(1)} %collective-permute-done.1.refs_3_.refs_9_.refs_8_), channel_id=1, source_target_pairs={{0,6},{1,7},{2,0},{3,1},{4,2},{5,3},{6,4},{7,5},{8,10},{9,11},{10,... | collective-permute-start | bytes 3981320 | tf_op jit(solution)/shard_map/ppermute | solution.py:570
  34.2 14.7 %collective-permute-start.12 = (bf16[432,1536]{1,0:T(8,128)(2,1)}, bf16[432,1536]{1,0:T(8,128)(2,1)}, u32[]{:S(2)}, u32[]{:S(2)}) collective-permute-start(bf16[432,1536]{1,0:T(8,128)(2,1)} %collective-permute-done.refs_2_.refs_8_.refs_7_), channel_id=1, source_target_pairs={{0,8},{1,9},{2,10},{3,11},{4,12},{5,13},{6,14},{7,15},{8,0},{9,1},... | collective-permute-start | bytes 3981320 | tf_op jit(solution)/shard_map/ppermute | solution.py:570
  41.9 9.2 %collective-permute-start.13 = (bf16[432,1536]{1,0:T(8,128)(2,1)S(1)}, bf16[432,1536]{1,0:T(8,128)(2,1)}, u32[]{:S(2)}, u32[]{:S(2)}) collective-permute-start(bf16[432,1536]{1,0:T(8,128)(2,1)S(1)} %collective-permute-done.1.refs_3_.refs_9_.refs_8_), channel_id=1, source_target_pairs={{0,8},{1,9},{2,10},{3,11},{4,12},{5,13},{6,14},{7,15},{8,0},{9,1},... | collective-permute-start | bytes 3981320 | tf_op jit(solution)/shard_map/ppermute | solution.py:570
  47.2 5.1 %collective-permute-start.14 = (bf16[432,1536]{1,0:T(8,128)(2,1)}, bf16[432,1536]{1,0:T(8,128)(2,1)S(1)}, u32[]{:S(2)}, u32[]{:S(2)}) collective-permute-start(bf16[432,1536]{1,0:T(8,128)(2,1)} %collective-permute-done.5.refs_6_.refs_12_.refs_11_), channel_id=1, source_target_pairs={{0,8},{1,9},{2,10},{3,11},{4,12},{5,13},{6,14},{7,15},{8,0},{9,1},... | collective-permute-start | bytes 3981320 | tf_op jit(solution)/shard_map/ppermute | solution.py:570
  47.2 5.3 %collective-permute-start.8 = (bf16[432,1536]{1,0:T(8,128)(2,1)}, bf16[432,1536]{1,0:T(8,128)(2,1)}, u32[]{:S(2)}, u32[]{:S(2)}) collective-permute-start(bf16[432,1536]{1,0:T(8,128)(2,1)} %collective-permute-done.7.refs_7_.refs_13_.refs_12_), channel_id=1, source_target_pairs={{0,8},{1,9},{2,10},{3,11},{4,12},{5,13},{6,14},{7,15},{8,0},{9,1},... | collective-permute-start | bytes 3981320 | tf_op jit(solution)/shard_map/ppermute | solution.py:570
  47.7 27.0 %collective-permute-start.11 = (bf16[432,1536]{1,0:T(8,128)(2,1)}, bf16[432,1536]{1,0:T(8,128)(2,1)}, u32[]{:S(2)}, u32[]{:S(2)}) collective-permute-start(bf16[432,1536]{1,0:T(8,128)(2,1)} %collective-permute-done.7.refs_7_.refs_13_.refs_12_), channel_id=1, source_target_pairs={{0,65},{1,64},{2,67},{3,66},{4,69},{5,68},{6,71},{7,70},{8,72},{9,... | collective-permute-start | bytes 3981320 | tf_op jit(solution)/shard_map/ppermute | solution.py:570
  48.9 25.8 %collective-permute-start.10 = (bf16[432,1536]{1,0:T(8,128)(2,1)}, bf16[432,1536]{1,0:T(8,128)(2,1)}, u32[]{:S(2)}, u32[]{:S(2)}) collective-permute-start(bf16[432,1536]{1,0:T(8,128)(2,1)} %collective-permute-done.6.refs_8_.refs_14_.refs_13_), channel_id=1, source_target_pairs={{0,6},{1,7},{2,0},{3,1},{4,2},{5,3},{6,4},{7,5},{8,10},{9,11},{10,... | collective-permute-start | bytes 3981320 | tf_op jit(solution)/shard_map/ppermute | solution.py:570
  51.1 24.2 %collective-permute-start.9 = (bf16[432,1536]{1,0:T(8,128)(2,1)}, bf16[432,1536]{1,0:T(8,128)(2,1)S(1)}, u32[]{:S(2)}, u32[]{:S(2)}) collective-permute-start(bf16[432,1536]{1,0:T(8,128)(2,1)} %collective-permute-done.6.refs_8_.refs_14_.refs_13_), channel_id=1, source_target_pairs={{0,8},{1,9},{2,10},{3,11},{4,12},{5,13},{6,14},{7,15},{8,0},{9,1},... | collective-permute-start | bytes 3981320 | tf_op jit(solution)/shard_map/ppermute | solution.py:570
  74.7 3.3 %collective-permute-start.15 = (bf16[432,1536]{1,0:T(8,128)(2,1)}, bf16[432,1536]{1,0:T(8,128)(2,1)S(1)}, u32[]{:S(2)}, u32[]{:S(2)}) collective-permute-start(bf16[432,1536]{1,0:T(8,128)(2,1)} %collective-permute-done.10.refs_2_.refs_12_.refs_17_), channel_id=1, source_target_pairs={{0,8},{1,9},{2,10},{3,11},{4,12},{5,13},{6,14},{7,15},{8,0},{9,1},... | collective-permute-start | bytes 3981320 | tf_op jit(solution)/shard_map/ppermute | solution.py:570
  74.9 5.0 %collective-permute-start.16 = (bf16[432,1536]{1,0:T(8,128)(2,1)}, bf16[432,1536]{1,0:T(8,128)(2,1)S(1)}, u32[]{:S(2)}, u32[]{:S(2)}) collective-permute-start(bf16[432,1536]{1,0:T(8,128)(2,1)} %collective-permute-done.11.refs_3_.refs_13_.refs_18_), channel_id=1, source_target_pairs={{0,8},{1,9},{2,10},{3,11},{4,12},{5,13},{6,14},{7,15},{8,0},{9,1},... | collective-permute-start | bytes 3981320 | tf_op jit(solution)/shard_map/ppermute | solution.py:570
  75.3 4.7 %copy-start.3 = (bf16[432,1536]{1,0:T(8,128)(2,1)}, bf16[432,1536]{1,0:T(8,128)(2,1)S(1)}, u32[]{:S(2)}) copy-start(bf16[432,1536]{1,0:T(8,128)(2,1)S(1)} %collective-permute-done.9.refs_1_.refs_11_.refs_16_) | copy-start | bytes 3981316
  97.5 6.6 %collective-permute-start.17 = (bf16[128,384]{1,0:T(8,128)(2,1)}, bf16[128,384]{1,0:T(8,128)(2,1)S(1)}, u32[]{:S(2)}, u32[]{:S(2)}) collective-permute-start(bf16[128,384]{1,0:T(8,128)(2,1)} %get-tuple-element.50), channel_id=1, source_target_pairs={{0,1},{1,0},{2,3},{3,2},{4,5},{5,4},{6,7},{7,6},{8,9},{9,8},{10,11... | collective-permute-start | bytes 294920 | tf_op jit(solution)/shard_map/ppermute | solution.py:614
  104.1 9.7 %copy-start.6 = (bf16[256,384]{1,0:T(8,128)(2,1)}, bf16[256,384]{1,0:T(8,128)(2,1)S(1)}, u32[]{:S(2)}) copy-start(bf16[256,384]{1,0:T(8,128)(2,1)S(1)} %constant_dynamic-update-slice_fusion.refs_1_) | copy-start | bytes 589828
  104.1 9.7 %collective-permute-start.20 = (bf16[256,384]{1,0:T(8,128)(2,1)S(1)}, bf16[256,384]{1,0:T(8,128)(2,1)S(1)}, u32[]{:S(2)}, u32[]{:S(2)}) collective-permute-start(bf16[256,384]{1,0:T(8,128)(2,1)S(1)} %constant_dynamic-update-slice_fusion.refs_1_), channel_id=1, source_target_pairs={{0,4},{1,5},{2,6},{3,7},{4,0},{5,1},{6,2},{7,3},{8,12},{9,13},{10,... | collective-permute-start | bytes 589832 | tf_op jit(solution)/shard_map/ppermute | solution.py:617
  107.2 9.5 %collective-permute-start.19 = (bf16[256,384]{1,0:T(8,128)(2,1)S(1)}, bf16[256,384]{1,0:T(8,128)(2,1)S(1)}, u32[]{:S(2)}, u32[]{:S(2)}) collective-permute-start(bf16[256,384]{1,0:T(8,128)(2,1)S(1)} %constant_dynamic-update-slice_fusion.refs_1_), channel_id=1, source_target_pairs={{0,6},{1,7},{2,0},{3,1},{4,2},{5,3},{6,4},{7,5},{8,14},{9,15},{10,... | collective-permute-start | bytes 589832 | tf_op jit(solution)/shard_map/ppermute | solution.py:617
  107.9 8.9 %collective-permute-start.18 = (bf16[256,384]{1,0:T(8,128)(2,1)S(1)}, bf16[256,384]{1,0:T(8,128)(2,1)S(1)}, u32[]{:S(2)}, u32[]{:S(2)}) collective-permute-start(bf16[256,384]{1,0:T(8,128)(2,1)S(1)} %constant_dynamic-update-slice_fusion.refs_1_), channel_id=1, source_target_pairs={{0,2},{1,3},{2,4},{3,5},{4,6},{5,7},{6,0},{7,1},{8,10},{9,11},{10,... | collective-permute-start | bytes 589832 | tf_op jit(solution)/shard_map/ppermute | solution.py:617
  113.8 3.0 %copy-start.7 = (bf16[256,384]{1,0:T(8,128)(2,1)}, bf16[256,384]{1,0:T(8,128)(2,1)S(1)}, u32[]{:S(2)}) copy-start(bf16[256,384]{1,0:T(8,128)(2,1)S(1)} %collective-permute-done.20.refs_4_) | copy-start | bytes 589828
  (5 other events, 5.5 us)

commit v4 on v3

--- a/solution.py
+++ b/solution.py
@@ -56,6 +56,7 @@
 FROM_Y = received_from(lambda x, y, z, core: (x, y + side(core), z, core))
 FROM_X = received_from(lambda x, y, z, core: (x + side(core), y, z, core))
 FROM_Z = received_from(lambda x, y, z, core: (x, y, z + turn(x, core), core))
+FROM_Z_CROSS = received_from(lambda x, y, z, core: (x, y, z + turn(x, 1 - core), 1 - core))
 FROM_CORE = received_from(lambda x, y, z, core: (x, y, z, 1 - core))
 
 
@@ -293,8 +294,7 @@
     return pieces
 
 
-COLUMNS = 512
-PAIRS = 4
+TILES = ((512, 8), (256, 8))
 KV_WIDTH = 384
 
 
@@ -312,8 +312,9 @@
     pieces = pieces_of(part)
     first = pieces[0][0]
     start, size = PARTS[part]
+    tile, pairs = TILES[part]
     third, step = pl.program_id(0), pl.program_id(1)
-    columns = pl.ds(pl.multiple_of(third * COLUMNS, COLUMNS), COLUMNS)
+    columns = pl.ds(pl.multiple_of(third * tile, tile), tile)
     homes = [(w_a, 0), (w_1, 0), (w_d, 0), (w_a, size), (w_d, size)]
 
     def copies():
@@ -385,14 +386,14 @@
         w_b[size:] = w_a[size:, columns] + w_d[size:, columns]
 
     def part_of(lhs):
-        return lhs[pl.ds(step * PAIRS, PAIRS)].reshape(PAIRS * ROWS, -1)
+        return lhs[pl.ds(step * pairs, pairs)].reshape(pairs * ROWS, -1)
 
     a = dot(part_of(lhs_a), w_a[:, columns])
     b = dot(part_of(lhs_b), w_b[...])
     c = dot(part_of(lhs_c), w_c[...])
     d = dot(part_of(lhs_d), w_d[:, columns])
-    even = (a + (b + c)).reshape(PAIRS, ROWS, COLUMNS)
-    odd = ((b - c) - d).reshape(PAIRS, ROWS, COLUMNS)
+    even = (a + (b + c)).reshape(pairs, ROWS, tile)
+    odd = ((b - c) - d).reshape(pairs, ROWS, tile)
     if part == 1:
         even = even + acc_in[0]
         odd = odd + acc_in[1]
@@ -408,18 +409,18 @@
         most_ref[...] = most
         least_ref[...] = least
 
-    last = POOL_B // 2 // PAIRS - 1
-    for n in range(D // COLUMNS):
+    last = POOL_B // 2 // pairs - 1
+    for n in range(D // tile):
 
         @pl.when((step == last) & (third == n))
         def _():
-            here = slice(n * COLUMNS, (n + 1) * COLUMNS)
+            here = slice(n * tile, (n + 1) * tile)
             shift = bias[:, here]
             high = jnp.maximum(most_ref[...], most) + shift
             low = jnp.minimum(least_ref[...], least) + shift
             coarse[:, here] = jnp.maximum(gelu(high), gelu(low)).astype(jnp.bfloat16)
 
-    @pl.when((step == last) & (third == D // COLUMNS - 1))
+    @pl.when((step == last) & (third == D // tile - 1))
     def _():
         residual = coarse[...].astype(jnp.float32)
         scale = lax.rsqrt(jnp.mean(residual * residual, axis=-1, keepdims=True) + EPSILON)
@@ -434,17 +435,18 @@
 def conv_part(part, order, front, back, patch, blocks, rest=()):
     pieces = pieces_of(part)
     start, size = PARTS[part]
+    tile, pairs = TILES[part]
     used = blocks[: pieces[-1][0] + 1] if part == 0 else blocks[pieces[0][0] :] + blocks[: pieces[0][0]]
     args = [order, front, back, patch, *used]
     whole = pl.BlockSpec(memory_space=pltpu.VMEM)
     in_specs = [
         pl.BlockSpec(memory_space=pltpu.SMEM),
-        pl.BlockSpec(memory_space=pl.ANY),
-        pl.BlockSpec(memory_space=pl.ANY),
+        pl.BlockSpec(memory_space=pltpu.HBM),
+        pl.BlockSpec(memory_space=pltpu.HBM),
         pl.BlockSpec((16, size), lambda i, j: (0, start // size)),
     ]
-    in_specs += [pl.BlockSpec(memory_space=pl.ANY)] * len(used)
-    acc_spec = pl.BlockSpec((2, PAIRS, ROWS, COLUMNS), lambda i, j: (0, j, 0, i))
+    in_specs += [pl.BlockSpec(memory_space=pltpu.HBM)] * len(used)
+    acc_spec = pl.BlockSpec((2, pairs, ROWS, tile), lambda i, j: (0, j, 0, i))
     lhs = (POOL_B // 2, ROWS)
     scratch = [
         pltpu.VMEM((POOL_B + 4, ROWS, size), jnp.bfloat16),
@@ -453,8 +455,8 @@
         pltpu.VMEM((*lhs, size), jnp.bfloat16),
         pltpu.VMEM((*lhs, 2 * size), jnp.bfloat16),
         pltpu.VMEM((2 * size, D), jnp.bfloat16),
-        pltpu.VMEM((2 * size, COLUMNS), jnp.bfloat16),
-        pltpu.VMEM((size, COLUMNS), jnp.bfloat16),
+        pltpu.VMEM((2 * size, tile), jnp.bfloat16),
+        pltpu.VMEM((size, tile), jnp.bfloat16),
         pltpu.VMEM((2 * size, D), jnp.bfloat16),
         pltpu.VMEM((size, D), jnp.bfloat16),
         pltpu.SemaphoreType.DMA((KW * len(pieces),)),
@@ -469,14 +471,14 @@
             jax.ShapeDtypeStruct((ROWS, KV_WIDTH), jnp.bfloat16),
         )
         out_spec = (whole, whole, whole)
-        scratch += [pltpu.VMEM((ROWS, COLUMNS), jnp.float32)] * 2
+        scratch += [pltpu.VMEM((ROWS, tile), jnp.float32)] * 2
         scratch += [pltpu.VMEM((D, KV_WIDTH), jnp.bfloat16), pltpu.SemaphoreType.DMA((SHARDS,))]
     else:
         out_shape = jax.ShapeDtypeStruct((2, POOL_B // 2, ROWS, D), jnp.float32)
         out_spec = acc_spec
     return pl.pallas_call(
         functools.partial(conv_kernel, part, len(used)),
-        grid=(D // COLUMNS, POOL_B // 2 // PAIRS),
+        grid=(D // tile, POOL_B // 2 // pairs),
         out_shape=out_shape,
         in_specs=in_specs,
         out_specs=out_spec,
@@ -521,7 +523,7 @@
     return pl.pallas_call(
         query_kernel,
         out_shape=jax.ShapeDtypeStruct((HEADS * ROWS, HEAD_K), jnp.bfloat16),
-        in_specs=[pl.BlockSpec(memory_space=pltpu.SMEM)] + [vmem] * 2 + [pl.BlockSpec(memory_space=pl.ANY)] * SHARDS,
+        in_specs=[pl.BlockSpec(memory_space=pltpu.SMEM)] + [vmem] * 2 + [pl.BlockSpec(memory_space=pltpu.HBM)] * SHARDS,
         out_specs=vmem,
         scratch_shapes=[pltpu.VMEM((D, HEADS * HEAD_K), jnp.bfloat16), pltpu.SemaphoreType.DMA((SHARDS,))],
         compiler_params=pltpu.CompilerParams(vmem_limit_bytes=VMEM_LIMIT),
@@ -557,7 +559,7 @@
     return pl.pallas_call(
         attention_kernel,
         out_shape=jax.ShapeDtypeStruct((ROWS, D), jnp.bfloat16),
-        in_specs=[pl.BlockSpec(memory_space=pltpu.SMEM)] + [vmem] * 6 + [pl.BlockSpec(memory_space=pl.ANY)] * SHARDS,
+        in_specs=[pl.BlockSpec(memory_space=pltpu.SMEM)] + [vmem] * 6 + [pl.BlockSpec(memory_space=pltpu.HBM)] * SHARDS,
         out_specs=vmem,
         scratch_shapes=[pltpu.VMEM((D, D), jnp.bfloat16), pltpu.SemaphoreType.DMA((SHARDS,))],
         compiler_params=pltpu.CompilerParams(vmem_limit_bytes=VMEM_LIMIT),
@@ -605,10 +607,11 @@
     zb, yza, zz, back, patch, *rest = lax.optimization_barrier((zb, yza, zz, back, patch, *rest))
     yzb = move(yza, FROM_X)
     yzz = move(zz, FROM_Y)
+    yzz_o = move(yza, FROM_Z_CROSS)
     blocks = [own, own_o, y, za, y_o, za_o, zb, zz, yza] + [move(b, FROM_CORE) for b in (zb, zz, yza)]
     total = conv_part(0, order, front, back, patch, blocks)
-    yzb, yzz, total = lax.optimization_barrier((yzb, yzz, total))
-    blocks += [yzb, yzz, move(yzb, FROM_CORE), move(yzz, FROM_CORE)]
+    yzb, yzz, yzz_o, total = lax.optimization_barrier((yzb, yzz, yzz_o, total))
+    blocks += [yzb, yzz, move(yzb, FROM_CORE), yzz_o]
     coarse, hidden, pair = conv_part(1, order, front, back, patch, blocks, (total, *rest))
 
     near = lax.ppermute(pair, "seq", [(i, i ^ 1) for i in range(8)])

time: 125 us -> 122 us (0.976)
  waiting for transfers between devices: 17.2 us -> 13.5 us
  starting transfers between devices: 27.6 us -> 29.1 us
  Pallas kernels: 70.1 us -> 68.8 us
    ppermute x15, waiting for transfers between devices: 9.01 us -> 6.05 us  [move(): return lax.ppermute(value, AXES, pairs)]
    pallas_call x2, Pallas kernels: 37.7 us -> 36.3 us  [conv_part(): pl.pallas_call(functools.partial(conv_kernel, part, len(used)), grid=(D /...]
  transfers between devices with their start and end apart: 21 -> 21, of which waited for: 8 -> 5; matrix products, arithmetic and copies ran while one was open for 5% -> 6% of each run, Pallas kernels for 35% -> 36%
where the time goes in v4:
time: 122 us; the launch traced here: 121 us
  Pallas kernels  68.8 us (56%)
  starting transfers between devices  29.1 us (24%)
  waiting for transfers between devices  13.5 us (11%)
  local copies, waits for them, and re-layouts  9.63 us (8%)
    pallas_call x2, Pallas kernels, conv_part(): pl.pallas_call(functools.partial(conv_kernel, part, len(used)), grid=(D /...  36.3 us
    ppermute x15, starting transfers between devices, move(): return lax.ppermute(value, AXES, pairs)  19.3 us
    pallas_call x1, Pallas kernels, stem_front(): pl.pallas_call(stem_kernel, out_shape=(jax.ShapeDtypeStruct((POOL_B // 2...  8.14 us
    pallas_call x1, Pallas kernels, stem_back(): pl.pallas_call(functools.partial(stem_rows, 1), out_shape=jax.ShapeDtypeS...  7.59 us
    pallas_call x1, Pallas kernels, attention(): pl.pallas_call(attention_kernel, out_shape=jax.ShapeDtypeStruct((ROWS, D)...  7.09 us
    ppermute x15, waiting for transfers between devices, move(): return lax.ppermute(value, AXES, pairs)  6.05 us
    ppermute x3, starting transfers between devices, body(): lax.ppermute(both, 'seq', [(i, (i + shift) % 8) for i in range(8)])  5.06 us
    ppermute x1, waiting for transfers between devices, body(): near = lax.ppermute(pair, 'seq', [(i, i ^ 1) for i in range(8)])  4.51 us
  transfers between devices with their start and end apart: 21, of which 5 were waited for; matrix products, arithmetic and copies ran while one was open for 6% of the time, Pallas kernels for 36%

profile of v4, /device:TPU:0, one launch (start us, length us, event | category | flops | bytes accessed | tf_op | source)
XLA Modules:
  0.0 121.4 jit_solution(18419313876968398098)
XLA Ops:
  0.0 2.4 %pack.1.refs_0_.refs_6_.refs_5_ = bf16[432,1536]{1,0:T(8,128)(2,1)} custom-call(bf16[5,48,1536]{2,1,0:T(8,128)(2,1)} %conv.3, bf16[96,1536]{1,0:T(8,128)(2,1)} %w_out.1, bf16[96,1024]{1,0:T(8,128)(2,1)} %w_query.1, bf16[96,128]{1,0:T(8,128)(2,1)} %w_key.1, bf16[96,192]{1,0:T(8,128)(2,1)} %w_value.1), custom_call_target="tpu_custom_call" | custom-call | tf_op jit(solution)/shard_map/pack/pallas_call | solution.py:272
  2.5 4.1 %collective-permute-start.1 = (bf16[432,1536]{1,0:T(8,128)(2,1)}, bf16[432,1536]{1,0:T(8,128)(2,1)S(1)}, u32[]{:S(2)}, u32[]{:S(2)}) collective-permute-start(bf16[432,1536]{1,0:T(8,128)(2,1)} %pack.1.refs_0_.refs_6_.refs_5_), channel_id=1, source_target_pairs={{0,48},{1,49},{2,18},{3,19},{4,52},{5,53},{6,22},{7,23},{8,24},{9,... | collective-permute-start | bytes 3981320 | tf_op jit(solution)/shard_map/ppermute | solution.py:572
  6.6 3.0 %collective-permute-start = (bf16[432,1536]{1,0:T(8,128)(2,1)}, bf16[432,1536]{1,0:T(8,128)(2,1)}, u32[]{:S(2)}, u32[]{:S(2)}) collective-permute-start(bf16[432,1536]{1,0:T(8,128)(2,1)} %pack.1.refs_0_.refs_6_.refs_5_), channel_id=1, source_target_pairs={{0,65},{1,64},{2,67},{3,66},{4,69},{5,68},{6,71},{7,70},{8,72},{9,... | collective-permute-start | bytes 3981320 | tf_op jit(solution)/shard_map/ppermute | solution.py:572
  9.6 0.7 fusion
  10.3 0.7 collective-permute-start.4
  11.0 2.8 %collective-permute-start.3 = (s32[1,128]{1,0:T(1,128)S(1)}, s32[1,128]{1,0:T(1,128)S(1)}, u32[]{:S(2)}, u32[]{:S(2)}) collective-permute-start(s32[1,128]{1,0:T(1,128)S(1)} %get-tuple-element.54), channel_id=1, source_target_pairs={{0,1},{1,2},{2,3},{3,4},{4,5},{5,6},{6,7},{7,0},{8,9},{9,10},{10,1... | collective-permute-start | bytes 1544 | tf_op jit(solution)/shard_map/ppermute | solution.py:594
  15.0 1.2 dynamic-slice_bitcast_fusion.1.order
  16.2 8.1 %stem_front.1 = (bf16[10,128,768]{2,1,0:T(8,128)(2,1)}, bf16[1024,768]{1,0:T(8,128)(2,1)}, f32[8,768]{1,0:T(8,128)}) custom-call(s32[17]{0:T(128)} %dynamic-slice_bitcast_fusion.1.order, s32[128,128]{1,0:T(8,128)} %bitcast.6, bf16[60,768]{1,0:T(8,128)(2,1)} %weight.1, f32[1,768]{1,0:T(1,128)} %broadcast_in_dim.15.bias, f32[1,768]{1,0:T(1,128)} %broadcast_in_dim.16.gain), custom_call_target="tpu_custom_call" | custom-call | flops 4000000000 | bytes 5000000 | tf_op jit(solution)/shard_map/stem_front/pallas_call | solution.py:190
  24.4 0.9 collective-permute-done.refs_2_.refs_8_.refs_7_
  25.8 3.5 %collective-permute-start.6 = (bf16[432,1536]{1,0:T(8,128)(2,1)S(1)}, bf16[432,1536]{1,0:T(8,128)(2,1)}, u32[]{:S(2)}, u32[]{:S(2)}) collective-permute-start(bf16[432,1536]{1,0:T(8,128)(2,1)S(1)} %collective-permute-done.1.refs_3_.refs_9_.refs_8_), channel_id=1, source_target_pairs={{0,65},{1,64},{2,67},{3,66},{4,69},{5,68},{6,71},{7,70},{8,72},{9,... | collective-permute-start | bytes 3981320 | tf_op jit(solution)/shard_map/ppermute | solution.py:572
  29.3 2.2 %collective-permute-start.5 = (bf16[432,1536]{1,0:T(8,128)(2,1)S(1)}, bf16[432,1536]{1,0:T(8,128)(2,1)}, u32[]{:S(2)}, u32[]{:S(2)}) collective-permute-start(bf16[432,1536]{1,0:T(8,128)(2,1)S(1)} %collective-permute-done.1.refs_3_.refs_9_.refs_8_), channel_id=1, source_target_pairs={{0,6},{1,7},{2,0},{3,1},{4,2},{5,3},{6,4},{7,5},{8,10},{9,11},{10,... | collective-permute-start | bytes 3981320 | tf_op jit(solution)/shard_map/ppermute | solution.py:572
  32.7 1.6 %dynamic-slice_bitcast_fusion.refs_19_.angles = f32[2,128,128]{2,1,0:T(8,128)} fusion(f32[8,2,128,128]{3,2,1,0:T(8,128)} %constant.20.clone, s32[]{:T(128)S(6)} %select_n.8), kind=kLoop, calls=%fused_computation | loop fusion | bytes 262148 | tf_op jit(solution)/shard_map/squeeze | solution.py:606
  34.8 7.6 %stem_back.1.back = bf16[10,128,768]{2,1,0:T(8,128)(2,1)} custom-call(s32[128,128]{1,0:T(8,128)} %bitcast.7, bf16[1024,768]{1,0:T(8,128)(2,1)} %get-tuple-element.32.taps, f32[8,768]{1,0:T(8,128)} %get-tuple-element.33.vectors), custom_call_target="tpu_custom_call" | custom-call | flops 3500000000 | bytes 4000000 | tf_op jit(solution)/shard_map/stem_back/pallas_call | solution.py:211
  42.4 2.7 %edges.1.patch = f32[16,768]{1,0:T(8,128)} custom-call(s32[17]{0:T(128)} %dynamic-slice_bitcast_fusion.1.order, s32[128,128]{1,0:T(8,128)} %bitcast.8, s32[1,128]{1,0:T(1,128)} %copy-done.15, s32[1,128]{1,0:T(1,128)} %copy-done.14, bf16[1024,768]{1,0:T(8,128)(2,1)} %get-tuple-element.32.taps, f32[8,768]{1,0:T(8,128)} %get-tuple-element.33.vectors), custom_call_target="tpu_custom_call" | custom-call | flops 30000000 | bytes 2000000 | tf_op jit(solution)/shard_map/edges/pallas_call | solution.py:247
  45.1 2.1 %collective-permute-done.5.refs_6_.refs_12_.refs_11_ = bf16[432,1536]{1,0:T(8,128)(2,1)} collective-permute-done((bf16[432,1536]{1,0:T(8,128)(2,1)S(1)}, bf16[432,1536]{1,0:T(8,128)(2,1)}, u32[]{:S(2)}, u32[]{:S(2)}) %collective-permute-start.5) | collective-permute-done | bytes 1327136 | tf_op jit(solution)/shard_map/ppermute | solution.py:572
  47.7 1.2 %collective-permute-start.11 = (bf16[432,1536]{1,0:T(8,128)(2,1)}, bf16[432,1536]{1,0:T(8,128)(2,1)}, u32[]{:S(2)}, u32[]{:S(2)}) collective-permute-start(bf16[432,1536]{1,0:T(8,128)(2,1)} %collective-permute-done.7.refs_7_.refs_13_.refs_12_), channel_id=1, source_target_pairs={{0,65},{1,64},{2,67},{3,66},{4,69},{5,68},{6,71},{7,70},{8,72},{9,... | collective-permute-start | bytes 3981320 | tf_op jit(solution)/shard_map/ppermute | solution.py:572
  48.9 3.5 %collective-permute-start.10 = (bf16[432,1536]{1,0:T(8,128)(2,1)}, bf16[432,1536]{1,0:T(8,128)(2,1)S(1)}, u32[]{:S(2)}, u32[]{:S(2)}) collective-permute-start(bf16[432,1536]{1,0:T(8,128)(2,1)} %collective-permute-done.6.refs_8_.refs_14_.refs_13_), channel_id=1, source_target_pairs={{0,6},{1,7},{2,0},{3,1},{4,2},{5,3},{6,4},{7,5},{8,10},{9,11},{10,... | collective-permute-start | bytes 3981320 | tf_op jit(solution)/shard_map/ppermute | solution.py:572
  52.5 1.0 copy-done.2
  53.5 20.4 %conv.4.refs_16_ = f32[2,8,128,1536]{3,2,1,0:T(8,128)} custom-call(s32[17]{0:T(128)} %dynamic-slice_bitcast_fusion.1.order, bf16[10,128,768]{2,1,0:T(8,128)(2,1)} %get-tuple-element.30.front, bf16[10,128,768]{2,1,0:T(8,128)(2,1)} %stem_back.1.back, f32[16,768]{1,0:T(8,128)} %edges.1.patch, bf16[432,1536]{1,0:T(8,128)(2,1)} %pack.1.refs_0_.refs_6_.refs_5_, ...), custom_call_target="tpu_custom_call" | custom-call | flops 11274289152 | bytes 20000000 | tf_op jit(solution)/shard_map/conv/pallas_call | solution.py:479
  74.1 3.0 %collective-permute-done.16.refs_4_.refs_14_.refs_19_ = bf16[432,1536]{1,0:T(8,128)(2,1)S(1)} collective-permute-done((bf16[432,1536]{1,0:T(8,128)(2,1)S(1)}, bf16[432,1536]{1,0:T(8,128)(2,1)S(1)}, u32[]{:S(2)}, u32[]{:S(2)}) %collective-permute-start.16) | collective-permute-done | bytes 1327136 | tf_op jit(solution)/shard_map/ppermute | solution.py:572
  77.1 1.1 copy-done.5
  78.1 15.9 %conv.5 = (bf16[128,1536]{1,0:T(8,128)(2,1)}, bf16[128,1536]{1,0:T(8,128)(2,1)}, bf16[128,384]{1,0:T(8,128)(2,1)}) custom-call(s32[17]{0:T(128)} %dynamic-slice_bitcast_fusion.1.order, bf16[10,128,768]{2,1,0:T(8,128)(2,1)} %get-tuple-element.30.front, bf16[10,128,768]{2,1,0:T(8,128)(2,1)} %stem_back.1.back, f32[16,768]{1,0:T(8,128)} %edges.1.patch, ...), custom_call_target="tpu_custom_call" | custom-call | flops 5637144576 | bytes 20000000 | tf_op jit(solution)/shard_map/conv/pallas_call | solution.py:479
  94.1 1.2 collective-permute-start.17
  95.3 0.9 constant_dynamic-update-slice_fusion.1
  96.2 4.5 %collective-permute-done.17 = bf16[128,384]{1,0:T(8,128)(2,1)S(1)} collective-permute-done((bf16[128,384]{1,0:T(8,128)(2,1)}, bf16[128,384]{1,0:T(8,128)(2,1)S(1)}, u32[]{:S(2)}, u32[]{:S(2)}) %collective-permute-start.17) | collective-permute-done | bytes 98336 | tf_op jit(solution)/shard_map/ppermute | solution.py:617
  100.8 3.0 %collective-permute-start.20 = (bf16[256,384]{1,0:T(8,128)(2,1)S(1)}, bf16[256,384]{1,0:T(8,128)(2,1)S(1)}, u32[]{:S(2)}, u32[]{:S(2)}) collective-permute-start(bf16[256,384]{1,0:T(8,128)(2,1)S(1)} %constant_dynamic-update-slice_fusion.refs_1_), channel_id=1, source_target_pairs={{0,4},{1,5},{2,6},{3,7},{4,0},{5,1},{6,2},{7,3},{8,12},{9,13},{10,... | collective-permute-start | bytes 589832 | tf_op jit(solution)/shard_map/ppermute | solution.py:620
  103.8 0.6 collective-permute-start.19
  104.4 1.4 %collective-permute-start.18 = (bf16[256,384]{1,0:T(8,128)(2,1)S(1)}, bf16[256,384]{1,0:T(8,128)(2,1)S(1)}, u32[]{:S(2)}, u32[]{:S(2)}) collective-permute-start(bf16[256,384]{1,0:T(8,128)(2,1)S(1)} %constant_dynamic-update-slice_fusion.refs_1_), channel_id=1, source_target_pairs={{0,2},{1,3},{2,4},{3,5},{4,6},{5,7},{6,0},{7,1},{8,10},{9,11},{10,... | collective-permute-start | bytes 589832 | tf_op jit(solution)/shard_map/ppermute | solution.py:620
  105.8 4.5 %query.1.refs_0_ = bf16[1024,128]{1,0:T(8,128)(2,1)} custom-call(s32[17]{0:T(128)} %dynamic-slice_bitcast_fusion.1.order, bf16[128,1536]{1,0:T(8,128)(2,1)} %get-tuple-element.51.hidden, f32[2,128,128]{2,1,0:T(8,128)} %dynamic-slice_bitcast_fusion.refs_19_.angles, bf16[432,1536]{1,0:T(8,128)(2,1)} %pack.1.refs_0_.refs_6_.refs_5_, bf16[432,1536]{1,0:T(8,128)(2,1)} %copy-done, ...), custom_call_target="tpu_custom_call" | custom-call | flops 1600000000 | bytes 4000000 | tf_op jit(solution)/shard_map/query/pallas_call | solution.py:523
  110.4 3.0 %collective-permute-done.19.refs_3_ = bf16[256,384]{1,0:T(8,128)(2,1)S(1)} collective-permute-done((bf16[256,384]{1,0:T(8,128)(2,1)S(1)}, bf16[256,384]{1,0:T(8,128)(2,1)S(1)}, u32[]{:S(2)}, u32[]{:S(2)}) %collective-permute-start.19) | collective-permute-done | bytes 196640 | tf_op jit(solution)/shard_map/ppermute | solution.py:620
  113.4 0.7 copy-done.8
  114.1 7.1 %attention.1 = bf16[128,1536]{1,0:T(8,128)(2,1)} custom-call(s32[17]{0:T(128)} %dynamic-slice_bitcast_fusion.1.order, bf16[128,1536]{1,0:T(8,128)(2,1)} %get-tuple-element.50.coarse, bf16[1024,128]{1,0:T(8,128)(2,1)} %query.1.refs_0_, bf16[256,384]{1,0:T(8,128)(2,1)} %copy-done.6, bf16[256,384]{1,0:T(8,128)(2,1)} %copy-done.9, bf16[256,384]{1,0:T(8,128)(2,1)} %copy-done.8, ...), custom_call_target="tpu_custom_call" | custom-call | flops 3000000000 | bytes 6000000 | tf_op jit(solution)/shard_map/attention/pallas_call | solution.py:559
  (59 shorter events, 4.4 us)
Async XLA Ops:
  0.0 13.8 %copy-start.12 = (f32[768]{0:T(1024)S(1)}, f32[768]{0:T(1024)}, u32[]{:S(2)}) copy-start(f32[768]{0:T(1024)} %param.15) | copy-start | bytes 9220
  0.0 14.4 %copy-start.13 = (f32[768]{0:T(1024)S(1)}, f32[768]{0:T(1024)}, u32[]{:S(2)}) copy-start(f32[768]{0:T(1024)} %param.16) | copy-start | bytes 9220
  2.4 21.9 %collective-permute-start.2 = (bf16[432,1536]{1,0:T(8,128)(2,1)}, bf16[432,1536]{1,0:T(8,128)(2,1)S(1)}, u32[]{:S(2)}, u32[]{:S(2)}) collective-permute-start(bf16[432,1536]{1,0:T(8,128)(2,1)} %pack.1.refs_0_.refs_6_.refs_5_), channel_id=1, source_target_pairs={{0,8},{1,9},{2,10},{3,11},{4,12},{5,13},{6,14},{7,15},{8,0},{9,1},... | collective-permute-start | bytes 3981320 | tf_op jit(solution)/shard_map/ppermute | solution.py:572
  2.5 21.9 %collective-permute-start.1 = (bf16[432,1536]{1,0:T(8,128)(2,1)}, bf16[432,1536]{1,0:T(8,128)(2,1)S(1)}, u32[]{:S(2)}, u32[]{:S(2)}) collective-permute-start(bf16[432,1536]{1,0:T(8,128)(2,1)} %pack.1.refs_0_.refs_6_.refs_5_), channel_id=1, source_target_pairs={{0,48},{1,49},{2,18},{3,19},{4,52},{5,53},{6,22},{7,23},{8,24},{9,... | collective-permute-start | bytes 3981320 | tf_op jit(solution)/shard_map/ppermute | solution.py:572
  6.6 18.7 %collective-permute-start = (bf16[432,1536]{1,0:T(8,128)(2,1)}, bf16[432,1536]{1,0:T(8,128)(2,1)}, u32[]{:S(2)}, u32[]{:S(2)}) collective-permute-start(bf16[432,1536]{1,0:T(8,128)(2,1)} %pack.1.refs_0_.refs_6_.refs_5_), channel_id=1, source_target_pairs={{0,65},{1,64},{2,67},{3,66},{4,69},{5,68},{6,71},{7,70},{8,72},{9,... | collective-permute-start | bytes 3981320 | tf_op jit(solution)/shard_map/ppermute | solution.py:572
  10.3 14.0 %collective-permute-start.4 = (s32[1,128]{1,0:T(1,128)S(1)}, s32[1,128]{1,0:T(1,128)S(1)}, u32[]{:S(2)}, u32[]{:S(2)}) collective-permute-start(s32[1,128]{1,0:T(1,128)S(1)} %get-tuple-element.53), channel_id=1, source_target_pairs={{0,7},{1,0},{2,1},{3,2},{4,3},{5,4},{6,5},{7,6},{8,15},{9,8},{10,9... | collective-permute-start | bytes 1544 | tf_op jit(solution)/shard_map/ppermute | solution.py:595
  11.0 13.3 %collective-permute-start.3 = (s32[1,128]{1,0:T(1,128)S(1)}, s32[1,128]{1,0:T(1,128)S(1)}, u32[]{:S(2)}, u32[]{:S(2)}) collective-permute-start(s32[1,128]{1,0:T(1,128)S(1)} %get-tuple-element.54), channel_id=1, source_target_pairs={{0,1},{1,2},{2,3},{3,4},{4,5},{5,6},{6,7},{7,0},{8,9},{9,10},{10,1... | collective-permute-start | bytes 1544 | tf_op jit(solution)/shard_map/ppermute | solution.py:594
  16.2 15.3 %copy-start.10 = (f32[1536]{0:T(1024)S(1)}, f32[1536]{0:T(1024)}, u32[]{:S(2)}) copy-start(f32[1536]{0:T(1024)} %param.18) | copy-start | bytes 18436
  16.2 15.9 %copy-start.11 = (f32[1536]{0:T(1024)S(1)}, f32[1536]{0:T(1024)}, u32[]{:S(2)}) copy-start(f32[1536]{0:T(1024)} %param.19) | copy-start | bytes 18436
  24.3 18.0 %copy-start.14 = (s32[1,128]{1,0:T(1,128)}, s32[1,128]{1,0:T(1,128)S(1)}, u32[]{:S(2)}) copy-start(s32[1,128]{1,0:T(1,128)S(1)} %collective-permute-done.4.high_row) | copy-start | bytes 1540
  24.3 18.0 %copy-start.15 = (s32[1,128]{1,0:T(1,128)}, s32[1,128]{1,0:T(1,128)S(1)}, u32[]{:S(2)}) copy-start(s32[1,128]{1,0:T(1,128)S(1)} %collective-permute-done.3.low_row) | copy-start | bytes 1540
  24.3 18.0 %copy-start = (bf16[432,1536]{1,0:T(8,128)(2,1)}, bf16[432,1536]{1,0:T(8,128)(2,1)S(1)}, u32[]{:S(2)}) copy-start(bf16[432,1536]{1,0:T(8,128)(2,1)S(1)} %collective-permute-done.2.refs_1_.refs_7_.refs_6_) | copy-start | bytes 3981316
  24.4 18.0 %copy-start.1 = (bf16[432,1536]{1,0:T(8,128)(2,1)}, bf16[432,1536]{1,0:T(8,128)(2,1)S(1)}, u32[]{:S(2)}) copy-start(bf16[432,1536]{1,0:T(8,128)(2,1)S(1)} %collective-permute-done.1.refs_3_.refs_9_.refs_8_) | copy-start | bytes 3981316
  25.2 19.8 %collective-permute-start.7 = (bf16[432,1536]{1,0:T(8,128)(2,1)S(1)}, bf16[432,1536]{1,0:T(8,128)(2,1)}, u32[]{:S(2)}, u32[]{:S(2)}) collective-permute-start(bf16[432,1536]{1,0:T(8,128)(2,1)S(1)} %collective-permute-done.1.refs_3_.refs_9_.refs_8_), channel_id=1, source_target_pairs={{0,48},{1,49},{2,18},{3,19},{4,52},{5,53},{6,22},{7,23},{8,24},{9,... | collective-permute-start | bytes 3981320 | tf_op jit(solution)/shard_map/ppermute | solution.py:572
  25.8 19.3 %collective-permute-start.6 = (bf16[432,1536]{1,0:T(8,128)(2,1)S(1)}, bf16[432,1536]{1,0:T(8,128)(2,1)}, u32[]{:S(2)}, u32[]{:S(2)}) collective-permute-start(bf16[432,1536]{1,0:T(8,128)(2,1)S(1)} %collective-permute-done.1.refs_3_.refs_9_.refs_8_), channel_id=1, source_target_pairs={{0,65},{1,64},{2,67},{3,66},{4,69},{5,68},{6,71},{7,70},{8,72},{9,... | collective-permute-start | bytes 3981320 | tf_op jit(solution)/shard_map/ppermute | solution.py:572
  29.3 17.9 %collective-permute-start.5 = (bf16[432,1536]{1,0:T(8,128)(2,1)S(1)}, bf16[432,1536]{1,0:T(8,128)(2,1)}, u32[]{:S(2)}, u32[]{:S(2)}) collective-permute-start(bf16[432,1536]{1,0:T(8,128)(2,1)S(1)} %collective-permute-done.1.refs_3_.refs_9_.refs_8_), channel_id=1, source_target_pairs={{0,6},{1,7},{2,0},{3,1},{4,2},{5,3},{6,4},{7,5},{8,10},{9,11},{10,... | collective-permute-start | bytes 3981320 | tf_op jit(solution)/shard_map/ppermute | solution.py:572
  34.2 14.7 %collective-permute-start.14 = (bf16[432,1536]{1,0:T(8,128)(2,1)S(1)}, bf16[432,1536]{1,0:T(8,128)(2,1)}, u32[]{:S(2)}, u32[]{:S(2)}) collective-permute-start(bf16[432,1536]{1,0:T(8,128)(2,1)S(1)} %collective-permute-done.1.refs_3_.refs_9_.refs_8_), channel_id=1, source_target_pairs={{0,8},{1,9},{2,10},{3,11},{4,12},{5,13},{6,14},{7,15},{8,0},{9,1},... | collective-permute-start | bytes 3981320 | tf_op jit(solution)/shard_map/ppermute | solution.py:572
  34.2 14.7 %collective-permute-start.13 = (bf16[432,1536]{1,0:T(8,128)(2,1)}, bf16[432,1536]{1,0:T(8,128)(2,1)}, u32[]{:S(2)}, u32[]{:S(2)}) collective-permute-start(bf16[432,1536]{1,0:T(8,128)(2,1)} %collective-permute-done.refs_2_.refs_8_.refs_7_), channel_id=1, source_target_pairs={{0,8},{1,9},{2,10},{3,11},{4,12},{5,13},{6,14},{7,15},{8,0},{9,1},... | collective-permute-start | bytes 3981320 | tf_op jit(solution)/shard_map/ppermute | solution.py:572
  47.2 5.2 %collective-permute-start.15 = (bf16[432,1536]{1,0:T(8,128)(2,1)}, bf16[432,1536]{1,0:T(8,128)(2,1)S(1)}, u32[]{:S(2)}, u32[]{:S(2)}) collective-permute-start(bf16[432,1536]{1,0:T(8,128)(2,1)} %collective-permute-done.5.refs_6_.refs_12_.refs_11_), channel_id=1, source_target_pairs={{0,8},{1,9},{2,10},{3,11},{4,12},{5,13},{6,14},{7,15},{8,0},{9,1},... | collective-permute-start | bytes 3981320 | tf_op jit(solution)/shard_map/ppermute | solution.py:572
  47.2 5.3 %collective-permute-start.8 = (bf16[432,1536]{1,0:T(8,128)(2,1)}, bf16[432,1536]{1,0:T(8,128)(2,1)}, u32[]{:S(2)}, u32[]{:S(2)}) collective-permute-start(bf16[432,1536]{1,0:T(8,128)(2,1)} %collective-permute-done.7.refs_7_.refs_13_.refs_12_), channel_id=1, source_target_pairs={{0,8},{1,9},{2,10},{3,11},{4,12},{5,13},{6,14},{7,15},{8,0},{9,1},... | collective-permute-start | bytes 3981320 | tf_op jit(solution)/shard_map/ppermute | solution.py:572
  47.7 26.1 %collective-permute-start.11 = (bf16[432,1536]{1,0:T(8,128)(2,1)}, bf16[432,1536]{1,0:T(8,128)(2,1)}, u32[]{:S(2)}, u32[]{:S(2)}) collective-permute-start(bf16[432,1536]{1,0:T(8,128)(2,1)} %collective-permute-done.7.refs_7_.refs_13_.refs_12_), channel_id=1, source_target_pairs={{0,65},{1,64},{2,67},{3,66},{4,69},{5,68},{6,71},{7,70},{8,72},{9,... | collective-permute-start | bytes 3981320 | tf_op jit(solution)/shard_map/ppermute | solution.py:572
  48.9 24.9 %collective-permute-start.12 = (bf16[432,1536]{1,0:T(8,128)(2,1)}, bf16[432,1536]{1,0:T(8,128)(2,1)}, u32[]{:S(2)}, u32[]{:S(2)}) collective-permute-start(bf16[432,1536]{1,0:T(8,128)(2,1)} %collective-permute-done.6.refs_8_.refs_14_.refs_13_), channel_id=1, source_target_pairs={{0,56},{1,57},{2,26},{3,27},{4,60},{5,61},{6,30},{7,31},{8,16},{9,... | collective-permute-start | bytes 3981320 | tf_op jit(solution)/shard_map/ppermute | solution.py:572
  48.9 24.9 %collective-permute-start.10 = (bf16[432,1536]{1,0:T(8,128)(2,1)}, bf16[432,1536]{1,0:T(8,128)(2,1)S(1)}, u32[]{:S(2)}, u32[]{:S(2)}) collective-permute-start(bf16[432,1536]{1,0:T(8,128)(2,1)} %collective-permute-done.6.refs_8_.refs_14_.refs_13_), channel_id=1, source_target_pairs={{0,6},{1,7},{2,0},{3,1},{4,2},{5,3},{6,4},{7,5},{8,10},{9,11},{10,... | collective-permute-start | bytes 3981320 | tf_op jit(solution)/shard_map/ppermute | solution.py:572
  52.4 21.6 %collective-permute-start.9 = (bf16[432,1536]{1,0:T(8,128)(2,1)}, bf16[432,1536]{1,0:T(8,128)(2,1)S(1)}, u32[]{:S(2)}, u32[]{:S(2)}) collective-permute-start(bf16[432,1536]{1,0:T(8,128)(2,1)} %collective-permute-done.6.refs_8_.refs_14_.refs_13_), channel_id=1, source_target_pairs={{0,8},{1,9},{2,10},{3,11},{4,12},{5,13},{6,14},{7,15},{8,0},{9,1},... | collective-permute-start | bytes 3981320 | tf_op jit(solution)/shard_map/ppermute | solution.py:572
  73.9 3.2 %copy-start.3 = (bf16[432,1536]{1,0:T(8,128)(2,1)}, bf16[432,1536]{1,0:T(8,128)(2,1)S(1)}, u32[]{:S(2)}) copy-start(bf16[432,1536]{1,0:T(8,128)(2,1)S(1)} %collective-permute-done.10.refs_2_.refs_12_.refs_17_) | copy-start | bytes 3981316
  73.9 3.1 %collective-permute-start.16 = (bf16[432,1536]{1,0:T(8,128)(2,1)S(1)}, bf16[432,1536]{1,0:T(8,128)(2,1)S(1)}, u32[]{:S(2)}, u32[]{:S(2)}) collective-permute-start(bf16[432,1536]{1,0:T(8,128)(2,1)S(1)} %collective-permute-done.10.refs_2_.refs_12_.refs_17_), channel_id=1, source_target_pairs={{0,8},{1,9},{2,10},{3,11},{4,12},{5,13},{6,14},{7,15},{8,0},{9,1},... | collective-permute-start | bytes 3981320 | tf_op jit(solution)/shard_map/ppermute | solution.py:572
  94.1 6.6 %collective-permute-start.17 = (bf16[128,384]{1,0:T(8,128)(2,1)}, bf16[128,384]{1,0:T(8,128)(2,1)S(1)}, u32[]{:S(2)}, u32[]{:S(2)}) collective-permute-start(bf16[128,384]{1,0:T(8,128)(2,1)} %get-tuple-element.52), channel_id=1, source_target_pairs={{0,1},{1,0},{2,3},{3,2},{4,5},{5,4},{6,7},{7,6},{8,9},{9,8},{10,11... | collective-permute-start | bytes 294920 | tf_op jit(solution)/shard_map/ppermute | solution.py:617
  100.8 9.6 %copy-start.6 = (bf16[256,384]{1,0:T(8,128)(2,1)}, bf16[256,384]{1,0:T(8,128)(2,1)S(1)}, u32[]{:S(2)}) copy-start(bf16[256,384]{1,0:T(8,128)(2,1)S(1)} %constant_dynamic-update-slice_fusion.refs_1_) | copy-start | bytes 589828
  100.8 9.6 %collective-permute-start.20 = (bf16[256,384]{1,0:T(8,128)(2,1)S(1)}, bf16[256,384]{1,0:T(8,128)(2,1)S(1)}, u32[]{:S(2)}, u32[]{:S(2)}) collective-permute-start(bf16[256,384]{1,0:T(8,128)(2,1)S(1)} %constant_dynamic-update-slice_fusion.refs_1_), channel_id=1, source_target_pairs={{0,4},{1,5},{2,6},{3,7},{4,0},{5,1},{6,2},{7,3},{8,12},{9,13},{10,... | collective-permute-start | bytes 589832 | tf_op jit(solution)/shard_map/ppermute | solution.py:620
  103.8 9.5 %collective-permute-start.19 = (bf16[256,384]{1,0:T(8,128)(2,1)S(1)}, bf16[256,384]{1,0:T(8,128)(2,1)S(1)}, u32[]{:S(2)}, u32[]{:S(2)}) collective-permute-start(bf16[256,384]{1,0:T(8,128)(2,1)S(1)} %constant_dynamic-update-slice_fusion.refs_1_), channel_id=1, source_target_pairs={{0,6},{1,7},{2,0},{3,1},{4,2},{5,3},{6,4},{7,5},{8,14},{9,15},{10,... | collective-permute-start | bytes 589832 | tf_op jit(solution)/shard_map/ppermute | solution.py:620
  104.4 8.9 %collective-permute-start.18 = (bf16[256,384]{1,0:T(8,128)(2,1)S(1)}, bf16[256,384]{1,0:T(8,128)(2,1)S(1)}, u32[]{:S(2)}, u32[]{:S(2)}) collective-permute-start(bf16[256,384]{1,0:T(8,128)(2,1)S(1)} %constant_dynamic-update-slice_fusion.refs_1_), channel_id=1, source_target_pairs={{0,2},{1,3},{2,4},{3,5},{4,6},{5,7},{6,0},{7,1},{8,10},{9,11},{10,... | collective-permute-start | bytes 589832 | tf_op jit(solution)/shard_map/ppermute | solution.py:620
  110.4 3.0 %copy-start.7 = (bf16[256,384]{1,0:T(8,128)(2,1)}, bf16[256,384]{1,0:T(8,128)(2,1)S(1)}, u32[]{:S(2)}) copy-start(bf16[256,384]{1,0:T(8,128)(2,1)S(1)} %collective-permute-done.20.refs_4_) | copy-start | bytes 589828
  (5 other events, 6.6 us)
